TPU v7x, 32 devices: a whole 2x2x4 slice. The times are simulated.
32 devices in a mesh: dp: 4 (over y, x), expert: 8 (over z, core).
Axes of the slice: x: 2, y: 2, z: 4, core: 2. Of those that a mesh axis runs over, the one named last changes fastest.
Arguments:
- tokens: bfloat16 [10240, 1024], P(('dp', 'expert')), may hold values from -6 to 6
- attn_gain: bfloat16 [1024], P('dp'), may hold values from 0.5 to 1.5
- w_query: bfloat16 [1024, 1024], P('dp'), may hold values from -0.1875 to 0.1875
- w_keyval: bfloat16 [1024, 1024], P('dp'), may hold values from -0.1875 to 0.1875
- w_output: bfloat16 [1024, 1024], P('dp'), may hold values from -1.5 to 1.5
- moe_gain: bfloat16 [1024], P('dp'), may hold values from 0.5 to 1.5
- w_router: bfloat16 [1024, 32], P('dp'), may hold values from -0.09375 to 0.09375
- expert_in: bfloat16 [32, 1024, 1024], P('expert'), may hold values from -0.1875 to 0.1875
- expert_out: bfloat16 [32, 512, 1024], P('expert'), may hold values from -0.75 to 0.75
- cotangent: bfloat16 [10240, 1024], P(('dp', 'expert')), may hold values from -6 to 6
- routes: int32 [10240, 8], P(('dp', 'expert')), may hold values from 0 to 31, all different within a row; in each aligned block of 320 rows (0 to 319, 320 to 639, ...) at most 120 rows name the same one
- parents: int32 [32, 13], P(('dp', 'expert')), may hold values from 0 to 4, as said below
Outputs:
- block_out: bfloat16 [10240, 1024], P(('dp', 'expert'))
- input_grad: float32 [10240, 1024], P(('dp', 'expert'))
- grad_attn_gain: float32 [1024], P('dp')
- grad_w_query: float32 [1024, 1024], P('dp')
- grad_w_keyval: float32 [1024, 1024], P('dp')
- grad_w_output: float32 [1024, 1024], P('dp')
- grad_moe_gain: float32 [1024], P('dp')
- grad_w_router: float32 [1024, 32], P('dp')
- grad_expert_in: float32 [32, 1024, 1024], P('expert', 'dp')
- grad_expert_out: float32 [32, 512, 1024], P('expert', 'dp')
Inputs may be any that keep to these rules, and one draw needn't show every extreme that they name: `routes`: each row names 8 different experts. In each aligned block of 320 rows (the rows of one tree) no expert is named by more than 120 rows, and in some block one expert is named by exactly 120 rows. `parents`: in each tree, segments 0 to 4 have parent 0, and segments 5 to 12 name each of 1, 2, 3, 4 as parent exactly twice.
All inputs are finite; a program needn't handle non-finite values.
Results may differ from a plain program's by a relative error of at most 0.02.
Values may be sent and summed in bfloat16 or wider, within the bound.
A program may use at most 256 MiB of HBM per device.

v0:
```python
import jax
import jax.numpy as jnp
from jax import lax
from jax.sharding import PartitionSpec as P

H = 16
KV = 8
HD = 64
EXPERTS = 32
TOPK = 8
CAP = 120


EPSILON = 1e-06


def tree_layout(tree_rows):
    unit_rows = tree_rows // 20
    row_index = jnp.arange(tree_rows, dtype=jnp.int32)
    segment = jnp.where(
        row_index < 8 * unit_rows,
        0,
        jnp.where(
            row_index < 12 * unit_rows,
            1 + (row_index - 8 * unit_rows) // unit_rows,
            5 + (row_index - 12 * unit_rows) // unit_rows,
        ),
    )
    depth_start = jnp.where(segment == 0, 0, jnp.where(segment < 5, 8 * unit_rows, 9 * unit_rows))
    seg_start = jnp.where(
        segment == 0,
        0,
        jnp.where(
            segment < 5,
            8 * unit_rows + (segment - 1) * unit_rows,
            12 * unit_rows + (segment - 5) * unit_rows,
        ),
    )
    position = depth_start + row_index - seg_start
    return (segment, position)


def path_allowed(parent_row, segment):
    segment_ids = jnp.arange(parent_row.shape[0], dtype=jnp.int32)
    grandparent = parent_row[parent_row]
    on_path = (
        (segment_ids[None, :] == segment_ids[:, None])
        | (segment_ids[None, :] == parent_row[:, None])
        | (segment_ids[None, :] == grandparent[:, None])
    ).astype(jnp.float32)
    seg_hot = (segment[:, None] == segment_ids[None, :]).astype(jnp.float32)
    reach = jnp.dot(
        jnp.dot(seg_hot, on_path, precision=lax.Precision.HIGHEST),
        seg_hot.T,
        precision=lax.Precision.HIGHEST,
    )
    row_index = jnp.arange(segment.shape[0], dtype=jnp.int32)
    return (reach > 0.5) & (row_index[None, :] <= row_index[:, None])


def rope_tables(position):
    frequency = 10000.0 ** (-jnp.arange(0, HD, 2, dtype=jnp.float32) / HD)
    angles = position.astype(jnp.float32)[:, None] * frequency[None, :]
    return (jnp.concatenate([jnp.cos(angles)] * 2, -1), jnp.concatenate([jnp.sin(angles)] * 2, -1))


def turn_half(field):
    half_width = field.shape[-1] // 2
    return jnp.concatenate([-field[..., half_width:], field[..., :half_width]], axis=-1)


def rotary(field, cosine, sine_table):
    return field * cosine + turn_half(field) * sine_table


def unrotate(grad_field, cosine, sine_table):
    return grad_field * cosine - turn_half(grad_field * sine_table)


def rms_norm(field, gain_vector):
    return (
        field * lax.rsqrt(jnp.mean(field * field, axis=-1, keepdims=True) + EPSILON) * gain_vector
    )


def gated_unit(gate_up):
    width_ff = gate_up.shape[-1] // 2
    gate_part = gate_up[..., :width_ff]
    return gate_part / (1.0 + jnp.exp(-gate_part)) * gate_up[..., width_ff:]


def slot_tables(route_rows, capacity):
    flat_routes = route_rows.reshape(-1)
    row_total = flat_routes.shape[0]
    expert_ids = jnp.arange(EXPERTS, dtype=jnp.int32)
    route_hot = (flat_routes[:, None] == expert_ids[None, :]).astype(jnp.int32)
    before = jnp.cumsum(route_hot, axis=0) - route_hot
    slot_rank = jnp.sum(before * route_hot, axis=1)
    slot_index = flat_routes * capacity + slot_rank
    source = (
        jnp.full((EXPERTS * capacity,), row_total, jnp.int32)
        .at[slot_index]
        .set(jnp.arange(row_total, dtype=jnp.int32))
    )
    return (slot_index, source)


def shards(
    tokens,
    attn_gain,
    w_query,
    w_keyval,
    w_output,
    moe_gain,
    w_router,
    expert_in,
    expert_out,
    cotangent,
    routes,
    parents,
):
    tree_rows = tokens.shape[0]
    width = tokens.shape[1]
    capacity = CAP
    groups = H // KV
    kv_width = KV * HD
    score_scale = HD ** (-0.5)
    gathered = (
        lax.all_gather(attn_gain, "dp", axis=0, tiled=True),
        lax.all_gather(w_query, "dp", axis=0, tiled=True),
        lax.all_gather(w_keyval, "dp", axis=0, tiled=True),
        lax.all_gather(w_output, "dp", axis=0, tiled=True),
        lax.all_gather(moe_gain, "dp", axis=0, tiled=True),
        lax.all_gather(w_router, "dp", axis=0, tiled=True),
    )
    gain_first, query_full, keyval_full, output_full, gain_second, router_full = gathered
    inputs = tokens.astype(jnp.float32)
    segment, position = tree_layout(tree_rows)
    allowed = path_allowed(parents[0], segment)
    cosine, sine_table = rope_tables(position)
    cos_four, sin_four = (cosine[:, None, None, :], sine_table[:, None, None, :])
    cos_three, sin_three = (cosine[:, None, :], sine_table[:, None, :])
    normed, first_back = jax.vjp(rms_norm, inputs, gain_first.astype(jnp.float32))
    hidden = normed.astype(jnp.bfloat16)
    query_pre = jnp.dot(hidden, query_full, preferred_element_type=jnp.float32)
    keyval_pre = jnp.dot(hidden, keyval_full, preferred_element_type=jnp.float32)
    queries = rotary(query_pre.reshape(tree_rows, KV, groups, HD), cos_four, sin_four).astype(
        jnp.bfloat16
    )
    key_heads = rotary(
        keyval_pre[:, :kv_width].reshape(tree_rows, KV, HD), cos_three, sin_three
    ).astype(jnp.bfloat16)
    values = keyval_pre[:, kv_width:].reshape(tree_rows, KV, HD).astype(jnp.bfloat16)

    def score_block():
        raw_scores = (
            jnp.einsum("tkgd,skd->kgts", queries, key_heads, preferred_element_type=jnp.float32)
            * score_scale
        )
        return jnp.where(allowed, raw_scores, -1e30)

    scores = score_block()
    row_max = jnp.max(scores, axis=-1, keepdims=True)
    exp_scores = jnp.exp(scores - row_max)
    row_total = jnp.sum(exp_scores, axis=-1, keepdims=True)
    log_total = row_max + jnp.log(row_total)
    attn_low = (exp_scores / row_total).astype(jnp.bfloat16)
    attended = jnp.einsum("kgts,skd->tkgd", attn_low, values, preferred_element_type=jnp.float32)
    attended = attended.reshape(tree_rows, H * HD).astype(jnp.bfloat16)
    middle = inputs + jnp.dot(attended, output_full, preferred_element_type=jnp.float32)
    normed2, second_back = jax.vjp(rms_norm, middle, gain_second.astype(jnp.float32))
    hidden2 = normed2.astype(jnp.bfloat16)
    logits = jnp.dot(hidden2, router_full, preferred_element_type=jnp.float32)
    expert_ids = jnp.arange(EXPERTS, dtype=jnp.int32)
    route_hot = (routes[:, :, None] == expert_ids[None, None, :]).astype(jnp.float32)
    picked = jnp.sum(route_hot * logits[:, None, :], axis=2)
    picked_exp = jnp.exp(picked - jnp.max(picked, axis=1, keepdims=True))
    gate_weights = picked_exp / jnp.sum(picked_exp, axis=1, keepdims=True)
    slot_index, source = slot_tables(routes, capacity)
    zero_row = jnp.zeros((1, width), jnp.bfloat16)
    token_of_slot = jnp.where(source < tree_rows * TOPK, source // TOPK, tree_rows)
    sent_rows = jnp.concatenate([hidden2, zero_row], axis=0)[token_of_slot].reshape(
        EXPERTS, capacity, width
    )
    received = lax.all_to_all(sent_rows, "expert", split_axis=0, concat_axis=1, tiled=True)
    gate_up = jnp.einsum("erd,edf->erf", received, expert_in, preferred_element_type=jnp.float32)
    activated, glu_back = jax.vjp(gated_unit, gate_up)
    act_low = activated.astype(jnp.bfloat16)
    expert_made = jnp.einsum(
        "erf,efd->erd", act_low, expert_out, preferred_element_type=jnp.float32
    ).astype(jnp.bfloat16)
    returned = lax.all_to_all(expert_made, "expert", split_axis=1, concat_axis=0, tiled=True)
    back_rows = (
        returned.reshape(EXPERTS * capacity, width)[slot_index]
        .reshape(tree_rows, TOPK, width)
        .astype(jnp.float32)
    )
    result = middle + jnp.sum(gate_weights[:, :, None] * back_rows, axis=1)
    block_out = result.astype(jnp.bfloat16)
    grad_result = cotangent.astype(jnp.float32)
    grad_gates = jnp.sum(back_rows * grad_result[:, None, :], axis=-1)
    grad_picked = gate_weights * (
        grad_gates - jnp.sum(gate_weights * grad_gates, axis=1, keepdims=True)
    )
    grad_logits = jnp.sum(route_hot * grad_picked[:, :, None], axis=1).astype(jnp.bfloat16)
    grad_router = jnp.einsum("td,te->de", hidden2, grad_logits, preferred_element_type=jnp.float32)
    grad_hidden2 = jnp.einsum(
        "te,de->td", grad_logits, router_full, preferred_element_type=jnp.float32
    )
    grad_copies = (
        (gate_weights[:, :, None] * grad_result[:, None, :])
        .astype(jnp.bfloat16)
        .reshape(tree_rows * TOPK, width)
    )
    grad_sent = jnp.concatenate([grad_copies, zero_row], axis=0)[source].reshape(
        EXPERTS, capacity, width
    )
    grad_received = lax.all_to_all(grad_sent, "expert", split_axis=0, concat_axis=1, tiled=True)
    grad_act = jnp.einsum(
        "erd,efd->erf", grad_received, expert_out, preferred_element_type=jnp.float32
    )
    grad_out_w = jnp.einsum(
        "erf,erd->efd", act_low, grad_received, preferred_element_type=jnp.float32
    )
    grad_gate_up = glu_back(grad_act)[0].astype(jnp.bfloat16)
    grad_in_rows = jnp.einsum(
        "erf,edf->erd", grad_gate_up, expert_in, preferred_element_type=jnp.float32
    ).astype(jnp.bfloat16)
    grad_in_w = jnp.einsum(
        "erd,erf->edf", received, grad_gate_up, preferred_element_type=jnp.float32
    )
    grad_back = lax.all_to_all(grad_in_rows, "expert", split_axis=1, concat_axis=0, tiled=True)
    grad_rows_back = grad_back.reshape(EXPERTS * capacity, width)[slot_index].reshape(
        tree_rows, TOPK, width
    )
    grad_hidden2 = grad_hidden2 + jnp.sum(grad_rows_back.astype(jnp.float32), axis=1)
    expert_in_share, expert_out_share = (
        lax.psum_scatter(
            grad_in_w.astype(jnp.bfloat16), "dp", scatter_dimension=1, tiled=True
        ).astype(jnp.float32),
        lax.psum_scatter(
            grad_out_w.astype(jnp.bfloat16), "dp", scatter_dimension=1, tiled=True
        ).astype(jnp.float32),
    )
    grad_mid_norm, grad_gain_second = second_back(grad_hidden2)
    grad_middle = grad_result + grad_mid_norm
    grad_branch = grad_middle.astype(jnp.bfloat16)
    grad_w_out = jnp.einsum("ti,td->id", attended, grad_branch, preferred_element_type=jnp.float32)
    grad_attended = jnp.einsum(
        "td,id->ti", grad_branch, output_full, preferred_element_type=jnp.float32
    )
    grad_attended = grad_attended.astype(jnp.bfloat16).reshape(tree_rows, KV, groups, HD)
    attn_probs = jnp.exp(score_block() - log_total)
    probs_low = attn_probs.astype(jnp.bfloat16)
    grad_values = jnp.einsum(
        "kgts,tkgd->skd", probs_low, grad_attended, preferred_element_type=jnp.float32
    )
    grad_probs = jnp.einsum(
        "tkgd,skd->kgts", grad_attended, values, preferred_element_type=jnp.float32
    )
    grad_scores = (
        attn_probs * (grad_probs - jnp.sum(attn_probs * grad_probs, axis=-1, keepdims=True))
    ).astype(jnp.bfloat16)
    grad_query_rot = (
        jnp.einsum("kgts,skd->tkgd", grad_scores, key_heads, preferred_element_type=jnp.float32)
        * score_scale
    )
    grad_keys_rot = (
        jnp.einsum("kgts,tkgd->skd", grad_scores, queries, preferred_element_type=jnp.float32)
        * score_scale
    )
    grad_query_pre = (
        unrotate(grad_query_rot, cos_four, sin_four).reshape(tree_rows, H * HD).astype(jnp.bfloat16)
    )
    grad_keyval_pre = jnp.concatenate(
        [
            unrotate(grad_keys_rot, cos_three, sin_three).reshape(tree_rows, kv_width),
            grad_values.reshape(tree_rows, kv_width),
        ],
        axis=1,
    ).astype(jnp.bfloat16)
    grad_w_q = jnp.einsum("td,ti->di", hidden, grad_query_pre, preferred_element_type=jnp.float32)
    grad_w_kv = jnp.einsum("td,ti->di", hidden, grad_keyval_pre, preferred_element_type=jnp.float32)
    grad_hidden = jnp.einsum(
        "ti,di->td", grad_query_pre, query_full, preferred_element_type=jnp.float32
    ) + jnp.einsum("ti,di->td", grad_keyval_pre, keyval_full, preferred_element_type=jnp.float32)
    grad_in_norm, grad_gain_first = first_back(grad_hidden)
    input_grad = grad_middle + grad_in_norm
    pieces = (
        lax.psum_scatter(
            grad_gain_first.astype(jnp.bfloat16), "dp", scatter_dimension=0, tiled=True
        ).astype(jnp.float32),
        lax.psum_scatter(
            grad_w_q.astype(jnp.bfloat16), "dp", scatter_dimension=0, tiled=True
        ).astype(jnp.float32),
        lax.psum_scatter(
            grad_w_kv.astype(jnp.bfloat16), "dp", scatter_dimension=0, tiled=True
        ).astype(jnp.float32),
        lax.psum_scatter(
            grad_w_out.astype(jnp.bfloat16), "dp", scatter_dimension=0, tiled=True
        ).astype(jnp.float32),
        lax.psum_scatter(
            grad_gain_second.astype(jnp.bfloat16), "dp", scatter_dimension=0, tiled=True
        ).astype(jnp.float32),
        lax.psum_scatter(
            grad_router.astype(jnp.bfloat16), "dp", scatter_dimension=0, tiled=True
        ).astype(jnp.float32),
    )
    shares = (
        lax.psum(pieces[0].astype(jnp.bfloat16), "expert").astype(jnp.float32),
        lax.psum(pieces[1].astype(jnp.bfloat16), "expert").astype(jnp.float32),
        lax.psum(pieces[2].astype(jnp.bfloat16), "expert").astype(jnp.float32),
        lax.psum(pieces[3].astype(jnp.bfloat16), "expert").astype(jnp.float32),
        lax.psum(pieces[4].astype(jnp.bfloat16), "expert").astype(jnp.float32),
        lax.psum(pieces[5].astype(jnp.bfloat16), "expert").astype(jnp.float32),
    )
    return (
        block_out,
        input_grad,
        shares[0],
        shares[1],
        shares[2],
        shares[3],
        shares[4],
        shares[5],
        expert_in_share,
        expert_out_share,
    )


def solution(mesh):
    in_specs = (
        P(("dp", "expert"), None),
        P("dp"),
        P("dp", None),
        P("dp", None),
        P("dp", None),
        P("dp"),
        P("dp", None),
        P("expert", None, None),
        P("expert", None, None),
        P(("dp", "expert"), None),
        P(("dp", "expert"), None),
        P(("dp", "expert"), None),
    )
    out_specs = (
        P(("dp", "expert"), None),
        P(("dp", "expert"), None),
        P("dp"),
        P("dp", None),
        P("dp", None),
        P("dp", None),
        P("dp"),
        P("dp", None),
        P("expert", "dp", None),
        P("expert", "dp", None),
    )
    return jax.shard_map(shards, mesh=mesh, in_specs=in_specs, out_specs=out_specs, check_vma=False)
```

profile of v0, /device:TPU:0, one launch (start us, length us, event | category | flops | bytes accessed | tf_op | source)
XLA Modules:
  0.0 1298.7 jit_solution(12203911237122392031)
XLA Ops:
  14.6 9.5 all-gather.1
  24.1 8.0 all-gather
  32.2 9.5 all_gather.23
  47.3 9.2 reduce-window.6
  58.1 10.4 scatter_custom_fusion
  68.7 2.9 fusion.89
  74.1 11.4 all-gather.8.cloned.1.call-done
  85.5 2.9 fusion.87
  89.3 1.5 fusion.91
  92.1 1.9 copy-done
  94.0 1.6 fusion.17
  95.6 27.0 %all-gather.10.cloned.1.call-done = bf16[1024,1024]{1,0:T(8,128)(2,1)} async-done(((bf16[256,1024]{1,0:T(8,128)(2,1)}), bf16[1024,1024]{1,0:T(8,128)(2,1)}) %all-gather.10.cloned.1.call-update) | async-done | bytes 2097168 | tf_op jit(solution)/shard_map/all_gather | solution.py:132
  122.7 2.6 multiply_reduce_fusion.2
  128.4 2.1 fusion.2
  130.5 2.9 concatenate.33
  133.4 20.6 %gather_fusion.3 = bf16[3840,1024]{1,0:T(8,128)(2,1)} fusion(bf16[2561,1024]{1,0:T(8,128)(2,1)} %concatenate.33, s32[4096]{0:T(1024)S(1)} %get-tuple-element.57), kind=kCustom, calls=%fused_computation.3 | custom fusion | bytes 15744000 | tf_op jit(solution)/shard_map/gather | solution.py:215
  154.0 5.1 all-to-all-start.2
  159.2 12.7 gather_fusion.1
  171.8 159.9 %all-to-all-done.2 = bf16[32,120,1024]{2,1,0:T(8,128)(2,1)} async-done(((bf16[32,120,1024]{2,1,0:T(8,128)(2,1)}), bf16[32,120,1024]{2,1,0:T(8,128)(2,1)}, u32[]{:S(2)}, u32[]{:S(2)}) %all-to-all-start.2) | async-done | bytes 7864352 | tf_op jit(solution)/shard_map/all_to_all | solution.py:218
  331.8 4.9 all-to-all-start
  336.7 7.7 copy.122
  344.3 165.0 %all-to-all-done = bf16[32,120,1024]{2,1,0:T(8,128)(2,1)} async-done(((bf16[32,120,1024]{2,1,0:T(8,128)(2,1)}), bf16[32,120,1024]{2,1,0:T(8,128)(2,1)}, u32[]{:S(2)}, u32[]{:S(2)}) %all-to-all-start) | async-done | bytes 7864352 | tf_op jit(solution)/shard_map/all_to_all | solution.py:185
  509.3 4.2 copy.116
  513.5 17.5 %fusion.93 = f32[4,960,1024]{2,1,0:T(8,128)} fusion(bf16[4,960,1024]{2,1,0:T(8,128)(2,1)S(1)} %bitcast.152, bf16[4,1024,1024]{2,1,0:T(8,128)(2,1)} %param.19), kind=kOutput, calls=%fused_computation.194 | convolution fusion | flops 8053063680 | bytes 31981568 | tf_op jit(solution)/shard_map/erd,edf->erf/dot_general | solution.py:186
  531.0 17.5 %fusion.18 = (f32[4,960,512]{2,1,0:T(8,128)}, f32[4,960,512]{2,1,0:T(8,128)}, bf16[4,960,512]{2,1,0:T(8,128)(2,1)}) fusion(f32[4,960,1024]{2,1,0:T(8,128)} %fusion.93, bf16[4,960,1024]{2,1,0:T(8,128)(2,1)} %bitcast.154, bf16[4,512,1024]{2,1,0:T(8,128)(2,1)} %param.20), kind=kOutput, calls=%fused_computation.59 | convolution fusion | flops 4057989120 | bytes 47448064 | tf_op jit(solution)/shard_map/erd,efd->erf/dot_general | solution.py:219
  548.5 16.0 %convolution_convert_fusion.1 = bf16[4,960,1024]{2,1,0:T(8,128)(2,1)} fusion(bf16[4,1024,1024]{2,1,0:T(8,128)(2,1)} %param.19, f32[4,960,512]{2,1,0:T(8,128)} %get-tuple-element.25, f32[4,960,512]{2,1,0:T(8,128)} %get-tuple-element.24), kind=kOutput, calls=%fused_computation.29 | convolution fusion | flops 8064860160 | bytes 31981568 | tf_op jit(solution)/shard_map/erf,edf->erd/dot_general | solution.py:226
  564.5 12.3 copy.123
  576.8 5.3 all-to-all-start.3
  582.1 10.7 convolution_convert_fusion.2
  592.8 12.4 copy.117
  605.2 149.6 %all-to-all-done.3 = bf16[4,960,1024]{2,0,1:T(4,128)(2,1)} async-done(((bf16[4,960,1024]{2,0,1:T(4,128)(2,1)}), bf16[4,960,1024]{2,0,1:T(4,128)(2,1)}, u32[]{:S(2)}, u32[]{:S(2)}) %all-to-all-start.3) | async-done | bytes 7864352 | tf_op jit(solution)/shard_map/all_to_all | solution.py:232
  754.8 4.9 all-to-all-start.1
  759.9 11.0 convolution_convert_fusion.3
  771.6 9.4 copy.124
  781.0 151.3 %all-to-all-done.1 = bf16[4,960,1024]{2,0,1:T(4,128)(2,1)} async-done(((bf16[4,960,1024]{2,0,1:T(4,128)(2,1)}), bf16[4,960,1024]{2,0,1:T(4,128)(2,1)}, u32[]{:S(2)}, u32[]{:S(2)}) %all-to-all-start.1) | async-done | bytes 7864352 | tf_op jit(solution)/shard_map/all_to_all | solution.py:192
  932.3 9.3 copy.118
  941.6 16.6 %gather_fusion.4 = bf16[2560,1024]{1,0:T(8,128)(2,1)} fusion(bf16[3840,1024]{1,0:T(8,128)(2,1)} %bitcast.146, s32[3072]{0:T(1024)S(1)} %pad_clamp_fusion.2), kind=kCustom, calls=%fused_computation.4 | custom fusion | bytes 10496000 | tf_op jit(solution)/shard_map/gather | solution.py:233
  958.2 16.5 %gather_fusion.2 = bf16[2560,1024]{1,0:T(8,128)(2,1)} fusion(bf16[3840,1024]{1,0:T(8,128)(2,1)} %bitcast.147, s32[3072]{0:T(1024)S(1)} %pad_clamp_fusion.2), kind=kCustom, calls=%fused_computation.2 | custom fusion | bytes 10496000 | tf_op jit(solution)/shard_map/gather | solution.py:194
  974.7 7.7 fusion.1
  982.7 6.9 convert_reduce_fusion
  991.6 2.6 convolution_convert_fusion.4
  994.8 2.5 convolution_convert_fusion.7
  998.4 9.0 fusion.3
  1007.4 7.1 fusion.5
  1014.5 3.6 broadcast_multiply_fusion
  1020.3 2.8 convolution_convert_fusion.5
  1023.2 3.0 bitcast_multiply_fusion.2
  1027.3 2.8 convolution_convert_fusion.6
  1031.3 15.6 %convolution_convert_fusion = bf16[4,1024,1024]{2,1,0:T(8,128)(2,1)} fusion(bf16[4,960,1024]{2,1,0:T(8,128)(2,1)} %bitcast.153, f32[4,960,512]{2,1,0:T(8,128)} %get-tuple-element.25, f32[4,960,512]{2,1,0:T(8,128)} %get-tuple-element.24), kind=kOutput, calls=%fused_computation.28 | convolution fusion | flops 8065122304 | bytes 31981568 | tf_op jit(solution)/shard_map/erd,erf->edf/dot_general | solution.py:229
  1048.8 2.8 convert_element_type.228
  1051.6 3.8 fusion.94
  1055.5 10.1 reduce-scatter.9.cloned.1.call-done
  1065.6 38.5 %reduce-scatter.7.cloned.1.call-done = bf16[256,1024]{1,0:T(8,128)(2,1)} async-done(((bf16[1024,1024]{1,0:T(8,128)(2,1)}), bf16[256,1024]{1,0:T(8,128)(2,1)}) %reduce-scatter.7.cloned.1.call-update) | async-done | bytes 524304 | tf_op jit(solution)/shard_map/reduce_scatter | solution.py:293
  1104.1 3.6 fusion.20
  1107.7 8.9 all-reduce.8
  1116.8 1.4 fusion.22
  1118.2 12.8 reduce-scatter.13.cloned.1.call-done
  1131.0 28.1 %all-reduce.6 = (bf16[256]{0:T(256)(128)(2,1)S(1)}, bf16[256]{0:T(256)(128)(2,1)S(1)}, bf16[256,32]{0,1:T(8,128)(2,1)S(1)}) all-reduce(bf16[256]{0:T(256)(128)(2,1)S(1)} %dynamic-slice.1, bf16[256]{0:T(256)(128)(2,1)S(1)} %dynamic-slice.3, ...), channel_id=1, replica_groups=mesh['dp'=4,'expert'=8] {'expert'}, use_global_device_ids=true, to_apply=%region_21.22 | all-reduce | flops 8704 | bytes 34816 | tf_op jit(solution)/shard_map/psum | solution.py:310
  1160.9 60.0 %reduce-scatter.15.cloned.1.call-done = bf16[4,256,1024]{2,1,0:T(8,128)(2,1)} async-done(((bf16[4,1024,1024]{2,1,0:T(8,128)(2,1)}), bf16[4,256,1024]{2,1,0:T(8,128)(2,1)}) %reduce-scatter.15.cloned.1.call-update) | async-done | bytes 2097168 | tf_op jit(solution)/shard_map/reduce_scatter | solution.py:238
  1220.9 4.1 convert_element_type.226
  1224.9 60.3 %all-reduce.11.cloned.1.call-done = (bf16[256,1024]{1,0:T(8,128)(2,1)}, bf16[256,1024]{1,0:T(8,128)(2,1)}, bf16[256,1024]{1,0:T(8,128)(2,1)}) async-done(((bf16[256,1024]{1,0:T(8,128)(2,1)}, bf16[256,1024]{1,0:T(8,128)(2,1)}, bf16[256,1024]{1,0:T(8,128)(2,1)}), (bf16[256,1024]{1,0:T(8,128)(2,1)}, bf16[256,1024]{1,0:T(8,128)(2,1)}, bf16[256,1024]{1,0:T(8,128)(2,1)})) %all-reduce.11.cloned.1.call-update) | async-done | bytes 1572880 | tf_op jit(solution)/shard_map/psum | solution.py:311
  1285.3 2.1 convert_element_type.216
  1287.4 2.1 convert_element_type.218
  1289.5 2.1 convert_element_type.220
  (226 shorter events, 34.6 us)
Async XLA Ops:
  7.2 61.5 %all-gather.6.cloned.1.call-start = ((), (), s32[]{:S(2)}) async-start(), calls=%async_computation.10 | async-start | bytes 2621440 | tf_op jit(solution)/shard_map/all_gather | solution.py:131
  7.9 77.6 %all-gather.8.cloned.1.call-start = ((), (), s32[]{:S(2)}) async-start(), calls=%async_computation.11 | async-start | bytes 2621440 | tf_op jit(solution)/shard_map/all_gather | solution.py:130
  8.7 114.0 %all-gather.10.cloned.1.call-start = ((), (), s32[]{:S(2)}) async-start(), calls=%async_computation.12 | async-start | bytes 2621440 | tf_op jit(solution)/shard_map/all_gather | solution.py:132
  11.0 57.5 %copy-start.20 = (bf16[320,1024]{1,0:T(8,128)(2,1)S(1)}, bf16[320,1024]{1,0:T(8,128)(2,1)}, u32[]{:S(2)}) copy-start(bf16[320,1024]{1,0:T(8,128)(2,1)} %param.21) | copy-start | bytes 1966084
  14.6 28.5 %copy-start.52 = (f32[320]{0:T(512)}, f32[320]{0:T(512)S(1)}, u32[]{:S(2)}) copy-start(f32[320]{0:T(512)S(1)} %fusion.23) | copy-start | bytes 3844
  14.6 70.9 %copy-start.58 = (f32[320]{0:T(512)}, f32[320]{0:T(512)S(1)}, u32[]{:S(2)}) copy-start(f32[320]{0:T(512)S(1)} %fusion.78) | copy-start | bytes 3844
  24.1 101.2 %copy-start.42 = (f32[4,1,256]{2,1,0:T(1,128)}, f32[4,1,256]{2,1,0:T(1,128)S(1)}, u32[]{:S(2)}) copy-start(f32[4,1,256]{2,1,0:T(1,128)S(1)} %convert_element_type.232) | copy-start | bytes 12292
  32.1 53.3 %copy-start.56 = (f32[4,1,256]{2,1,0:T(1,128)}, f32[4,1,256]{2,1,0:T(1,128)S(1)}, u32[]{:S(2)}) copy-start(f32[4,1,256]{2,1,0:T(1,128)S(1)} %convert_element_type.231) | copy-start | bytes 12292
  43.9 24.7 %copy-start.12 = (bf16[320,1024]{1,0:T(8,128)(2,1)S(1)}, bf16[320,1024]{1,0:T(8,128)(2,1)}, u32[]{:S(2)}) copy-start(bf16[320,1024]{1,0:T(8,128)(2,1)} %param.12) | copy-start | bytes 1966084
  68.6 59.7 %copy-start.3 = (f32[320,1024]{1,0:T(8,128)}, f32[320,1024]{1,0:T(8,128)S(1)}, u32[]{:S(2)}) copy-start(f32[320,1024]{1,0:T(8,128)S(1)} %convert_element_type.200) | copy-start | bytes 3932164
  74.0 14.8 %copy-start.16 = (bf16[320,8,64,1]{0,2,3,1:T(8,128)(2,1)}, bf16[320,8,64,1]{0,2,3,1:T(8,128)(2,1)S(1)}, u32[]{:S(2)}) copy-start(bf16[320,8,64,1]{0,2,3,1:T(8,128)(2,1)S(1)} %fusion.35) | copy-start | bytes 983044
  74.0 14.5 %copy-start.27 = (f32[320,64]{0,1:T(8,128)S(1)}, f32[320,64]{0,1:T(8,128)}, u32[]{:S(2)}) copy-start(f32[320,64]{0,1:T(8,128)} %get-tuple-element.40) | copy-start | bytes 245764
  90.8 3.1 copy-start
  90.8 3.2 copy-start.36
  90.8 3.2 copy-start.22
  92.1 2.0 copy-start.40
  95.6 29.7 %copy-start.18 = (bf16[8,64,2,320]{3,1,2,0:T(8,128)(2,1)}, bf16[8,64,2,320]{3,1,2,0:T(8,128)(2,1)S(1)}, u32[]{:S(2)}) copy-start(bf16[8,64,2,320]{3,1,2,0:T(8,128)(2,1)S(1)} %fusion.17) | copy-start | bytes 1966084
  95.6 30.9 %copy-start.29 = (bf16[1024,32]{0,1:T(8,128)(2,1)S(1)}, bf16[1024,32]{0,1:T(8,128)(2,1)}, u32[]{:S(2)}) copy-start(bf16[1024,32]{0,1:T(8,128)(2,1)} %all_gather.23) | copy-start | bytes 196612
  122.7 4.2 copy-start.38
  125.2 5.2 copy-start.54
  125.3 1.7 copy-start.48
  126.5 32.6 %copy-start.7 = (bf16[320,1024]{1,0:T(8,128)(2,1)}, bf16[320,1024]{1,0:T(8,128)(2,1)S(1)}, u32[]{:S(2)}) copy-start(bf16[320,1024]{1,0:T(8,128)(2,1)S(1)} %multiply_convert_fusion.1) | copy-start | bytes 1966084
  128.2 5.2 copy-start.24
  154.0 177.7 %all-to-all-start.2 = ((bf16[32,120,1024]{2,1,0:T(8,128)(2,1)}), bf16[32,120,1024]{2,1,0:T(8,128)(2,1)}, u32[]{:S(2)}, u32[]{:S(2)}) async-start(bf16[32,120,1024]{2,1,0:T(8,128)(2,1)} %bitcast.151), calls=%async_computation.2 | async-start | bytes 15728640 | tf_op jit(solution)/shard_map/all_to_all | solution.py:218
  331.8 177.6 %all-to-all-start = ((bf16[32,120,1024]{2,1,0:T(8,128)(2,1)}), bf16[32,120,1024]{2,1,0:T(8,128)(2,1)}, u32[]{:S(2)}, u32[]{:S(2)}) async-start(bf16[32,120,1024]{2,1,0:T(8,128)(2,1)} %bitcast.150), calls=%async_computation | async-start | bytes 15728640 | tf_op jit(solution)/shard_map/all_to_all | solution.py:185
  513.5 17.5 %copy-start.9 = (bf16[4,8,120,1024]{3,2,1,0:T(8,128)(2,1)}, bf16[4,8,120,1024]{3,2,1,0:T(8,128)(2,1)S(1)}, u32[]{:S(2)}) copy-start(bf16[4,8,120,1024]{3,2,1,0:T(8,128)(2,1)S(1)} %copy.116) | copy-start | bytes 23592964
  576.8 178.0 %all-to-all-start.3 = ((bf16[4,960,1024]{2,0,1:T(4,128)(2,1)}), bf16[4,960,1024]{2,0,1:T(4,128)(2,1)}, u32[]{:S(2)}, u32[]{:S(2)}) async-start(bf16[4,960,1024]{2,0,1:T(4,128)(2,1)} %copy.123), calls=%async_computation.3 | async-start | bytes 15728640 | tf_op jit(solution)/shard_map/all_to_all | solution.py:232
  754.8 177.5 %all-to-all-start.1 = ((bf16[4,960,1024]{2,0,1:T(4,128)(2,1)}), bf16[4,960,1024]{2,0,1:T(4,128)(2,1)}, u32[]{:S(2)}, u32[]{:S(2)}) async-start(bf16[4,960,1024]{2,0,1:T(4,128)(2,1)} %copy.117), calls=%async_computation.1 | async-start | bytes 15728640 | tf_op jit(solution)/shard_map/all_to_all | solution.py:192
  759.6 289.2 %reduce-scatter.17.cloned.1.call-start = ((), (), s32[]{:S(2)}) async-start(), calls=%async_computation.18 | async-start | bytes 5242880 | tf_op jit(solution)/shard_map/reduce_scatter | solution.py:241
  770.9 284.6 %reduce-scatter.11.cloned.1.call-start = ((), (), s32[]{:S(2)}) async-start(), calls=%async_computation.15 | async-start | bytes 2621440 | tf_op jit(solution)/shard_map/reduce_scatter | solution.py:299
  958.2 16.5 %copy-start.4 = (f32[320,1024]{1,0:T(8,128)S(1)}, f32[320,1024]{1,0:T(8,128)}, u32[]{:S(2)}) copy-start(f32[320,1024]{1,0:T(8,128)} %copy-done.3) | copy-start | bytes 3932164
  958.2 16.5 %copy-start.25 = (f32[320,8]{1,0:T(8,128)S(1)}, f32[320,8]{1,0:T(8,128)}, u32[]{:S(2)}) copy-start(f32[320,8]{1,0:T(8,128)} %copy-done.24) | copy-start | bytes 30724
  974.6 7.9 copy-start.33
  974.6 7.9 copy-start.45
  974.6 7.8 copy-start.51
  974.7 7.9 copy-start.39
  982.4 7.2 copy-start.2
  982.4 7.2 copy-start.30
  982.4 7.2 copy-start.43
  982.4 7.2 copy-start.49
  982.6 7.6 copy-start.55
  982.6 7.6 copy-start.15
  982.7 7.6 copy-start.21
  991.6 5.7 copy-start.5
  991.6 3.1 copy-start.37
  991.6 3.1 copy-start.41
  994.2 4.2 copy-start.23
  994.3 71.3 %reduce-scatter.9.cloned.1.call-start = ((), (), s32[]{:S(2)}) async-start(), calls=%async_computation.14 | async-start | bytes 2621440 | tf_op jit(solution)/shard_map/reduce_scatter | solution.py:296
  998.4 9.0 slice-start
  998.4 9.0 slice-start.1
  1007.4 7.1 copy-start.28
  1014.5 3.7 copy-start.26
  1014.5 3.8 copy-start.10
  1018.3 2.0 copy-start.13
  1018.3 2.0 copy-start.57
  1018.3 2.0 copy-start.59
  1019.6 3.6 copy-start.17
  1023.1 80.9 %reduce-scatter.7.cloned.1.call-start = ((), (), s32[]{:S(2)}) async-start(), calls=%async_computation.13 | async-start | bytes 2621440 | tf_op jit(solution)/shard_map/reduce_scatter | solution.py:293
  1026.7 3.5 copy-start.8
  1030.1 100.9 %reduce-scatter.13.cloned.1.call-start = ((), (), s32[]{:S(2)}) async-start(), calls=%async_computation.16 | async-start | bytes 81920 | tf_op jit(solution)/shard_map/reduce_scatter | solution.py:305
  1031.1 189.8 %reduce-scatter.15.cloned.1.call-start = ((), (), s32[]{:S(2)}) async-start(), calls=%async_computation.17 | async-start | bytes 10485760 | tf_op jit(solution)/shard_map/reduce_scatter | solution.py:238
  1047.0 238.3 %all-reduce.11.cloned.1.call-start = ((), (), s32[]{:S(2)}) async-start(), calls=%async_computation.19 | async-start | bytes 3145728 | tf_op jit(solution)/shard_map/psum | solution.py:311
  1104.1 12.7 copy-start.53
  1104.1 12.7 copy-start.6
  (13 other events, 11.6 us)
Sparse Core Ops, SparseCore 0:
  9.9 38.3 all-gather.5
  50.1 35.3 all-gather.7
  87.3 35.2 all-gather.9
  771.0 53.0 reduce-scatter.16
  994.4 33.1 reduce-scatter.10
  1030.4 35.1 reduce-scatter.8
  1068.8 35.2 reduce-scatter.6
  1107.4 23.6 reduce-scatter.12
  1134.4 86.4 reduce-scatter.14
  1223.3 61.9 all-reduce.10
where the time goes:
time: 1300 us
  waiting for transfers between devices  848 us (65%)
  local copies, waits for them, and re-layouts  152 us (12%)
  matrix products  138 us (11%)
  blocking collectives  64.1 us (5%)
  other arithmetic  59.5 us (5%)
  starting transfers between devices  21.3 us (2%)
  between operations  16 us (1%)
    all_to_all x1, waiting for transfers between devices, shards(): lax.all_to_all(sent_rows, 'expert', split_axis=0, concat_axis=1, tiled=True)  165 us
    all_to_all x1, waiting for transfers between devices, shards(): lax.all_to_all(grad_sent, 'expert', split_axis=0, concat_axis=1, tiled=True)  160 us
    all_to_all x1, waiting for transfers between devices, shards(): lax.all_to_all(expert_made, 'expert', split_axis=1, concat_axis=0, tiled=...  151 us
    all_to_all x1, waiting for transfers between devices, shards(): lax.all_to_all(grad_in_rows, 'expert', split_axis=1, concat_axis=0, tiled...  150 us
    psum x1, waiting for transfers between devices, shards(): lax.psum(pieces[1].astype(jnp.bfloat16), 'expert').astype(jnp.float32)  60.3 us
    reduce_scatter x1, waiting for transfers between devices, shards(): lax.psum_scatter(grad_in_w.astype(jnp.bfloat16), 'dp', scatter_dimension=...  60 us
    reduce_scatter x1, waiting for transfers between devices, shards(): lax.psum_scatter(grad_w_q.astype(jnp.bfloat16), 'dp', scatter_dimension=0...  38.5 us
    psum x1, blocking collectives, shards(): lax.psum(pieces[0].astype(jnp.bfloat16), 'expert').astype(jnp.float32)  28.1 us
  transfers between devices with their start and end apart: 14, of which 11 were waited for; matrix products, arithmetic and copies ran while one was open for 18% of the time, Pallas kernels for 0%

commit v1 on v0

--- a/solution.py
+++ b/solution.py
@@ -87,22 +87,6 @@
     width_ff = gate_up.shape[-1] // 2
     gate_part = gate_up[..., :width_ff]
     return gate_part / (1.0 + jnp.exp(-gate_part)) * gate_up[..., width_ff:]
-
-
-def slot_tables(route_rows, capacity):
-    flat_routes = route_rows.reshape(-1)
-    row_total = flat_routes.shape[0]
-    expert_ids = jnp.arange(EXPERTS, dtype=jnp.int32)
-    route_hot = (flat_routes[:, None] == expert_ids[None, :]).astype(jnp.int32)
-    before = jnp.cumsum(route_hot, axis=0) - route_hot
-    slot_rank = jnp.sum(before * route_hot, axis=1)
-    slot_index = flat_routes * capacity + slot_rank
-    source = (
-        jnp.full((EXPERTS * capacity,), row_total, jnp.int32)
-        .at[slot_index]
-        .set(jnp.arange(row_total, dtype=jnp.int32))
-    )
-    return (slot_index, source)
 
 
 def shards(
@@ -176,64 +160,84 @@
     picked = jnp.sum(route_hot * logits[:, None, :], axis=2)
     picked_exp = jnp.exp(picked - jnp.max(picked, axis=1, keepdims=True))
     gate_weights = picked_exp / jnp.sum(picked_exp, axis=1, keepdims=True)
-    slot_index, source = slot_tables(routes, capacity)
-    zero_row = jnp.zeros((1, width), jnp.bfloat16)
-    token_of_slot = jnp.where(source < tree_rows * TOPK, source // TOPK, tree_rows)
-    sent_rows = jnp.concatenate([hidden2, zero_row], axis=0)[token_of_slot].reshape(
-        EXPERTS, capacity, width
-    )
-    received = lax.all_to_all(sent_rows, "expert", split_axis=0, concat_axis=1, tiled=True)
-    gate_up = jnp.einsum("erd,edf->erf", received, expert_in, preferred_element_type=jnp.float32)
+    trees = lax.axis_size("expert")
+    here = lax.axis_index("expert")
+    local = expert_in.shape[0]
+    first = here * local
+    routes_all = lax.all_gather(routes, "expert", axis=0, tiled=False)
+    grad_y = lax.all_gather(cotangent, "expert", axis=0, tiled=False)
+    hidden_all = lax.all_gather(hidden2, "expert", axis=0, tiled=False)
+    own_ids = first + jnp.arange(local, dtype=jnp.int32)
+    hot_all = routes_all[:, :, :, None] == expert_ids[None, None, None, :]
+    chosen_all = jnp.any(hot_all, axis=2)
+    chosen = jnp.any(routes_all[:, :, :, None] == own_ids[None, None, None, :], axis=2)
+    lower = jnp.tril(jnp.ones((tree_rows, tree_rows), jnp.bfloat16), -1)
+    rank = jnp.einsum(
+        "tu,jue->jet", lower, chosen.astype(jnp.bfloat16), preferred_element_type=jnp.float32
+    ).astype(jnp.int32)
+    slots = jnp.arange(capacity, dtype=jnp.int32)
+    chosen_t = chosen.transpose(0, 2, 1)
+    place = (rank[:, :, None, :] == slots[None, None, :, None]) & chosen_t[:, :, None, :]
+    place = place.astype(jnp.bfloat16)
+    logits_all = jnp.einsum(
+        "jtd,de->jte", hidden_all, router_full, preferred_element_type=jnp.float32
+    )
+    masked = jnp.where(chosen_all, logits_all, -1e30)
+    weight = jnp.exp(masked - jnp.max(masked, axis=-1, keepdims=True))
+    weight = weight / jnp.sum(weight, axis=-1, keepdims=True)
+    gates_own = lax.dynamic_slice_in_dim(weight, first, local, axis=2)
+    gate_slot = jnp.einsum(
+        "jest,jte->ejs", place.astype(jnp.float32), gates_own, precision=lax.Precision.HIGHEST
+    )[..., None]
+    sent = jnp.einsum("jest,jtd->ejsd", place, hidden_all, preferred_element_type=jnp.float32)
+    sent = sent.astype(jnp.bfloat16)
+    grad_rows = jnp.einsum("jest,jtd->ejsd", place, grad_y, preferred_element_type=jnp.float32)
+    grad_rows = grad_rows.astype(jnp.bfloat16)
+    gate_up = jnp.einsum("ejsd,edf->ejsf", sent, expert_in, preferred_element_type=jnp.float32)
     activated, glu_back = jax.vjp(gated_unit, gate_up)
-    act_low = activated.astype(jnp.bfloat16)
-    expert_made = jnp.einsum(
-        "erf,efd->erd", act_low, expert_out, preferred_element_type=jnp.float32
-    ).astype(jnp.bfloat16)
-    returned = lax.all_to_all(expert_made, "expert", split_axis=1, concat_axis=0, tiled=True)
-    back_rows = (
-        returned.reshape(EXPERTS * capacity, width)[slot_index]
-        .reshape(tree_rows, TOPK, width)
-        .astype(jnp.float32)
-    )
-    result = middle + jnp.sum(gate_weights[:, :, None] * back_rows, axis=1)
+    act_low = activated.astype(jnp.bfloat16).astype(jnp.float32)
+    act_scaled = (act_low * gate_slot).astype(jnp.bfloat16)
+    made = jnp.einsum(
+        "ejsf,efd->ejsd", act_scaled, expert_out, preferred_element_type=jnp.float32
+    ).astype(jnp.bfloat16)
+    out_part = jnp.einsum("jest,ejsd->jtd", place, made, preferred_element_type=jnp.float32)
+    out_sum = lax.psum_scatter(
+        out_part.astype(jnp.bfloat16), "expert", scatter_dimension=0, tiled=False
+    ).astype(jnp.float32)
+    result = middle + out_sum
     block_out = result.astype(jnp.bfloat16)
     grad_result = cotangent.astype(jnp.float32)
-    grad_gates = jnp.sum(back_rows * grad_result[:, None, :], axis=-1)
-    grad_picked = gate_weights * (
-        grad_gates - jnp.sum(gate_weights * grad_gates, axis=1, keepdims=True)
-    )
-    grad_logits = jnp.sum(route_hot * grad_picked[:, :, None], axis=1).astype(jnp.bfloat16)
+    grad_act = jnp.einsum(
+        "ejsd,efd->ejsf", grad_rows, expert_out, preferred_element_type=jnp.float32
+    )
+    gate_dot = jnp.sum(act_low * grad_act, axis=-1)
+    gates_back = jnp.einsum(
+        "jest,ejs->jte", place.astype(jnp.float32), gate_dot, precision=lax.Precision.HIGHEST
+    )
+    grad_out_w = jnp.einsum(
+        "ejsf,ejsd->efd", act_scaled, grad_rows, preferred_element_type=jnp.float32
+    )
+    grad_gate_up = glu_back(grad_act * gate_slot)[0].astype(jnp.bfloat16)
+    grad_sent = jnp.einsum(
+        "ejsf,edf->ejsd", grad_gate_up, expert_in, preferred_element_type=jnp.float32
+    ).astype(jnp.bfloat16)
+    grad_in_w = jnp.einsum(
+        "ejsd,ejsf->edf", sent, grad_gate_up, preferred_element_type=jnp.float32
+    )
+    hid_part = jnp.einsum("jest,ejsd->jtd", place, grad_sent, preferred_element_type=jnp.float32)
+    gates_mine = lax.all_to_all(gates_back, "expert", split_axis=0, concat_axis=2, tiled=True)[0]
+    hid_sum = lax.psum_scatter(
+        hid_part.astype(jnp.bfloat16), "expert", scatter_dimension=0, tiled=False
+    ).astype(jnp.float32)
+    gate_dense = jnp.sum(route_hot * gate_weights[:, :, None], axis=1)
+    grad_logits = (
+        gate_dense
+        * (gates_mine - jnp.sum(gate_dense * gates_mine, axis=1, keepdims=True))
+    ).astype(jnp.bfloat16)
     grad_router = jnp.einsum("td,te->de", hidden2, grad_logits, preferred_element_type=jnp.float32)
-    grad_hidden2 = jnp.einsum(
+    grad_hidden2 = hid_sum + jnp.einsum(
         "te,de->td", grad_logits, router_full, preferred_element_type=jnp.float32
     )
-    grad_copies = (
-        (gate_weights[:, :, None] * grad_result[:, None, :])
-        .astype(jnp.bfloat16)
-        .reshape(tree_rows * TOPK, width)
-    )
-    grad_sent = jnp.concatenate([grad_copies, zero_row], axis=0)[source].reshape(
-        EXPERTS, capacity, width
-    )
-    grad_received = lax.all_to_all(grad_sent, "expert", split_axis=0, concat_axis=1, tiled=True)
-    grad_act = jnp.einsum(
-        "erd,efd->erf", grad_received, expert_out, preferred_element_type=jnp.float32
-    )
-    grad_out_w = jnp.einsum(
-        "erf,erd->efd", act_low, grad_received, preferred_element_type=jnp.float32
-    )
-    grad_gate_up = glu_back(grad_act)[0].astype(jnp.bfloat16)
-    grad_in_rows = jnp.einsum(
-        "erf,edf->erd", grad_gate_up, expert_in, preferred_element_type=jnp.float32
-    ).astype(jnp.bfloat16)
-    grad_in_w = jnp.einsum(
-        "erd,erf->edf", received, grad_gate_up, preferred_element_type=jnp.float32
-    )
-    grad_back = lax.all_to_all(grad_in_rows, "expert", split_axis=1, concat_axis=0, tiled=True)
-    grad_rows_back = grad_back.reshape(EXPERTS * capacity, width)[slot_index].reshape(
-        tree_rows, TOPK, width
-    )
-    grad_hidden2 = grad_hidden2 + jnp.sum(grad_rows_back.astype(jnp.float32), axis=1)
     expert_in_share, expert_out_share = (
         lax.psum_scatter(
             grad_in_w.astype(jnp.bfloat16), "dp", scatter_dimension=1, tiled=True

time: 1300 us -> 837 us (0.64)
  waiting for transfers between devices: 848 us -> 492 us
  local copies, waits for them, and re-layouts: 152 us -> 12.8 us
  matrix products: 138 us -> 190 us
  other arithmetic: 59.5 us -> 34.4 us
  starting transfers between devices: 21.3 us -> 4.37 us
  blocking collectives: 64.1 us -> 78 us
    all_to_all x4 -> x1, waiting for transfers between devices: 626 us -> 6.42 us  [shards(): lax.all_to_all(gates_back, 'expert', split_axis=0, concat_axis=2, tiled=T...]
    reduce_scatter x0 -> x2, waiting for transfers between devices: none -> 82.3 us  [the longest x1 58.3 us: shards(): lax.psum_scatter(out_part.astype(jnp.bfloat16), 'expert', scatter_dimensi...]
    all_gather x0 -> x2, waiting for transfers between devices: none -> 75.6 us  [the longest x1 45.4 us: shards(): hidden_all = lax.all_gather(hidden2, 'expert', axis=0, tiled=False)]
    gather x4 -> x0, local copies, waits for them, and re-layouts: 66.3 us -> none  [the longest x1 20.6 us: shards(): jnp.concatenate([grad_copies, zero_row], axis=0)[source]]
    dot_general x6 -> x14, matrix products: 88.2 us -> 139 us  [the longest x1 18.6 us: shards(): jnp.einsum('ejsd,efd->ejsf', grad_rows, expert_out, preferred_element_typ...]
    reduce_scatter x1, waiting for transfers between devices: 0.02 us -> 38.8 us  [shards(): lax.psum_scatter(grad_out_w.astype(jnp.bfloat16), 'dp', scatter_dimension...]
    reduce_scatter x1, waiting for transfers between devices: 0.01 us -> 38 us  [shards(): lax.psum_scatter(grad_w_out.astype(jnp.bfloat16), 'dp', scatter_dimension...]
    all_to_all x4 -> x0, local copies, waits for them, and re-layouts: 30.5 us -> none  [the longest x1 9.39 us: shards(): lax.all_to_all(grad_in_rows, 'expert', split_axis=1, concat_axis=0, tiled...]
  transfers between devices with their start and end apart: 14 -> 15, of which waited for: 11 -> 15; matrix products, arithmetic and copies ran while one was open for 18% -> 14% of each run, Pallas kernels for 0% -> 0%
where the time goes in v1:
time: 837 us; the launch traced here: 828 us
  waiting for transfers between devices  492 us (59%)
  matrix products  190 us (23%)
  blocking collectives  78 us (9%)
  other arithmetic  34.4 us (4%)
  between operations  15.7 us (2%)
  local copies, waits for them, and re-layouts  12.8 us (2%)
    reduce_scatter x1, waiting for transfers between devices, shards(): lax.psum_scatter(grad_in_w.astype(jnp.bfloat16), 'dp', scatter_dimension=...  83 us
    reduce_scatter x1, waiting for transfers between devices, shards(): lax.psum_scatter(out_part.astype(jnp.bfloat16), 'expert', scatter_dimensi...  58.3 us
    all_gather x1, waiting for transfers between devices, shards(): hidden_all = lax.all_gather(hidden2, 'expert', axis=0, tiled=False)  45.4 us
    reduce_scatter x1, waiting for transfers between devices, shards(): lax.psum_scatter(grad_w_q.astype(jnp.bfloat16), 'dp', scatter_dimension=0...  39.1 us
    reduce_scatter x1, waiting for transfers between devices, shards(): lax.psum_scatter(grad_out_w.astype(jnp.bfloat16), 'dp', scatter_dimension...  38.8 us
    reduce_scatter x1, waiting for transfers between devices, shards(): lax.psum_scatter(grad_w_out.astype(jnp.bfloat16), 'dp', scatter_dimension...  38 us
    all_gather x1, waiting for transfers between devices, shards(): lax.all_gather(w_query, 'dp', axis=0, tiled=True)  33.2 us
    psum x1, waiting for transfers between devices, shards(): lax.psum(pieces[1].astype(jnp.bfloat16), 'expert').astype(jnp.float32)  31.9 us
  transfers between devices with their start and end apart: 15, of which 15 were waited for; matrix products, arithmetic and copies ran while one was open for 14% of the time, Pallas kernels for 0%

profile of v1, /device:TPU:0, one launch (start us, length us, event | category | flops | bytes accessed | tf_op | source)
XLA Modules:
  0.0 827.8 jit_solution(3863279979970076853)
XLA Ops:
  10.7 9.5 %all-gather.3 = bf16[4,1,256]{2,1,0:T(2,128)(2,1)S(1)} all-gather(bf16[1,1,256]{2,1,0:T(2,128)(2,1)S(1)} %reshape.270), channel_id=1, replica_groups=mesh['dp'=4,'expert'=8] {'dp'}, dimensions={0}, use_global_device_ids=true | all-gather | bytes 2560 | tf_op jit(solution)/shard_map/all_gather | solution.py:113
  20.9 1.3 gather_fusion
  24.0 8.0 all-gather.5
  33.9 14.0 %all-gather.12.cloned.1.call-done = bf16[1024,1024]{1,0:T(8,128)(2,1)} async-done(((bf16[256,1024]{1,0:T(8,128)(2,1)}), bf16[1024,1024]{1,0:T(8,128)(2,1)}) %all-gather.12.cloned.1.call-update) | async-done | bytes 2097168 | tf_op jit(solution)/shard_map/all_gather | solution.py:115
  47.9 2.5 fusion.117
  51.9 33.2 %all-gather.14.cloned.1.call-done = bf16[1024,1024]{1,0:T(8,128)(2,1)} async-done(((bf16[256,1024]{1,0:T(8,128)(2,1)}), bf16[1024,1024]{1,0:T(8,128)(2,1)}) %all-gather.14.cloned.1.call-update) | async-done | bytes 2097168 | tf_op jit(solution)/shard_map/all_gather | solution.py:114
  85.1 2.9 fusion.115
  88.5 1.5 fusion.125
  90.0 1.2 fusion.14
  91.2 1.9 copy-done
  93.2 1.6 fusion.45
  94.8 27.5 %all-gather.16.cloned.1.call-done = bf16[1024,1024]{1,0:T(8,128)(2,1)} async-done(((bf16[256,1024]{1,0:T(8,128)(2,1)}), bf16[1024,1024]{1,0:T(8,128)(2,1)}) %all-gather.16.cloned.1.call-update) | async-done | bytes 2097168 | tf_op jit(solution)/shard_map/all_gather | solution.py:116
  122.3 2.6 multiply_reduce_fusion.2
  126.0 14.3 %all-gather.4 = s32[8,320,8]{1,2,0:T(8,128)S(1)} all-gather(s32[1,320,8]{1,2,0:T(8,128)S(1)} %bitcast.194), channel_id=2, replica_groups=mesh['dp'=4,'expert'=8] {'expert'}, dimensions={0}, use_global_device_ids=true | all-gather | bytes 92160 | tf_op jit(solution)/shard_map/all_gather | solution.py:167
  140.9 8.6 %all_gather.45 = bf16[1024,32]{0,1:T(8,128)(2,1)S(1)} all-gather(bf16[256,32]{0,1:T(8,128)(2,1)S(1)} %copy-done.31), channel_id=1, replica_groups=mesh['dp'=4,'expert'=8] {'dp'}, dimensions={0}, use_global_device_ids=true | all-gather | bytes 81920 | tf_op jit(solution)/shard_map/all_gather | solution.py:118
  150.0 30.2 %all-gather.20.cloned.1.call-done = bf16[2560,1024]{1,0:T(8,128)(2,1)} async-done(((bf16[320,1024]{1,0:T(8,128)(2,1)}), bf16[2560,1024]{1,0:T(8,128)(2,1)}) %all-gather.20.cloned.1.call-update) | async-done | bytes 5242896 | tf_op jit(solution)/shard_map/all_gather | solution.py:168
  180.2 10.8 %convert_bitcast_fusion = bf16[4,8,120,1024]{3,2,0,1:T(8,128)(2,1)} fusion(bf16[8,320,1024,1]{2,1,3,0:T(8,128)(2,1)} %bitcast.176, s32[8,4,320]{2,1,0:T(4,128)S(1)} %copy.93, pred[8,4,320]{2,1,0:T(4,128)(4,1)S(1)} %bitcast.199), kind=kOutput, calls=%fused_computation.26 | convolution fusion | flops 2522972160 | bytes 13158400 | tf_op jit(solution)/shard_map/jest,jtd->ejsd/dot_general | solution.py:194
  191.1 45.4 %all-gather.18.cloned.1.call-done = bf16[2560,1024]{1,0:T(8,128)(2,1)} async-done(((bf16[320,1024]{1,0:T(8,128)(2,1)}), bf16[2560,1024]{1,0:T(8,128)(2,1)}) %all-gather.18.cloned.1.call-update) | async-done | bytes 5242896 | tf_op jit(solution)/shard_map/all_gather | solution.py:169
  236.5 11.7 %convert_bitcast_fusion.1 = bf16[4,8,120,1024]{3,2,0,1:T(8,128)(2,1)} fusion(bf16[8,320,1024,1]{2,1,3,0:T(8,128)(2,1)} %bitcast.177, s32[8,4,320]{2,1,0:T(4,128)S(1)} %copy.93, pred[8,4,320]{2,1,0:T(4,128)(4,1)S(1)} %bitcast.200), kind=kOutput, calls=%fused_computation.31 | convolution fusion | flops 2522972160 | bytes 13158400 | tf_op jit(solution)/shard_map/jest,jtd->ejsd/dot_general | solution.py:192
  248.2 1.7 fusion.126
  250.1 6.7 fusion.23
  256.9 13.8 %fusion = f32[4,8,120,1024]{3,2,1,0:T(8,128)} fusion(bf16[4,1024,1024]{2,1,0:T(8,128)(2,1)S(1)} %bitcast.212, bf16[4,8,120,1024]{3,2,0,1:T(8,128)(2,1)} %convert_bitcast_fusion.1), kind=kOutput, calls=%fused_computation.7 | convolution fusion | flops 8053063680 | bytes 31981568 | tf_op jit(solution)/shard_map/ejsd,edf->ejsf/dot_general | solution.py:196
  270.7 18.6 %multiply_multiply_fusion = (f32[4,8,120,512]{3,2,1,0:T(8,128)}, f32[4,8,120,512]{3,2,1,0:T(8,128)}, f32[4,8,120]{2,1,0:T(8,128)S(1)}, bf16[4,8,120,512]{3,2,1,0:T(8,128)(2,1)}) fusion(f32[4,8,120]{2,1,0:T(8,128)S(1)} %bitcast.213, f32[4,8,120,1024]{3,2,1,0:T(8,128)} %fusion, bf16[4,512,1024]{2,1,0:T(8,128)(2,1)} %param.20, ...), kind=kOutput, calls=%fused_computation.34 | convolution fusion | flops 4065849600 | bytes 47478784 | tf_op jit(solution)/shard_map/ejsd,efd->ejsf/dot_general | solution.py:210
  289.3 15.8 %fusion.2 = bf16[4,8,120,1024]{3,2,0,1:T(8,128)(2,1)} fusion(bf16[4,1024,1024]{2,1,0:T(8,128)(2,1)} %param.19, f32[4,8,120,512]{3,2,1,0:T(8,128)} %get-tuple-element.27, f32[4,8,120,512]{3,2,1,0:T(8,128)} %get-tuple-element.26), kind=kOutput, calls=%fused_computation.10 | convolution fusion | flops 8060928000 | bytes 31981568 | tf_op jit(solution)/shard_map/ejsf,edf->ejsd/dot_general | solution.py:221
  305.1 9.1 %bitcast_convert_fusion.1 = bf16[8,320,1024]{2,1,0:T(8,128)(2,1)} fusion(bf16[4,8,120,1024]{3,2,0,1:T(8,128)(2,1)} %fusion.2, s32[8,4,320]{2,1,0:T(4,128)S(1)} %copy.93, pred[8,4,320]{2,1,0:T(4,128)(4,1)S(1)} %bitcast.202), kind=kOutput, calls=%fused_computation.3 | convolution fusion | flops 2521661440 | bytes 13158400 | tf_op jit(solution)/shard_map/jest,ejsd->jtd/dot_general | solution.py:227
  314.3 7.7 fusion.26
  322.1 8.2 bitcast_convert_fusion.2
  330.2 1.1 copy-done.3
  331.8 7.5 fusion.79
  340.0 3.3 all-to-all-start
  343.5 6.4 all-to-all-done
  350.0 24.0 %reduce-scatter.11.cloned.1.call-done = bf16[1,320,1024]{2,1,0:T(8,128)(2,1)} async-done(((bf16[8,320,1024]{2,1,0:T(8,128)(2,1)}), bf16[1,320,1024]{2,1,0:T(8,128)(2,1)}) %reduce-scatter.11.cloned.1.call-update) | async-done | bytes 655376 | tf_op jit(solution)/shard_map/reduce_scatter | solution.py:229
  373.9 2.3 multiply_reduce_fusion
  376.2 58.3 %reduce-scatter.9.cloned.1.call-done = bf16[1,320,1024]{2,1,0:T(8,128)(2,1)} async-done(((bf16[8,320,1024]{2,1,0:T(8,128)(2,1)}), bf16[1,320,1024]{2,1,0:T(8,128)(2,1)}) %reduce-scatter.9.cloned.1.call-update) | async-done | bytes 655376 | tf_op jit(solution)/shard_map/reduce_scatter | solution.py:204
  434.6 2.7 fusion.48
  437.3 1.1 copy-done.1
  439.2 1.2 copy.98
  440.4 9.0 %fusion.6 = (f32[8,2,320]{2,1,0:T(2,128)}, f32[8,320,320,2]{2,1,3,0:T(8,128)}) fusion(f32[8,2,320,320]{2,3,1,0:T(8,128)} %copy-done, f32[8,2,320]{2,1,0:T(2,128)S(1)} %bitcast.186, bf16[320,8,64,1]{0,2,3,1:T(8,128)(2,1)} %bitcast.181, bf16[320,8,2,64]{0,3,2,1:T(8,128)(2,1)} %bitcast.170), kind=kOutput, calls=%fused_computation.16 | convolution fusion | flops 214625280 | bytes 14131200 | tf_op jit(solution)/shard_map/tkgd,skd->kgts/dot_general | solution.py:262
  449.4 5.2 fusion.56
  454.6 6.9 fusion.8
  461.6 3.6 broadcast_multiply_fusion
  465.4 2.8 convolution_convert_fusion.1
  468.4 3.0 bitcast_multiply_fusion.1
  472.8 2.8 convolution_convert_fusion.2
  475.7 2.6 convolution_convert_fusion
  478.4 11.5 %bitcast_convert_fusion.3 = bf16[4,512,1024]{2,1,0:T(8,128)(2,1)} fusion(bf16[4,8,120,1024]{3,2,0,1:T(8,128)(2,1)} %convert_bitcast_fusion, bf16[4,8,120,512]{3,2,1,0:T(8,128)(2,1)} %get-tuple-element.29, f32[4,8,120]{2,1,0:T(8,128)S(1)} %bitcast.215), kind=kOutput, calls=%fused_computation.9 | convolution fusion | flops 4034527232 | bytes 16006144 | tf_op jit(solution)/shard_map/ejsf,ejsd->efd/dot_general | solution.py:217
  491.9 10.0 %reduce-scatter.15.cloned.1.call-done = bf16[256,1024]{1,0:T(8,128)(2,1)} async-done(((bf16[1024,1024]{1,0:T(8,128)(2,1)}), bf16[256,1024]{1,0:T(8,128)(2,1)}) %reduce-scatter.15.cloned.1.call-update) | async-done | bytes 524304 | tf_op jit(solution)/shard_map/reduce_scatter | solution.py:300
  501.9 39.1 %reduce-scatter.13.cloned.1.call-done = bf16[256,1024]{1,0:T(8,128)(2,1)} async-done(((bf16[1024,1024]{1,0:T(8,128)(2,1)}), bf16[256,1024]{1,0:T(8,128)(2,1)}) %reduce-scatter.13.cloned.1.call-update) | async-done | bytes 524304 | tf_op jit(solution)/shard_map/reduce_scatter | solution.py:297
  541.0 38.0 %reduce-scatter.17.cloned.1.call-done = bf16[256,1024]{1,0:T(8,128)(2,1)} async-done(((bf16[1024,1024]{1,0:T(8,128)(2,1)}), bf16[256,1024]{1,0:T(8,128)(2,1)}) %reduce-scatter.17.cloned.1.call-update) | async-done | bytes 524304 | tf_op jit(solution)/shard_map/reduce_scatter | solution.py:303
  579.3 15.6 %bitcast_convert_fusion = bf16[4,1024,1024]{2,1,0:T(8,128)(2,1)} fusion(bf16[4,8,120,1024]{3,2,0,1:T(8,128)(2,1)} %convert_bitcast_fusion.1, f32[4,8,120,512]{3,2,1,0:T(8,128)} %get-tuple-element.27, f32[4,8,120,512]{3,2,1,0:T(8,128)} %get-tuple-element.26), kind=kOutput, calls=%fused_computation.1 | convolution fusion | flops 8065122304 | bytes 31981568 | tf_op jit(solution)/shard_map/ejsd,ejsf->edf/dot_general | solution.py:224
  596.8 38.8 %reduce-scatter.23.cloned.1.call-done = bf16[4,128,1024]{2,1,0:T(8,128)(2,1)} async-done(((bf16[4,512,1024]{2,1,0:T(8,128)(2,1)}), bf16[4,128,1024]{2,1,0:T(8,128)(2,1)}) %reduce-scatter.23.cloned.1.call-update) | async-done | bytes 1048592 | tf_op jit(solution)/shard_map/reduce_scatter | solution.py:245
  635.6 2.8 convert_element_type.250
  638.4 2.9 fusion.128
  641.3 2.3 fusion.47
  643.6 8.9 %all-reduce.6 = (bf16[1024]{0:T(1024)(128)(2,1)S(1)}, bf16[1024]{0:T(1024)(128)(2,1)S(1)}) all-reduce(bf16[1024]{0:T(1024)(128)(2,1)S(1)} %get-tuple-element.12, bf16[1024]{0:T(1024)(128)(2,1)S(1)} %copy-done.34), channel_id=7, replica_groups=mesh['dp'=4,'expert'=8] {'dp'}, use_global_device_ids=true, to_apply=%region_20.21.clone | all-reduce | flops 2048 | bytes 8192
  652.7 9.8 %reduce-scatter.19.cloned.1.call-done = bf16[256,32]{0,1:T(8,128)(2,1)} async-done(((bf16[1024,32]{0,1:T(8,128)(2,1)}), bf16[256,32]{0,1:T(8,128)(2,1)}) %reduce-scatter.19.cloned.1.call-update) | async-done | bytes 16400 | tf_op jit(solution)/shard_map/reduce_scatter | solution.py:309
  662.4 28.6 %all-reduce.4 = (bf16[256]{0:T(256)(128)(2,1)S(1)}, bf16[256]{0:T(256)(128)(2,1)S(1)}, bf16[256,32]{0,1:T(8,128)(2,1)S(1)}) all-reduce(bf16[256]{0:T(256)(128)(2,1)S(1)} %dynamic-slice.1, bf16[256]{0:T(256)(128)(2,1)S(1)} %dynamic-slice.3, ...), channel_id=1, replica_groups=mesh['dp'=4,'expert'=8] {'expert'}, use_global_device_ids=true, to_apply=%region_21.22 | all-reduce | flops 8704 | bytes 34816 | tf_op jit(solution)/shard_map/psum | solution.py:314
  692.8 2.7 fusion.49
  695.5 31.9 %all-reduce.9.cloned.1.call-done = (bf16[256,1024]{1,0:T(8,128)(2,1)}, bf16[256,1024]{1,0:T(8,128)(2,1)}, bf16[256,1024]{1,0:T(8,128)(2,1)}) async-done(((bf16[256,1024]{1,0:T(8,128)(2,1)}, bf16[256,1024]{1,0:T(8,128)(2,1)}, bf16[256,1024]{1,0:T(8,128)(2,1)}), (bf16[256,1024]{1,0:T(8,128)(2,1)}, bf16[256,1024]{1,0:T(8,128)(2,1)}, bf16[256,1024]{1,0:T(8,128)(2,1)})) %all-reduce.9.cloned.1.call-update) | async-done | bytes 1572880 | tf_op jit(solution)/shard_map/psum | solution.py:315
  727.4 2.1 convert_element_type.238
  729.5 2.1 convert_element_type.240
  731.6 2.1 convert_element_type.242
  733.7 83.0 %reduce-scatter.21.cloned.1.call-done = bf16[4,256,1024]{2,1,0:T(8,128)(2,1)} async-done(((bf16[4,1024,1024]{2,1,0:T(8,128)(2,1)}), bf16[4,256,1024]{2,1,0:T(8,128)(2,1)}) %reduce-scatter.21.cloned.1.call-update) | async-done | bytes 2097168 | tf_op jit(solution)/shard_map/reduce_scatter | solution.py:242
  816.7 4.1 convert_element_type.248
  (176 shorter events, 21.5 us)
Async XLA Ops:
  7.2 16.8 %copy-start.36 = (bf16[256]{0:T(256)(128)(2,1)S(1)}, bf16[256]{0:T(256)(128)(2,1)}, u32[]{:S(2)}) copy-start(bf16[256]{0:T(256)(128)(2,1)} %param.17) | copy-start | bytes 1540
  7.2 26.5 %copy-start.7 = (bf16[320,1024]{1,0:T(8,128)(2,1)S(1)}, bf16[320,1024]{1,0:T(8,128)(2,1)}, u32[]{:S(2)}) copy-start(bf16[320,1024]{1,0:T(8,128)(2,1)} %param.12) | copy-start | bytes 1966084
  7.2 40.7 %all-gather.12.cloned.1.call-start = ((), (), s32[]{:S(2)}) async-start(), calls=%async_computation.9 | async-start | bytes 2621440 | tf_op jit(solution)/shard_map/all_gather | solution.py:115
  7.9 77.2 %all-gather.14.cloned.1.call-start = ((), (), s32[]{:S(2)}) async-start(), calls=%async_computation.10 | async-start | bytes 2621440 | tf_op jit(solution)/shard_map/all_gather | solution.py:114
  8.7 113.6 %all-gather.16.cloned.1.call-start = ((), (), s32[]{:S(2)}) async-start(), calls=%async_computation.11 | async-start | bytes 2621440 | tf_op jit(solution)/shard_map/all_gather | solution.py:116
  9.4 170.8 %all-gather.20.cloned.1.call-start = ((), (), s32[]{:S(2)}) async-start(), calls=%async_computation.21 | async-start | bytes 5898240 | tf_op jit(solution)/shard_map/all_gather | solution.py:168
  10.0 226.5 %all-gather.18.cloned.1.call-start = ((), (), s32[]{:S(2)}) async-start(), calls=%async_computation.20 | async-start | bytes 5898240 | tf_op jit(solution)/shard_map/all_gather | solution.py:169
  20.2 64.9 %copy-start.29 = (f32[4,1,256]{2,1,0:T(1,128)}, f32[4,1,256]{2,1,0:T(1,128)S(1)}, u32[]{:S(2)}) copy-start(f32[4,1,256]{2,1,0:T(1,128)S(1)} %convert_element_type.253) | copy-start | bytes 12292
  33.9 16.9 %copy-start.25 = (f32[320]{0:T(512)}, f32[320]{0:T(512)S(1)}, u32[]{:S(2)}) copy-start(f32[320]{0:T(512)S(1)} %fusion.50) | copy-start | bytes 3844
  33.9 51.2 %copy-start.32 = (f32[320]{0:T(512)}, f32[320]{0:T(512)S(1)}, u32[]{:S(2)}) copy-start(f32[320]{0:T(512)S(1)} %fusion.106) | copy-start | bytes 3844
  88.5 1.5 copy-start.6
  90.0 3.2 copy-start
  90.0 3.2 copy-start.13
  91.2 3.5 copy-start.23
  94.8 31.2 %copy-start.10 = (bf16[8,64,2,320]{3,1,2,0:T(8,128)(2,1)}, bf16[8,64,2,320]{3,1,2,0:T(8,128)(2,1)S(1)}, u32[]{:S(2)}) copy-start(bf16[8,64,2,320]{3,1,2,0:T(8,128)(2,1)S(1)} %fusion.45) | copy-start | bytes 1966084
  122.3 3.7 copy-start.22
  122.3 18.5 %copy-start.31 = (bf16[256,32]{0,1:T(8,128)(2,1)S(1)}, bf16[256,32]{0,1:T(8,128)(2,1)}, u32[]{:S(2)}) copy-start(bf16[256,32]{0,1:T(8,128)(2,1)} %param.18) | copy-start | bytes 49156
  124.9 66.2 %copy-start.27 = (f32[320]{0:T(512)}, f32[320]{0:T(512)S(1)}, u32[]{:S(2)}) copy-start(f32[320]{0:T(512)S(1)} %get-tuple-element.48) | copy-start | bytes 3844
  126.0 248.0 %reduce-scatter.11.cloned.1.call-start = ((), (), s32[]{:S(2)}) async-start(), calls=%async_computation.13 | async-start | bytes 5898240 | tf_op jit(solution)/shard_map/reduce_scatter | solution.py:229
  236.5 20.3 %slice-start.2 = ((s8[8388608]{0:T(1024)(128)(4,1)}), s8[4194304]{0:T(1024)(128)(4,1)S(1)}, s32[]{:S(2)}) async-start(s8[8388608]{0:T(1024)(128)(4,1)} %bitcast.211), calls=%async_computation.25 | async-start | bytes 8388608
  236.5 11.7 %copy-start.9 = (bf16[2560,1024]{1,0:T(8,128)(2,1)S(1)}, bf16[2560,1024]{1,0:T(8,128)(2,1)}, u32[]{:S(2)}) copy-start(bf16[2560,1024]{1,0:T(8,128)(2,1)} %all-gather.18.cloned.1.call-done) | copy-start | bytes 15728644
  236.5 20.3 %slice-start.3 = ((s8[8388608]{0:T(1024)(128)(4,1)}), s8[4194304]{0:T(1024)(128)(4,1)S(1)}, s32[]{:S(2)}) async-start(s8[8388608]{0:T(1024)(128)(4,1)} %bitcast.211), calls=%async_computation.26 | async-start | bytes 8388608
  256.9 57.5 %copy-start.37 = (f32[4,8,1,120]{3,2,1,0:T(1,128)}, f32[4,8,1,120]{3,2,1,0:T(1,128)S(1)}, u32[]{:S(2)}) copy-start(f32[4,8,1,120]{3,2,1,0:T(1,128)S(1)} %fusion.23) | copy-start | bytes 46084
  314.3 120.3 %reduce-scatter.9.cloned.1.call-start = ((), (), s32[]{:S(2)}) async-start(), calls=%async_computation.12 | async-start | bytes 5898240 | tf_op jit(solution)/shard_map/reduce_scatter | solution.py:204
  330.2 1.1 copy-start.3
  330.2 1.6 copy-start.24
  331.6 44.6 %copy-start.28 = (f32[320]{0:T(512)S(1)}, f32[320]{0:T(512)}, u32[]{:S(2)}) copy-start(f32[320]{0:T(512)} %copy-done.27) | copy-start | bytes 3844
  340.0 9.9 %all-to-all-start = ((f32[8,320,4]{1,2,0:T(4,128)}), f32[8,320,4]{1,2,0:T(4,128)S(1)}, u32[]{:S(2)}, u32[]{:S(2)}) async-start(f32[8,320,4]{1,2,0:T(4,128)} %bitcast.162), calls=%async_computation.2 | async-start | bytes 98304 | tf_op jit(solution)/shard_map/all_to_all | solution.py:228
  343.4 158.5 %reduce-scatter.15.cloned.1.call-start = ((), (), s32[]{:S(2)}) async-start(), calls=%async_computation.15 | async-start | bytes 2621440 | tf_op jit(solution)/shard_map/reduce_scatter | solution.py:300
  434.6 3.8 copy-start.12
  437.3 1.1 copy-start.1
  440.4 14.3 %slice-start = ((s8[7864320]{0:T(1024)(128)(4,1)}), s8[4194304]{0:T(1024)(128)(4,1)S(1)}, s32[]{:S(2)}) async-start(s8[7864320]{0:T(1024)(128)(4,1)} %bitcast.168), calls=%async_computation.23 | async-start | bytes 8388608
  440.4 9.1 %copy-start.5 = (bf16[320,1024]{0,1:T(8,128)(2,1)S(1)}, bf16[320,1024]{0,1:T(8,128)(2,1)}, u32[]{:S(2)}) copy-start(bf16[320,1024]{0,1:T(8,128)(2,1)} %copy.98) | copy-start | bytes 1966084
  440.4 14.3 %slice-start.1 = ((s8[7864320]{0:T(1024)(128)(4,1)}), s8[3670016]{0:T(1024)(128)(4,1)S(1)}, s32[]{:S(2)}) async-start(s8[7864320]{0:T(1024)(128)(4,1)} %bitcast.168), calls=%async_computation.24 | async-start | bytes 7340032
  461.5 3.7 copy-start.14
  461.5 3.8 copy-start.8
  461.5 3.8 copy-start.18
  461.5 3.8 copy-start.30
  461.5 3.8 copy-start.33
  465.2 3.2 copy-start.15
  465.3 6.2 copy-start.20
  468.2 72.8 %reduce-scatter.13.cloned.1.call-start = ((), (), s32[]{:S(2)}) async-start(), calls=%async_computation.14 | async-start | bytes 2621440 | tf_op jit(solution)/shard_map/reduce_scatter | solution.py:297
  472.0 0.9 copy-start.16
  472.0 3.7 copy-start.2
  472.0 3.7 copy-start.11
  475.6 2.7 copy-start.38
  475.6 103.3 %reduce-scatter.17.cloned.1.call-start = ((), (), s32[]{:S(2)}) async-start(), calls=%async_computation.16 | async-start | bytes 2621440 | tf_op jit(solution)/shard_map/reduce_scatter | solution.py:303
  478.3 157.3 %reduce-scatter.23.cloned.1.call-start = ((), (), s32[]{:S(2)}) async-start(), calls=%async_computation.19 | async-start | bytes 5242880 | tf_op jit(solution)/shard_map/reduce_scatter | solution.py:245
  489.8 1.1 copy-start.4
  489.9 172.5 %reduce-scatter.19.cloned.1.call-start = ((), (), s32[]{:S(2)}) async-start(), calls=%async_computation.17 | async-start | bytes 81920 | tf_op jit(solution)/shard_map/reduce_scatter | solution.py:309
  491.8 235.5 %all-reduce.9.cloned.1.call-start = ((), (), s32[]{:S(2)}) async-start(), calls=%async_computation.22 | async-start | bytes 3145728 | tf_op jit(solution)/shard_map/psum | solution.py:315
  579.0 237.7 %reduce-scatter.21.cloned.1.call-start = ((), (), s32[]{:S(2)}) async-start(), calls=%async_computation.18 | async-start | bytes 10485760 | tf_op jit(solution)/shard_map/reduce_scatter | solution.py:242
  594.9 0.7 copy-start.39
  594.9 43.5 %copy-start.17 = (bf16[320,8,2,64]{0,3,2,1:T(8,128)(2,1)S(1)}, bf16[320,8,2,64]{0,3,2,1:T(8,128)(2,1)}, u32[]{:S(2)}) copy-start(bf16[320,8,2,64]{0,3,2,1:T(8,128)(2,1)} %copy-done.16) | copy-start | bytes 1966084
  638.4 2.9 copy-start.19
  638.4 2.9 copy-start.21
  638.4 3.0 copy-start.35
  641.3 2.3 copy-start.34
  641.3 51.4 %copy-start.26 = (f32[320]{0:T(512)S(1)}, f32[320]{0:T(512)}, u32[]{:S(2)}) copy-start(f32[320]{0:T(512)} %copy-done.25) | copy-start | bytes 3844
Sparse Core Ops, SparseCore 0:
  9.9 38.0 all-gather.11
  49.8 35.2 all-gather.13
  87.0 35.2 all-gather.15
  123.8 56.3 all-gather.19
  181.7 54.7 all-gather.17
  314.4 59.4 reduce-scatter.10
  376.2 58.2 reduce-scatter.8
  468.3 33.5 reduce-scatter.14
  505.7 35.2 reduce-scatter.12
  543.8 35.1 reduce-scatter.16
  582.8 52.7 reduce-scatter.22
  638.7 23.6 reduce-scatter.18
  665.2 62.1 all-reduce.8
  730.6 86.0 reduce-scatter.20

commit v2 on v1

--- a/solution.py
+++ b/solution.py
@@ -1,6 +1,10 @@
+import functools
+
 import jax
 import jax.numpy as jnp
 from jax import lax
+from jax.experimental import pallas as pl
+from jax.experimental.pallas import tpu as pltpu
 from jax.sharding import PartitionSpec as P
 
 H = 16
@@ -12,6 +16,552 @@
 
 
 EPSILON = 1e-06
+
+
+MESH = pl.DeviceIdType.MESH
+MIB = 1024 * 1024
+VMEM = pltpu.VMEM
+ANY = pl.ANY
+
+
+def remote(src, dst, send_sem, recv_sem, **where):
+    return pltpu.make_async_remote_copy(
+        src_ref=src, dst_ref=dst, send_sem=send_sem, recv_sem=recv_sem,
+        device_id=where, device_id_type=MESH,
+    )
+
+
+def greet(partners):
+    barrier = pltpu.get_barrier_semaphore()
+    for condition, where in partners:
+        def signal(where=where):
+            pl.semaphore_signal(barrier, inc=1, device_id=where, device_id_type=MESH)
+        if condition is None:
+            signal()
+        else:
+            pl.when(condition)(signal)
+    count = sum(1 if c is None else c.astype(jnp.int32) for c, _ in partners)
+    pl.semaphore_wait(barrier, count)
+
+
+def add_rows(out, *terms, step=16):
+    rows = out.shape[0]
+
+    def body(i, carry):
+        at = pl.ds(pl.multiple_of(i * step, step), step)
+        total = terms[0][at, :].astype(jnp.float32)
+        for term in terms[1:]:
+            total = total + term[at, :].astype(jnp.float32)
+        out[at, :] = total.astype(out.dtype)
+        return carry
+
+    lax.fori_loop(0, rows // step, body, 0)
+
+
+def bit_orders(n):
+    bits = [1 << j for j in range(n.bit_length() - 1)]
+    return [bits[p:] + bits[:p] for p in range(len(bits))] or [[]]
+
+
+def weights_body(n_dp, *refs):
+    arrays = 4
+    ins, outs = refs[:arrays], refs[arrays : 2 * arrays]
+    send_sem, recv_sem, pair_send, pair_recv, own_sem = refs[2 * arrays :]
+    me, mine = lax.axis_index("dp"), lax.axis_index("expert")
+    core = lax.rem(mine, 2)
+    pair = mine + 1 - 2 * core
+    orders = bit_orders(n_dp)
+    greet([(None, {"dp": me ^ bit}) for bit in orders[0]] + [(None, {"expert": pair})])
+    shard = ins[0].shape[0]
+    half = shard // 2
+    sends, pairs, owns = [], [], []
+    cuts = min(2, len(orders), half // 16)
+    size = half // cuts
+
+    def pieces(a):
+        return cuts
+
+    def rows(start, side, p):
+        return pl.ds(pl.multiple_of(start + side * half + p * size, 16), size)
+
+    def push(a, p, r, bit):
+        to = me ^ bit
+        there = outs[a].at[rows((me ^ r) * shard, core, p)]
+        src = ins[a].at[rows(0, core, p)] if r == 0 else there
+        copy = remote(src, there, send_sem.at[a, p, r, bit.bit_length() - 1], recv_sem.at[a, p, r ^ bit], dp=to)
+        copy.start()
+        sends.append(copy)
+
+    for a in range(arrays):
+        for p in range(pieces(a)):
+            for bit in orders[p]:
+                push(a, p, 0, bit)
+    for a in range(arrays):
+        copy = pltpu.make_async_copy(
+            ins[a], outs[a].at[pl.ds(pl.multiple_of(me * shard, 16), shard)], own_sem.at[a])
+        copy.start()
+        owns.append(copy)
+    def reach(order):
+        blocks = [0]
+        steps = []
+        for j, bit in enumerate(order):
+            new = [r | bit for r in blocks]
+            steps.append((j, new))
+            blocks = blocks + new
+        return steps
+
+    for j in range(len(orders[0])):
+        for a in range(arrays):
+            for p in range(pieces(a)):
+                order = orders[p]
+                for r in reach(order)[j][1]:
+                    here = outs[a].at[rows((me ^ r) * shard, core, p)]
+                    remote(here, here, send_sem.at[a, p, r, 0], recv_sem.at[a, p, r], dp=me).wait_recv()
+                    for bit in order[j + 1 :]:
+                        push(a, p, r, bit)
+                    copy = remote(here, here, pair_send.at[a, p, r], pair_recv.at[a, p, r], expert=pair)
+                    copy.start()
+                    pairs.append((copy, a, p, r))
+    for copy in owns:
+        copy.wait()
+    for copy in sends:
+        copy.wait_send()
+    for copy, a, p, r in pairs:
+        copy.wait_send()
+        here = outs[a].at[rows((me ^ r) * shard, 1 - core, p)]
+        remote(here, here, pair_send.at[a, p, r], pair_recv.at[a, p, r], expert=pair).wait_recv()
+
+
+def gather_weights(n_dp, arrays, collective_id):
+    orders = bit_orders(n_dp)
+    count, pieces = len(arrays), min(2, len(orders))
+    out_shape = [jax.ShapeDtypeStruct((n_dp * a.shape[0], a.shape[1]), a.dtype) for a in arrays]
+    return pl.pallas_call(
+        functools.partial(weights_body, n_dp),
+        out_shape=out_shape,
+        in_specs=[pl.BlockSpec(memory_space=VMEM)] * count,
+        out_specs=[pl.BlockSpec(memory_space=ANY)] * count,
+        scratch_shapes=[
+            pltpu.SemaphoreType.DMA((count, pieces, n_dp, max(1, n_dp.bit_length() - 1))),
+            pltpu.SemaphoreType.DMA((count, pieces, n_dp)),
+            pltpu.SemaphoreType.DMA((count, pieces, n_dp)),
+            pltpu.SemaphoreType.DMA((count, pieces, n_dp)),
+            pltpu.SemaphoreType.DMA((count,)),
+        ],
+        compiler_params=pltpu.CompilerParams(collective_id=collective_id, has_side_effects=True),
+        name="gather_weights",
+    )(*arrays)
+
+
+class Ring:
+    def __init__(self, n_exp):
+        self.mine = lax.axis_index("expert")
+        self.core = lax.rem(self.mine, 2)
+        self.z = lax.div(self.mine, 2)
+        self.depth = n_exp // 2
+        self.far = self.depth // 2
+        self.pair = self.mine + 1 - 2 * self.core
+        self.right, self.left = self.dev(1), self.dev(-1)
+
+    def dev(self, d):
+        return lax.rem(self.z + d + self.depth, self.depth) * 2 + self.core
+
+    def partners(self):
+        return [(None, {"expert": e}) for e in (self.pair, self.right, self.left)]
+
+
+class RingGather:
+    def __init__(self, ring, own, out, sems):
+        self.ring, self.own, self.out = ring, own, out
+        self.send, self.recv, self.pair_send, self.pair_recv = sems
+        self.half = own.shape[0] // 2
+        self.copies, self.pairs = [], []
+
+    @staticmethod
+    def scratch(n_exp):
+        far, depth = n_exp // 4, n_exp // 2
+        sem = pltpu.SemaphoreType.DMA
+        return [sem((2, far + 1, 2)), sem((2, far + 1, 2)), sem((depth, 2)), sem((depth, 2))]
+
+    def rows(self, h):
+        return pl.ds(h * self.half, self.half)
+
+    def goes(self, side, s, h):
+        far = self.ring.far
+        return s < far or (s == far and h == side)
+
+    def block(self, d, h):
+        return self.out.at[self.ring.dev(d), self.rows(h)]
+
+    def push(self, side, s, h):
+        d = -s if side == 0 else s
+        src = self.own.at[self.rows(h)] if s == 0 else self.block(d, h)
+        to = self.ring.right if side == 0 else self.ring.left
+        copy = remote(src, self.block(d, h), self.send.at[side, s, h], self.recv.at[side, s + 1, h], expert=to)
+        copy.start()
+        self.copies.append(copy)
+
+    def across(self, d, h):
+        src = self.own.at[self.rows(h)] if d == 0 else self.block(d, h)
+        slot = d % self.ring.depth
+        copy = remote(src, self.block(d, h), self.pair_send.at[slot, h], self.pair_recv.at[slot, h], expert=self.ring.pair)
+        copy.start()
+        self.pairs.append((copy, d, h))
+
+    def start(self):
+        for side, h in ((0, 0), (1, 1), (0, 1), (1, 0)):
+            if self.goes(side, 1, h):
+                self.push(side, 0, h)
+        self.across(0, 0)
+        self.across(0, 1)
+
+    def events(self):
+        return [
+            (side, s, h)
+            for s in range(1, self.ring.far + 1)
+            for side, h in ((0, 0), (1, 1), (0, 1), (1, 0))
+            if self.goes(side, s, h)
+        ]
+
+    def handle(self, event):
+        side, s, h = event
+        d = -s if side == 0 else s
+        here = self.block(d, h)
+        remote(here, here, self.send.at[side, s, h], self.recv.at[side, s, h], expert=self.ring.mine).wait_recv()
+        if self.goes(side, s + 1, h):
+            self.push(side, s, h)
+        self.across(d, h)
+
+    def wait_pair(self, d, h):
+        slot = d % self.ring.depth
+        here = self.out.at[self.ring.pair - self.ring.mine + self.ring.dev(d), self.rows(h)]
+        remote(here, here, self.pair_send.at[slot, h], self.pair_recv.at[slot, h], expert=self.ring.mine).wait_recv()
+
+    def finish_pairs(self):
+        for _, d, h in self.pairs:
+            self.wait_pair(d, h)
+
+    def finish_sends(self):
+        for copy in self.copies:
+            copy.wait_send()
+        for copy, _, _ in self.pairs:
+            copy.wait_send()
+
+
+class RingScatter:
+    def __init__(self, ring, part, bufs, sems):
+        self.ring, self.part = ring, part
+        self.pair_buf, self.held, self.got = bufs
+        self.pair_send, self.pair_recv, self.send, self.recv = sems
+        self.half = self.held.shape[1] // 2
+        self.copies = []
+
+    @staticmethod
+    def scratch(n_exp, block, dtype):
+        far, depth = n_exp // 4, n_exp // 2
+        sem = pltpu.SemaphoreType.DMA
+        bufs = [pltpu.VMEM((depth,) + block, dtype), pltpu.VMEM((depth,) + block, dtype),
+                pltpu.VMEM((2, far) + block, dtype)]
+        return bufs, [sem((depth,)), sem((depth,)), sem((2, far + 1, 2)), sem((2, far + 1, 2))]
+
+    def rows(self, h):
+        return pl.ds(h * self.half, self.half)
+
+    def order(self):
+        far, depth = self.ring.far, self.ring.depth
+        order = [far]
+        for s in range(far - 1, 0, -1):
+            order += [s, depth - s]
+        return order + [0]
+
+    def comes(self, side, d, h):
+        far = self.ring.far
+        return d + 1 < far or (d + 1 == far and h == side)
+
+    def across(self, d):
+        ring = self.ring
+        return remote(self.part(ring.dev(d) + 1 - 2 * ring.core), self.pair_buf.at[d],
+                      self.pair_send.at[d], self.pair_recv.at[d], expert=ring.pair)
+
+    def start_pair(self, d):
+        self.across(d).start()
+
+    def wait_pair(self, d):
+        self.across(d).wait_recv()
+
+    def wait_got(self, side, d, h):
+        here = self.got.at[side, d, self.rows(h)]
+        remote(here, here, self.send.at[side, d, h], self.recv.at[side, d, h], expert=self.ring.mine).wait_recv()
+
+    def push(self, side, d, h):
+        ring = self.ring
+        slot = d if side == 0 else ring.depth - d
+        rows = self.rows(h)
+        terms = [self.part(ring.dev(slot)).at[rows], self.pair_buf.at[slot, rows]]
+        if self.comes(side, d, h):
+            self.wait_got(side, d, h)
+            terms.append(self.got.at[side, d, rows])
+        add_rows(self.held.at[slot, rows], *terms)
+        copy = remote(self.held.at[slot, rows], self.got.at[side, d - 1, rows], self.send.at[side, d, h],
+                      self.recv.at[side, d - 1, h], expert=ring.right if side == 0 else ring.left)
+        copy.start()
+        self.copies.append(copy)
+
+    def first(self):
+        far = self.ring.far
+        self.wait_pair(far)
+        self.push(0, far, 0)
+        self.push(1, far, 1)
+
+    def rest(self):
+        ring, far = self.ring, self.ring.far
+        for d in range(far - 1, 0, -1):
+            self.wait_pair(d)
+            self.push(0, d, 1)
+            self.wait_pair(ring.depth - d)
+            self.push(1, d, 0)
+            self.push(0, d, 0)
+            self.push(1, d, 1)
+
+    def last(self, out, *more):
+        self.wait_pair(0)
+        for h in range(2):
+            rows = self.rows(h)
+            terms = [self.part(self.ring.mine).at[rows], self.pair_buf.at[0, rows]] + [m.at[rows] for m in more]
+            for side in range(2):
+                if self.comes(side, 0, h):
+                    self.wait_got(side, 0, h)
+                    terms.append(self.got.at[side, 0, rows])
+            add_rows(out.at[rows], *terms)
+
+    def finish_sends(self):
+        for copy in self.copies:
+            copy.wait_send()
+        for d in range(self.ring.depth):
+            self.across(d).wait_send()
+
+
+def ring_gather_body(n_exp, x_ref, out_ref, own_sem, *sems):
+    ring = Ring(n_exp)
+    greet(ring.partners())
+    own = pltpu.make_async_copy(x_ref, out_ref.at[ring.mine], own_sem)
+    own.start()
+    gather = RingGather(ring, x_ref, out_ref, sems)
+    gather.start()
+    for event in gather.events():
+        gather.handle(event)
+    own.wait()
+    gather.finish_pairs()
+    gather.finish_sends()
+
+
+def ring_gather(n_exp, x, collective_id):
+    return pl.pallas_call(
+        functools.partial(ring_gather_body, n_exp),
+        out_shape=jax.ShapeDtypeStruct((n_exp,) + x.shape, x.dtype),
+        in_specs=[pl.BlockSpec(memory_space=VMEM)],
+        out_specs=pl.BlockSpec(memory_space=ANY),
+        scratch_shapes=[pltpu.SemaphoreType.DMA] + RingGather.scratch(n_exp),
+        compiler_params=pltpu.CompilerParams(collective_id=collective_id, has_side_effects=True),
+        name="ring_gather",
+    )(x)
+
+
+def ring_scatter_body(n_exp, more, part, *refs):
+    extra, (out, *rest) = refs[:more], refs[more:]
+    ring = Ring(n_exp)
+    greet(ring.partners())
+    scatter = RingScatter(ring, lambda e: part.at[e], rest[:3], rest[3:])
+    for d in scatter.order():
+        scatter.start_pair(d)
+    scatter.first()
+    scatter.rest()
+    scatter.last(out, *extra)
+    scatter.finish_sends()
+
+
+def ring_scatter(n_exp, part, more, out_type, collective_id):
+    block = part.shape[1:]
+    bufs, sems = RingScatter.scratch(n_exp, block, part.dtype)
+    return pl.pallas_call(
+        functools.partial(ring_scatter_body, n_exp, len(more)),
+        out_shape=jax.ShapeDtypeStruct(block, out_type),
+        in_specs=[pl.BlockSpec(memory_space=VMEM)] * (1 + len(more)),
+        out_specs=pl.BlockSpec(memory_space=VMEM),
+        scratch_shapes=bufs + sems,
+        compiler_params=pltpu.CompilerParams(
+            collective_id=collective_id, has_side_effects=True, vmem_limit_bytes=48 * MIB),
+        name="ring_scatter",
+    )(part, *more)
+
+
+def grads_body(n_dp, n_exp, chunks, g_ref, out_ref, pair_buf, total, dp_buf, prefix, suffix, go_r, go_l, final, other,
+               pair_send, pair_recv, dp_send, dp_recv, send_r, send_l, recv_r, recv_l, last_send, last_recv):
+    me, mine = lax.axis_index("dp"), lax.axis_index("expert")
+    core = lax.rem(mine, 2)
+    z = lax.div(mine, 2)
+    depth = n_exp // 2
+    pair = mine + 1 - 2 * core
+    has_left, has_right = z > 0, z < depth - 1
+    orders = bit_orders(n_dp)
+    rows = g_ref.shape[0] // n_dp
+    half = rows // 2
+    width = g_ref.shape[1] // chunks
+    greet([(None, {"expert": pair})] + [(None, {"dp": me ^ bit}) for bit in orders[0]]
+          + [(has_left, {"expert": mine - 2}), (has_right, {"expert": mine + 2})])
+
+    def columns(i):
+        return pl.ds(pl.multiple_of(i * width, 128), width)
+
+    def block_of(d, side, i):
+        return g_ref.at[pl.ds(pl.multiple_of(d * rows + side * half, 16), half), columns(i)]
+
+    def across(i, d):
+        return remote(block_of(d, 1 - core, i), pair_buf.at[i, d], pair_send.at[i, d], pair_recv.at[i, d], expert=pair)
+
+    for i in range(chunks):
+        for d in range(n_dp):
+            across(i, d).start()
+
+    def moved(i, j):
+        order = orders[i % len(orders)]
+        blocks = [0]
+        for bit in order[j + 1 :]:
+            blocks = blocks + [r | bit for r in blocks]
+        return order[j], [r | order[j] for r in blocks]
+
+    def dp_copy(i, j, r, bit):
+        return remote(total.at[i, r], dp_buf.at[i, r ^ bit, j], dp_send.at[i, r], dp_recv.at[i, r ^ bit, j], dp=me ^ bit)
+
+    stages = len(orders[0])
+    for i in range(chunks):
+        for r in range(n_dp - 1, -1, -1):
+            d = me ^ r
+            across(i, d).wait_recv()
+            add_rows(total.at[i, r], block_of(d, core, i), pair_buf.at[i, d])
+        if stages:
+            bit, blocks = moved(i, 0)
+            for r in blocks:
+                dp_copy(i, 0, r, bit).start()
+    for j in range(stages):
+        for i in range(chunks):
+            bit, blocks = moved(i, j)
+            for r in blocks:
+                kept = r ^ bit
+                dp_copy(i, j, r, bit).wait_recv()
+                add_rows(total.at[i, kept], total.at[i, kept], dp_buf.at[i, kept, j])
+            if j + 1 < stages:
+                bit, blocks = moved(i, j + 1)
+                for r in blocks:
+                    dp_copy(i, j + 1, r, bit).start()
+
+    def right(i):
+        return remote(go_r.at[i], prefix.at[i], send_r.at[i], recv_r.at[i], expert=mine + 2)
+
+    def left(i):
+        return remote(go_l.at[i], suffix.at[i], send_l.at[i], recv_l.at[i], expert=mine - 2)
+
+    def line(t, carry):
+        i = t - z
+
+        @pl.when(jnp.logical_and(i >= 0, i < chunks))
+        def _():
+            @pl.when(has_left)
+            def _():
+                remote(go_r.at[i], prefix.at[i], send_r.at[i], recv_r.at[i], expert=mine).wait_recv()
+
+            @pl.when(jnp.logical_and(has_left, has_right))
+            def _():
+                add_rows(go_r.at[i], total.at[i, 0], prefix.at[i])
+
+            @pl.when(jnp.logical_not(has_left))
+            def _():
+                add_rows(go_r.at[i], total.at[i, 0])
+
+            pl.when(has_right)(lambda: right(i).start())
+
+        k = t - (depth - 1 - z)
+
+        @pl.when(jnp.logical_and(k >= 0, k < chunks))
+        def _():
+            @pl.when(has_right)
+            def _():
+                remote(go_l.at[k], suffix.at[k], send_l.at[k], recv_l.at[k], expert=mine).wait_recv()
+
+            @pl.when(jnp.logical_and(has_left, has_right))
+            def _():
+                add_rows(go_l.at[k], total.at[k, 0], suffix.at[k])
+
+            @pl.when(jnp.logical_not(has_right))
+            def _():
+                add_rows(go_l.at[k], total.at[k, 0])
+
+            pl.when(has_left)(lambda: left(k).start())
+
+        return carry
+
+    lax.fori_loop(0, chunks + depth - 1, line, 0)
+
+    def last(i):
+        return remote(final.at[i], other.at[i], last_send.at[i], last_recv.at[i], expert=pair)
+
+    for i in range(chunks):
+        @pl.when(jnp.logical_and(has_left, has_right))
+        def _():
+            add_rows(final.at[i], total.at[i, 0], prefix.at[i], suffix.at[i])
+
+        @pl.when(jnp.logical_not(has_left))
+        def _():
+            add_rows(final.at[i], total.at[i, 0], suffix.at[i])
+
+        @pl.when(jnp.logical_not(has_right))
+        def _():
+            add_rows(final.at[i], total.at[i, 0], prefix.at[i])
+
+        last(i).start()
+
+    def place(side, i):
+        return out_ref.at[pl.ds(pl.multiple_of(side * half, 16), half), columns(i)]
+
+    for i in range(chunks):
+        add_rows(place(core, i), final.at[i])
+    for i in range(chunks):
+        last(i).wait_recv()
+        add_rows(place(1 - core, i), other.at[i])
+        last(i).wait_send()
+        pl.when(has_right)(lambda: right(i).wait_send())
+        pl.when(has_left)(lambda: left(i).wait_send())
+        for d in range(n_dp):
+            across(i, d).wait_send()
+        for j in range(stages):
+            bit, blocks = moved(i, j)
+            for r in blocks:
+                dp_copy(i, j, r, bit).wait_send()
+
+
+def reduce_grads(n_dp, n_exp, grads, chunks, collective_id):
+    rows = grads.shape[0] // n_dp
+    half, width = rows // 2, grads.shape[1] // chunks
+    stages = max(1, n_dp.bit_length() - 1)
+    sem = pltpu.SemaphoreType.DMA
+    one = pltpu.VMEM((chunks, half, width), grads.dtype)
+    return pl.pallas_call(
+        functools.partial(grads_body, n_dp, n_exp, chunks),
+        out_shape=jax.ShapeDtypeStruct((rows, grads.shape[1]), jnp.float32),
+        in_specs=[pl.BlockSpec(memory_space=VMEM)],
+        out_specs=pl.BlockSpec(memory_space=VMEM),
+        scratch_shapes=[
+            pltpu.VMEM((chunks, n_dp, half, width), grads.dtype),
+            pltpu.VMEM((chunks, n_dp, half, width), grads.dtype),
+            pltpu.VMEM((chunks, n_dp, stages, half, width), grads.dtype),
+            one, one, one, one, one, one,
+            sem((chunks, n_dp)), sem((chunks, n_dp)), sem((chunks, n_dp)), sem((chunks, n_dp, stages)),
+            sem((chunks,)), sem((chunks,)), sem((chunks,)), sem((chunks,)), sem((chunks,)), sem((chunks,)),
+        ],
+        compiler_params=pltpu.CompilerParams(
+            collective_id=collective_id, has_side_effects=True, vmem_limit_bytes=56 * MIB),
+        name="reduce_grads",
+    )(grads)
 
 
 def tree_layout(tree_rows):
@@ -109,15 +659,16 @@
     groups = H // KV
     kv_width = KV * HD
     score_scale = HD ** (-0.5)
-    gathered = (
-        lax.all_gather(attn_gain, "dp", axis=0, tiled=True),
-        lax.all_gather(w_query, "dp", axis=0, tiled=True),
-        lax.all_gather(w_keyval, "dp", axis=0, tiled=True),
-        lax.all_gather(w_output, "dp", axis=0, tiled=True),
-        lax.all_gather(moe_gain, "dp", axis=0, tiled=True),
-        lax.all_gather(w_router, "dp", axis=0, tiled=True),
-    )
-    gain_first, query_full, keyval_full, output_full, gain_second, router_full = gathered
+    n_dp, n_exp = lax.axis_size("dp"), lax.axis_size("expert")
+    rows = w_query.shape[0]
+    small = jnp.concatenate(
+        [w_router, attn_gain[:, None], moe_gain[:, None], jnp.zeros((rows, 128 - EXPERTS - 2), w_router.dtype)], axis=1
+    )
+    query_full, keyval_full, output_full, small_full = gather_weights(
+        n_dp, (w_query, w_keyval, w_output, small), 1
+    )
+    router_full = small_full[:, :EXPERTS]
+    gain_first, gain_second = small_full[:, EXPERTS], small_full[:, EXPERTS + 1]
     inputs = tokens.astype(jnp.float32)
     segment, position = tree_layout(tree_rows)
     allowed = path_allowed(parents[0], segment)
@@ -166,7 +717,7 @@
     first = here * local
     routes_all = lax.all_gather(routes, "expert", axis=0, tiled=False)
     grad_y = lax.all_gather(cotangent, "expert", axis=0, tiled=False)
-    hidden_all = lax.all_gather(hidden2, "expert", axis=0, tiled=False)
+    hidden_all = ring_gather(n_exp, hidden2, 2)
     own_ids = first + jnp.arange(local, dtype=jnp.int32)
     hot_all = routes_all[:, :, :, None] == expert_ids[None, None, None, :]
     chosen_all = jnp.any(hot_all, axis=2)
@@ -201,11 +752,7 @@
         "ejsf,efd->ejsd", act_scaled, expert_out, preferred_element_type=jnp.float32
     ).astype(jnp.bfloat16)
     out_part = jnp.einsum("jest,ejsd->jtd", place, made, preferred_element_type=jnp.float32)
-    out_sum = lax.psum_scatter(
-        out_part.astype(jnp.bfloat16), "expert", scatter_dimension=0, tiled=False
-    ).astype(jnp.float32)
-    result = middle + out_sum
-    block_out = result.astype(jnp.bfloat16)
+    block_out = ring_scatter(n_exp, out_part.astype(jnp.bfloat16), (middle,), jnp.bfloat16, 3)
     grad_result = cotangent.astype(jnp.float32)
     grad_act = jnp.einsum(
         "ejsd,efd->ejsf", grad_rows, expert_out, preferred_element_type=jnp.float32
@@ -226,9 +773,7 @@
     )
     hid_part = jnp.einsum("jest,ejsd->jtd", place, grad_sent, preferred_element_type=jnp.float32)
     gates_mine = lax.all_to_all(gates_back, "expert", split_axis=0, concat_axis=2, tiled=True)[0]
-    hid_sum = lax.psum_scatter(
-        hid_part.astype(jnp.bfloat16), "expert", scatter_dimension=0, tiled=False
-    ).astype(jnp.float32)
+    hid_sum = ring_scatter(n_exp, hid_part.astype(jnp.bfloat16), (), jnp.float32, 4)
     gate_dense = jnp.sum(route_hot * gate_weights[:, :, None], axis=1)
     grad_logits = (
         gate_dense
@@ -290,33 +835,33 @@
     ) + jnp.einsum("ti,di->td", grad_keyval_pre, keyval_full, preferred_element_type=jnp.float32)
     grad_in_norm, grad_gain_first = first_back(grad_hidden)
     input_grad = grad_middle + grad_in_norm
-    pieces = (
-        lax.psum_scatter(
-            grad_gain_first.astype(jnp.bfloat16), "dp", scatter_dimension=0, tiled=True
-        ).astype(jnp.float32),
-        lax.psum_scatter(
-            grad_w_q.astype(jnp.bfloat16), "dp", scatter_dimension=0, tiled=True
-        ).astype(jnp.float32),
-        lax.psum_scatter(
-            grad_w_kv.astype(jnp.bfloat16), "dp", scatter_dimension=0, tiled=True
-        ).astype(jnp.float32),
-        lax.psum_scatter(
-            grad_w_out.astype(jnp.bfloat16), "dp", scatter_dimension=0, tiled=True
-        ).astype(jnp.float32),
-        lax.psum_scatter(
-            grad_gain_second.astype(jnp.bfloat16), "dp", scatter_dimension=0, tiled=True
-        ).astype(jnp.float32),
-        lax.psum_scatter(
-            grad_router.astype(jnp.bfloat16), "dp", scatter_dimension=0, tiled=True
-        ).astype(jnp.float32),
-    )
+    low = jnp.bfloat16
+    share = reduce_grads(
+        n_dp,
+        n_exp,
+        jnp.concatenate(
+            [
+                grad_w_q.astype(low),
+                grad_w_kv.astype(low),
+                grad_w_out.astype(low),
+                grad_router.astype(low),
+                grad_gain_first.astype(low)[:, None],
+                grad_gain_second.astype(low)[:, None],
+                jnp.zeros((width, 128 - EXPERTS - 2), low),
+            ],
+            axis=1,
+        ),
+        5,
+        5,
+    )
+    at = 3 * width
     shares = (
-        lax.psum(pieces[0].astype(jnp.bfloat16), "expert").astype(jnp.float32),
-        lax.psum(pieces[1].astype(jnp.bfloat16), "expert").astype(jnp.float32),
-        lax.psum(pieces[2].astype(jnp.bfloat16), "expert").astype(jnp.float32),
-        lax.psum(pieces[3].astype(jnp.bfloat16), "expert").astype(jnp.float32),
-        lax.psum(pieces[4].astype(jnp.bfloat16), "expert").astype(jnp.float32),
-        lax.psum(pieces[5].astype(jnp.bfloat16), "expert").astype(jnp.float32),
+        share[:, at + EXPERTS],
+        share[:, :width],
+        share[:, width : 2 * width],
+        share[:, 2 * width : at],
+        share[:, at + EXPERTS + 1],
+        share[:, at : at + EXPERTS],
     )
     return (
         block_out,

time: 837 us -> 551 us (0.66)
  waiting for transfers between devices: 492 us -> 0.72 us
  Pallas kernels: 0 us -> 265 us
  blocking collectives: 78 us -> 15.2 us
  local copies, waits for them, and re-layouts: 12.8 us -> 36.2 us
  matrix products: 190 us -> 177 us
    pallas_call x0 -> x5, Pallas kernels: none -> 265 us  [the longest x2 104 us: ring_scatter(): pl.pallas_call(functools.partial(ring_scatter_body, n_exp, len(more)), ou...]
    reduce_scatter x6 -> x0, waiting for transfers between devices: 179 us -> none  [the longest x1 58.3 us: shards(): lax.psum_scatter(out_part.astype(jnp.bfloat16), 'expert', scatter_dimensi...]
    all_gather x4 -> x0, waiting for transfers between devices: 120 us -> none  [the longest x1 45.4 us: shards(): hidden_all = lax.all_gather(hidden2, 'expert', axis=0, tiled=False)]
    reduce_scatter x1, waiting for transfers between devices: 83 us -> 0.01 us  [shards(): lax.psum_scatter(grad_in_w.astype(jnp.bfloat16), 'dp', scatter_dimension=...]
    reduce_scatter x1, waiting for transfers between devices: 38.8 us -> 0.01 us  [shards(): lax.psum_scatter(grad_out_w.astype(jnp.bfloat16), 'dp', scatter_dimension...]
    psum x1 -> x0, waiting for transfers between devices: 31.9 us -> none  [shards(): lax.psum(pieces[1].astype(jnp.bfloat16), 'expert').astype(jnp.float32)]
    all_gather x1, waiting for transfers between devices: 30.2 us -> 0.01 us  [shards(): grad_y = lax.all_gather(cotangent, 'expert', axis=0, tiled=False)]
    psum x1 -> x0, blocking collectives: 28.6 us -> none  [shards(): lax.psum(pieces[0].astype(jnp.bfloat16), 'expert').astype(jnp.float32)]
  transfers between devices with their start and end apart: 15 -> 4, of which waited for: 15 -> 0; matrix products, arithmetic and copies ran while one was open for 14% -> 35% of each run, Pallas kernels for 0% -> 49%
where the time goes in v2:
time: 551 us; the launch traced here: 541 us
  Pallas kernels  265 us (48%)
  matrix products  177 us (32%)
  local copies, waits for them, and re-layouts  36.2 us (7%)
  other arithmetic  27.4 us (5%)
  between operations  15.3 us (3%)
  blocking collectives  15.2 us (3%)
    pallas_call x2, Pallas kernels, ring_scatter(): pl.pallas_call(functools.partial(ring_scatter_body, n_exp, len(more)), ou...  104 us
    pallas_call x1, Pallas kernels, reduce_grads(): pl.pallas_call(functools.partial(grads_body, n_dp, n_exp, chunks), out_sh...  76 us
    pallas_call x1, Pallas kernels, ring_gather(): pl.pallas_call(functools.partial(ring_gather_body, n_exp), out_shape=jax....  49.5 us
    pallas_call x1, Pallas kernels, gather_weights(): pl.pallas_call(functools.partial(weights_body, n_dp), out_shape=out_shape...  35.7 us
    dot_general x1, matrix products, shards(): jnp.einsum('ejsd,efd->ejsf', grad_rows, expert_out, preferred_element_typ...  18.6 us
    dot_general x1, matrix products, shards(): jnp.einsum('ejsf,edf->ejsd', grad_gate_up, expert_in, preferred_element_t...  15.9 us
    dot_general x1, matrix products, shards(): jnp.einsum('ejsd,ejsf->edf', sent, grad_gate_up, preferred_element_type=j...  15.6 us
    all_gather x1, blocking collectives, shards(): routes_all = lax.all_gather(routes, 'expert', axis=0, tiled=False)  15.2 us
  transfers between devices with their start and end apart: 4, of which 0 were waited for; matrix products, arithmetic and copies ran while one was open for 35% of the time, Pallas kernels for 49%

profile of v2, /device:TPU:0, one launch (start us, length us, event | category | flops | bytes accessed | tf_op | source)
XLA Modules:
  0.0 541.4 jit_solution(6599329964955401146)
XLA Ops:
  8.0 0.8 broadcast_in_dim.58
  8.8 0.8 broadcast_in_dim.59
  9.5 0.8 copy.146
  10.4 0.7 maximum_maximum_fusion.refs_3_
  11.2 35.7 %gather_weights.1 = (bf16[1024,1024]{1,0:T(8,128)(2,1)}, bf16[1024,1024]{1,0:T(8,128)(2,1)}, bf16[1024,1024]{1,0:T(8,128)(2,1)}, bf16[1024,128]{1,0:T(8,128)(2,1)}) custom-call(bf16[256,1024]{1,0:T(8,128)(2,1)} %refs_0_.1, bf16[256,1024]{1,0:T(8,128)(2,1)} %refs_1_.1, bf16[256,1024]{1,0:T(8,128)(2,1)} %refs_2_.1, bf16[256,128]{1,0:T(8,128)(2,1)} %maximum_maximum_fusion.refs_3_), custom_call_target="tpu_custom_call" | custom-call | tf_op jit(solution)/shard_map/gather_weights/pallas_call | solution.py:139
  46.9 1.4 convert_reduce_fusion
  48.4 1.3 fusion.51
  51.2 2.5 fusion.121
  56.5 1.3 fusion.119
  58.3 1.5 fusion.130
  59.8 1.2 fusion.14
  61.0 1.9 copy-done.1
  62.9 1.6 fusion.46
  64.5 1.0 multiply_reduce_fusion.2
  65.6 1.0 multiply_convert_fusion.1.x_ref
  66.6 49.5 %ring_gather.1 = bf16[8,320,1024]{2,1,0:T(8,128)(2,1)} custom-call(bf16[320,1024]{1,0:T(8,128)(2,1)} %multiply_convert_fusion.1.x_ref), custom_call_target="tpu_custom_call" | custom-call | tf_op jit(solution)/shard_map/ring_gather/pallas_call | solution.py:359
  116.1 15.2 %all-gather.2 = s32[8,320,8]{1,2,0:T(8,128)S(1)} all-gather(s32[1,320,8]{1,2,0:T(8,128)S(1)} %bitcast.181), channel_id=2, replica_groups=mesh['dp'=4,'expert'=8] {'expert'}, dimensions={0}, use_global_device_ids=true | all-gather | bytes 92160 | tf_op jit(solution)/shard_map/all_gather | solution.py:718
  132.4 4.4 fusion.131
  136.9 6.7 %fusion.24 = f32[4,8,1,120]{3,2,1,0:T(1,128)S(1)} fusion(f32[8,320,4,1]{1,2,0,3:T(4,128)S(1)} %fusion.80, s32[8,4,320]{2,1,0:T(4,128)S(1)} %copy.145, pred[8,4,320]{2,1,0:T(4,128)(4,1)S(1)} %bitcast.183), kind=kOutput, calls=%fused_computation.46 | convolution fusion | flops 17203200 | bytes 107520 | tf_op jit(solution)/shard_map/jest,jte->ejs/dot_general | solution.py:740
  143.7 9.1 %convert_bitcast_fusion.1 = bf16[4,8,120,1024]{3,2,0,1:T(8,128)(2,1)} fusion(bf16[8,320,1024]{2,1,0:T(8,128)(2,1)S(1)} %bitcast.159, s32[8,4,320]{2,1,0:T(4,128)S(1)} %copy.145, pred[8,4,320]{2,1,0:T(4,128)(4,1)S(1)} %bitcast.184), kind=kOutput, calls=%fused_computation.31 | convolution fusion | flops 2522972160 | bytes 13158400 | tf_op jit(solution)/shard_map/jest,jtd->ejsd/dot_general | solution.py:743
  152.9 13.9 %fusion = f32[4,8,120,1024]{3,2,1,0:T(8,128)} fusion(bf16[4,1024,1024]{2,1,0:T(8,128)(2,1)S(1)} %bitcast.190, bf16[4,8,120,1024]{3,2,0,1:T(8,128)(2,1)} %convert_bitcast_fusion.1), kind=kOutput, calls=%fused_computation.7 | convolution fusion | flops 8053063680 | bytes 31981568 | tf_op jit(solution)/shard_map/ejsd,edf->ejsf/dot_general | solution.py:747
  166.7 10.8 %convert_bitcast_fusion = bf16[4,8,120,1024]{3,2,0,1:T(8,128)(2,1)} fusion(bf16[8,320,1024,1]{2,1,3,0:T(8,128)(2,1)} %bitcast.166, s32[8,4,320]{2,1,0:T(4,128)S(1)} %copy.145, pred[8,4,320]{2,1,0:T(4,128)(4,1)S(1)} %bitcast.185), kind=kOutput, calls=%fused_computation.26 | convolution fusion | flops 2522972160 | bytes 13158400 | tf_op jit(solution)/shard_map/jest,jtd->ejsd/dot_general | solution.py:745
  177.5 18.6 %multiply_multiply_fusion = (f32[4,8,120,512]{3,2,1,0:T(8,128)}, f32[4,8,120,512]{3,2,1,0:T(8,128)}, f32[4,8,120]{2,1,0:T(8,128)S(1)}, bf16[4,8,120,512]{3,2,1,0:T(8,128)(2,1)}) fusion(f32[4,8,120]{2,1,0:T(8,128)S(1)} %bitcast.191, f32[4,8,120,1024]{3,2,1,0:T(8,128)} %fusion, bf16[4,512,1024]{2,1,0:T(8,128)(2,1)} %param.20, ...), kind=kOutput, calls=%fused_computation.34 | convolution fusion | flops 4065849600 | bytes 47478784 | tf_op jit(solution)/shard_map/ejsd,efd->ejsf/dot_general | solution.py:757
  196.1 11.1 %bitcast_convert_fusion.3 = bf16[4,512,1024]{2,1,0:T(8,128)(2,1)} fusion(bf16[4,8,120,1024]{3,2,0,1:T(8,128)(2,1)} %convert_bitcast_fusion, bf16[4,8,120,512]{3,2,1,0:T(8,128)(2,1)} %get-tuple-element.83, f32[4,8,120]{2,1,0:T(8,128)S(1)} %bitcast.192), kind=kOutput, calls=%fused_computation.9 | convolution fusion | flops 4034527232 | bytes 16006144 | tf_op jit(solution)/shard_map/ejsf,ejsd->efd/dot_general | solution.py:764
  207.2 15.6 %bitcast_convert_fusion = bf16[4,1024,1024]{2,1,0:T(8,128)(2,1)} fusion(bf16[4,8,120,1024]{3,2,0,1:T(8,128)(2,1)} %convert_bitcast_fusion.1, f32[4,8,120,512]{3,2,1,0:T(8,128)} %get-tuple-element.81, f32[4,8,120,512]{3,2,1,0:T(8,128)} %get-tuple-element.80), kind=kOutput, calls=%fused_computation.1 | convolution fusion | flops 8065122304 | bytes 31981568 | tf_op jit(solution)/shard_map/ejsd,ejsf->edf/dot_general | solution.py:771
  222.9 1.2 copy-done.2
  225.8 7.4 %fusion.83 = f32[8,4,1,320]{3,2,1,0:T(1,128)S(1)} fusion(f32[4,8,120,1]{2,1,0,3:T(8,128)S(1)} %bitcast.194, s32[8,4,320]{2,1,0:T(4,128)S(1)} %copy-done.31, pred[8,4,320]{2,1,0:T(4,128)(4,1)S(1)} %bitcast.186), kind=kOutput, calls=%fused_computation.153 | convolution fusion | flops 17203200 | bytes 107520 | tf_op jit(solution)/shard_map/jest,ejs->jte/dot_general | solution.py:761
  233.9 5.0 all-to-all-start
  238.9 15.9 %fusion.2 = bf16[4,8,120,1024]{3,2,0,1:T(8,128)(2,1)} fusion(bf16[4,1024,1024]{2,1,0:T(8,128)(2,1)} %param.19, f32[4,8,120,512]{3,2,1,0:T(8,128)} %get-tuple-element.81, f32[4,8,120,512]{3,2,1,0:T(8,128)} %get-tuple-element.80), kind=kOutput, calls=%fused_computation.10 | convolution fusion | flops 8060928000 | bytes 31981568 | tf_op jit(solution)/shard_map/ejsf,edf->ejsd/dot_general | solution.py:768
  254.8 10.1 %bitcast_convert_fusion.1.part = bf16[8,320,1024]{2,1,0:T(8,128)(2,1)} fusion(bf16[4,8,120,1024]{3,2,0,1:T(8,128)(2,1)} %fusion.2, s32[8,4,320]{2,1,0:T(4,128)S(1)} %copy-done.31, pred[8,4,320]{2,1,0:T(4,128)(4,1)S(1)} %bitcast.187), kind=kOutput, calls=%fused_computation.3 | convolution fusion | flops 2521661440 | bytes 13158400 | tf_op jit(solution)/shard_map/jest,ejsd->jtd/dot_general | solution.py:774
  264.8 6.5 %fusion.27 = bf16[4,8,120,1024]{3,2,0,1:T(8,128)(2,1)} fusion(bf16[4,512,1024]{2,1,0:T(8,128)(2,1)S(1)} %copy-done.46, bf16[4,8,120,512]{3,2,1,0:T(8,128)(2,1)S(1)} %copy-done.50, f32[4,8,120]{2,1,0:T(8,128)S(1)} %bitcast.193), kind=kOutput, calls=%fused_computation.49 | convolution fusion | flops 4032430080 | bytes 16006144 | tf_op jit(solution)/shard_map/ejsf,efd->ejsd/dot_general | solution.py:751
  271.3 9.2 %bitcast_convert_fusion.2.part = bf16[8,320,1024]{2,1,0:T(8,128)(2,1)} fusion(bf16[4,8,120,1024]{3,2,0,1:T(8,128)(2,1)} %fusion.27, s32[8,4,320]{2,1,0:T(4,128)S(1)} %copy-done.31, pred[8,4,320]{2,1,0:T(4,128)(4,1)S(1)} %bitcast.188), kind=kOutput, calls=%fused_computation.4 | convolution fusion | flops 2521661440 | bytes 13158400 | tf_op jit(solution)/shard_map/jest,ejsd->jtd/dot_general | solution.py:754
  280.5 52.1 %ring_scatter.3 = f32[320,1024]{1,0:T(8,128)S(1)} custom-call(bf16[8,320,1024]{2,1,0:T(8,128)(2,1)} %bitcast_convert_fusion.1.part), custom_call_target="tpu_custom_call" | custom-call | tf_op jit(solution)/shard_map/ring_scatter/pallas_call | solution.py:386
  332.6 51.8 %ring_scatter.2 = bf16[320,1024]{1,0:T(8,128)(2,1)S(1)} custom-call(bf16[8,320,1024]{2,1,0:T(8,128)(2,1)} %bitcast_convert_fusion.2.part, f32[320,1024]{1,0:T(8,128)S(1)} %get-tuple-element.104.refs_0_), custom_call_target="tpu_custom_call" | custom-call | tf_op jit(solution)/shard_map/ring_scatter/pallas_call | solution.py:386
  384.4 1.4 squeeze.15
  385.8 0.9 multiply_reduce_fusion.3
  386.7 0.8 multiply_convert_fusion.2
  389.2 1.7 convolution_convert_fusion.3
  390.9 1.4 copy.159
  392.4 8.0 %fusion.6 = (f32[8,2,320]{2,1,0:T(2,128)S(1)}, f32[8,320,320,2]{2,1,3,0:T(8,128)}) fusion(f32[8,2,320,320]{2,3,1,0:T(8,128)} %copy-done.1, f32[8,2,320]{2,1,0:T(2,128)S(1)} %bitcast.173, bf16[320,8,64,1]{0,2,3,1:T(8,128)(2,1)S(1)} %bitcast.170, bf16[320,8,2,64]{0,3,2,1:T(8,128)(2,1)S(1)} %bitcast.160), kind=kOutput, calls=%fused_computation.16 | convolution fusion | flops 214625280 | bytes 14131200 | tf_op jit(solution)/shard_map/tkgd,skd->kgts/dot_general | solution.py:807
  400.5 7.3 %fusion.8 = bf16[8,2,320,320]{2,3,1,0:T(8,128)(2,1)S(1)} fusion(f32[8,320,320,2]{2,1,3,0:T(8,128)} %get-tuple-element.109, f32[8,2,320,320]{2,3,1,0:T(8,128)} %copy-done.1, f32[8,2,320]{2,1,0:T(2,128)S(1)} %get-tuple-element.108, f32[8,2,320]{2,1,0:T(2,128)S(1)} %bitcast.174), kind=kLoop, calls=%fused_computation.18 | loop fusion | flops 6553600 | bytes 16424960 | tf_op jit(solution)/shard_map/convert_element_type | solution.py:812
  407.8 1.2 broadcast_multiply_fusion
  409.2 0.9 bitcast_multiply_fusion.1
  410.7 0.9 copy-done.22
  411.5 1.0 copy-done.49
  412.5 1.2 fusion.132
  413.8 1.2 fusion.56
  415.6 2.8 fusion.48
  418.7 0.9 convolution_convert_fusion.4
  419.5 1.0 copy.166
  420.8 4.2 convolution_convert_fusion.1
  425.0 2.8 convolution_convert_fusion.2
  427.8 2.6 convolution_convert_fusion
  430.4 0.7 broadcast_in_dim.57
  431.1 11.1 %concatenate.36.g_ref = bf16[1024,3200]{1,0:T(8,128)(2,1)} concatenate(bf16[1024,1024]{1,0:T(8,128)(2,1)} %convolution_convert_fusion.2, bf16[1024,1024]{1,0:T(8,128)(2,1)} %convolution_convert_fusion.1, bf16[1024,1024]{1,0:T(8,128)(2,1)} %convolution_convert_fusion, bf16[1024,32]{1,0:T(8,128)(2,1)S(1)} %copy.166, bf16[1024,1]{1,0:T(8,128)(2,1)S(1)} %convert_element_type.235, ...), dimensions={1} | concatenate | bytes 13107200 | tf_op jit(solution)/shard_map/concatenate | solution.py:842
  442.2 76.0 %reduce_grads.1 = f32[256,3200]{1,0:T(8,128)} custom-call(bf16[1024,3200]{1,0:T(8,128)(2,1)} %concatenate.36.g_ref), custom_call_target="tpu_custom_call" | custom-call | tf_op jit(solution)/shard_map/reduce_grads/pallas_call | solution.py:548
  518.2 0.9 slice.84
  519.1 0.7 copy.171
  519.8 1.9 slice_reduce_fusion
  521.7 3.6 fusion.129
  525.3 1.4 fusion.50
  526.7 2.8 convert_element_type.232
  529.5 4.1 convert_element_type.230
  533.6 0.8 copy.225
  (173 shorter events, 12.5 us)
Async XLA Ops:
  7.2 44.1 %copy-start.6 = (bf16[320,1024]{1,0:T(8,128)(2,1)S(1)}, bf16[320,1024]{1,0:T(8,128)(2,1)}, u32[]{:S(2)}) copy-start(bf16[320,1024]{1,0:T(8,128)(2,1)} %param.12) | copy-start | bytes 1966084
  7.2 42.5 %copy-start = (s32[1,13]{1,0:T(1,128)S(1)}, s32[1,13]{1,0:T(1,128)}, u32[]{:S(2)}) copy-start(s32[1,13]{1,0:T(1,128)} %param.23) | copy-start | bytes 160
  7.2 159.5 %all-gather.5.cloned.1.call-start = ((), (), s32[]{:S(2)}) async-start(), calls=%async_computation.5 | async-start | bytes 5898240 | tf_op jit(solution)/shard_map/all_gather | solution.py:719
  7.9 518.8 %reduce-scatter.5.cloned.1.call-start = ((), (), s32[]{:S(2)}) async-start(), calls=%async_computation.4 | async-start | bytes 5242880 | tf_op jit(solution)/shard_map/reduce_scatter | solution.py:790
  48.4 7.5 %copy-start.41 = (f32[1024]{0:T(1024)}, f32[1024]{0:T(1024)S(1)}, u32[]{:S(2)}) copy-start(f32[1024]{0:T(1024)S(1)} %get-tuple-element.75) | copy-start | bytes 12292
  49.7 4.1 copy-start.37
  49.7 6.1 %copy-start.43 = (f32[320]{0:T(512)}, f32[320]{0:T(512)S(1)}, u32[]{:S(2)}) copy-start(f32[320]{0:T(512)S(1)} %fusion.110) | copy-start | bytes 3844
  54.6 6.4 %copy-start.17 = (bf16[320,512]{0,1:T(8,128)(2,1)}, bf16[320,512]{0,1:T(8,128)(2,1)S(1)}, u32[]{:S(2)}) copy-start(bf16[320,512]{0,1:T(8,128)(2,1)S(1)} %copy.149) | copy-start | bytes 983044
  54.7 1.8 copy-start.48
  55.8 2.4 copy-start.10
  58.3 1.5 copy-start.4
  59.8 3.1 copy-start.1
  61.0 3.5 copy-start.33
  62.9 1.6 copy-start.15
  64.5 1.0 copy-start.12
  65.5 50.5 %copy-start.39 = (f32[320]{0:T(512)}, f32[320]{0:T(512)S(1)}, u32[]{:S(2)}) copy-start(f32[320]{0:T(512)S(1)} %get-tuple-element.103) | copy-start | bytes 3844
  65.5 50.5 %copy-start.35 = (f32[320]{0:T(512)}, f32[320]{0:T(512)S(1)}, u32[]{:S(2)}) copy-start(f32[320]{0:T(512)S(1)} %fusion.111) | copy-start | bytes 3844
  65.5 50.5 %copy-start.32 = (s32[320,8]{0,1:T(8,128)S(1)}, s32[320,8]{0,1:T(8,128)}, u32[]{:S(2)}) copy-start(s32[320,8]{0,1:T(8,128)} %param.22) | copy-start | bytes 30724
  65.6 66.8 %copy-start.9 = (bf16[1024,128]{1,0:T(8,128)(2,1)S(1)}, bf16[1024,128]{1,0:T(8,128)(2,1)}, u32[]{:S(2)}) copy-start(bf16[1024,128]{1,0:T(8,128)(2,1)} %get-tuple-element.14) | copy-start | bytes 786436
  116.1 27.6 %slice-start.2 = ((s8[5242880]{0:T(1024)(128)(4,1)}), s8[1048576]{0:T(1024)(128)(4,1)S(1)}, s32[]{:S(2)}) async-start(s8[5242880]{0:T(1024)(128)(4,1)} %bitcast.158), calls=%async_computation.8 | async-start | bytes 2097152
  131.8 34.9 %copy-start.30 = (s32[8,4,320]{2,1,0:T(4,128)}, s32[8,4,320]{2,1,0:T(4,128)S(1)}, u32[]{:S(2)}) copy-start(s32[8,4,320]{2,1,0:T(4,128)S(1)} %copy.145) | copy-start | bytes 122884
  132.4 11.3 %slice-start.3 = ((s8[5242880]{0:T(1024)(128)(4,1)}), s8[4194304]{0:T(1024)(128)(4,1)S(1)}, s32[]{:S(2)}) async-start(s8[5242880]{0:T(1024)(128)(4,1)} %bitcast.158), calls=%async_computation.9 | async-start | bytes 8388608
  136.9 15.9 %slice-start.4 = ((s8[8388608]{0:T(1024)(128)(4,1)}), s8[4194304]{0:T(1024)(128)(4,1)S(1)}, s32[]{:S(2)}) async-start(s8[8388608]{0:T(1024)(128)(4,1)} %bitcast.189), calls=%async_computation.10 | async-start | bytes 8388608
  143.7 9.2 %slice-start.5 = ((s8[8388608]{0:T(1024)(128)(4,1)}), s8[4194304]{0:T(1024)(128)(4,1)S(1)}, s32[]{:S(2)}) async-start(s8[8388608]{0:T(1024)(128)(4,1)} %bitcast.189), calls=%async_computation.11 | async-start | bytes 8388608
  207.2 322.3 %reduce-scatter.3.cloned.1.call-start = ((), (), s32[]{:S(2)}) async-start(), calls=%async_computation.3 | async-start | bytes 10485760 | tf_op jit(solution)/shard_map/reduce_scatter | solution.py:787
  222.8 1.2 copy-start.2
  222.8 2.4 copy-start.34
  222.8 3.0 copy-start.31
  224.5 30.2 %copy-start.24 = (f32[320,32]{0,1:T(8,128)}, f32[320,32]{0,1:T(8,128)S(1)}, u32[]{:S(2)}) copy-start(f32[320,32]{0,1:T(8,128)S(1)} %select_reduce_fusion) | copy-start | bytes 122884
  233.9 150.5 %all-to-all-start = ((f32[8,320,4]{1,2,0:T(4,128)}), f32[8,320,4]{1,2,0:T(4,128)}, u32[]{:S(2)}, u32[]{:S(2)}) async-start(f32[8,320,4]{1,2,0:T(4,128)} %bitcast.150), calls=%async_computation | async-start | bytes 98304 | tf_op jit(solution)/shard_map/all_to_all | solution.py:775
  254.8 10.1 %copy-start.46 = (bf16[4,512,1024]{2,1,0:T(8,128)(2,1)S(1)}, bf16[4,512,1024]{2,1,0:T(8,128)(2,1)}, u32[]{:S(2)}) copy-start(bf16[4,512,1024]{2,1,0:T(8,128)(2,1)} %param.20) | copy-start | bytes 12582916
  254.8 10.1 %copy-start.50 = (bf16[4,8,120,512]{3,2,1,0:T(8,128)(2,1)S(1)}, bf16[4,8,120,512]{3,2,1,0:T(8,128)(2,1)}, u32[]{:S(2)}) copy-start(bf16[4,8,120,512]{3,2,1,0:T(8,128)(2,1)} %get-tuple-element.83) | copy-start | bytes 11796484
  332.5 55.0 %copy-start.36 = (f32[320]{0:T(512)S(1)}, f32[320]{0:T(512)}, u32[]{:S(2)}) copy-start(f32[320]{0:T(512)} %copy-done.35) | copy-start | bytes 3844
  384.3 3.9 copy-start.40
  385.8 2.4 copy-start.14
  387.6 0.7 copy-start.28
  387.6 1.6 copy-start.16
  389.2 3.2 copy-start.18
  389.2 3.2 copy-start.25
  400.4 7.3 %copy-start.5 = (bf16[320,8,2,64]{0,3,2,1:T(8,128)(2,1)S(1)}, bf16[320,8,2,64]{0,3,2,1:T(8,128)(2,1)}, u32[]{:S(2)}) copy-start(bf16[320,8,2,64]{0,3,2,1:T(8,128)(2,1)} %copy-done.4) | copy-start | bytes 1966084
  400.4 7.3 %copy-start.21 = (f32[320,64]{0,1:T(8,128)S(1)}, f32[320,64]{0,1:T(8,128)}, u32[]{:S(2)}) copy-start(f32[320,64]{0,1:T(8,128)} %get-tuple-element.97) | copy-start | bytes 245764
  407.8 1.3 copy-start.20
  407.8 1.4 copy-start.11
  409.2 5.9 %copy-start.27 = (bf16[320,8,64]{0,2,1:T(8,128)(2,1)}, bf16[320,8,64]{0,2,1:T(8,128)(2,1)S(1)}, u32[]{:S(2)}) copy-start(bf16[320,8,64]{0,2,1:T(8,128)(2,1)S(1)} %fusion.62) | copy-start | bytes 983044
  409.2 4.5 slice-start
  410.2 2.3 copy-start.49
  410.3 3.5 slice-start.1
  410.7 0.9 copy-start.22
  413.8 1.3 copy-start.7
  413.8 1.3 copy-start.42
  413.8 1.3 copy-start.44
  413.8 1.8 copy-start.47
  415.1 3.6 copy-start.26
  415.1 3.6 copy-start.3
  415.1 3.6 copy-start.29
  415.6 5.1 copy-start.8
  420.5 4.5 copy-start.23
  420.8 7.0 %copy-start.13 = (bf16[8,64,2,320]{3,1,2,0:T(8,128)(2,1)S(1)}, bf16[8,64,2,320]{3,1,2,0:T(8,128)(2,1)}, u32[]{:S(2)}) copy-start(bf16[8,64,2,320]{3,1,2,0:T(8,128)(2,1)} %copy-done.12) | copy-start | bytes 1966084
  442.2 79.5 %copy-start.38 = (f32[320]{0:T(512)S(1)}, f32[320]{0:T(512)}, u32[]{:S(2)}) copy-start(f32[320]{0:T(512)} %copy-done.37) | copy-start | bytes 3844
  442.2 79.5 %copy-start.45 = (f32[320]{0:T(512)S(1)}, f32[320]{0:T(512)}, u32[]{:S(2)}) copy-start(f32[320]{0:T(512)} %get-tuple-element.73) | copy-start | bytes 3844
  519.8 5.5 %copy-start.19 = (f32[320,1024]{1,0:T(8,128)S(1)}, f32[320,1024]{1,0:T(8,128)}, u32[]{:S(2)}) copy-start(f32[320,1024]{1,0:T(8,128)} %get-tuple-element.114) | copy-start | bytes 3932164
Sparse Core Ops, SparseCore 0:
  9.7 58.7 all-gather.4
  207.3 52.7 reduce-scatter.4
  263.5 86.3 reduce-scatter.2

commit v3 on v2

--- a/solution.py
+++ b/solution.py
@@ -175,7 +175,6 @@
         self.ring, self.own, self.out = ring, own, out
         self.send, self.recv, self.pair_send, self.pair_recv = sems
         self.half = own.shape[0] // 2
-        self.copies, self.pairs = [], []
 
     @staticmethod
     def scratch(n_exp):
@@ -193,35 +192,28 @@
     def block(self, d, h):
         return self.out.at[self.ring.dev(d), self.rows(h)]
 
-    def push(self, side, s, h):
+    def hop(self, side, s, h):
         d = -s if side == 0 else s
         src = self.own.at[self.rows(h)] if s == 0 else self.block(d, h)
         to = self.ring.right if side == 0 else self.ring.left
-        copy = remote(src, self.block(d, h), self.send.at[side, s, h], self.recv.at[side, s + 1, h], expert=to)
-        copy.start()
-        self.copies.append(copy)
+        return remote(src, self.block(d, h), self.send.at[side, s, h], self.recv.at[side, s + 1, h], expert=to)
 
     def across(self, d, h):
         src = self.own.at[self.rows(h)] if d == 0 else self.block(d, h)
         slot = d % self.ring.depth
-        copy = remote(src, self.block(d, h), self.pair_send.at[slot, h], self.pair_recv.at[slot, h], expert=self.ring.pair)
-        copy.start()
-        self.pairs.append((copy, d, h))
+        return remote(src, self.block(d, h), self.pair_send.at[slot, h], self.pair_recv.at[slot, h], expert=self.ring.pair)
+
+    ORDER = ((0, 0), (1, 1), (0, 1), (1, 0))
 
     def start(self):
-        for side, h in ((0, 0), (1, 1), (0, 1), (1, 0)):
+        for side, h in self.ORDER:
             if self.goes(side, 1, h):
-                self.push(side, 0, h)
-        self.across(0, 0)
-        self.across(0, 1)
+                self.hop(side, 0, h).start()
+        self.across(0, 0).start()
+        self.across(0, 1).start()
 
     def events(self):
-        return [
-            (side, s, h)
-            for s in range(1, self.ring.far + 1)
-            for side, h in ((0, 0), (1, 1), (0, 1), (1, 0))
-            if self.goes(side, s, h)
-        ]
+        return [(side, s, h) for s in range(1, self.ring.far + 1) for side, h in self.ORDER if self.goes(side, s, h)]
 
     def handle(self, event):
         side, s, h = event
@@ -229,23 +221,26 @@
         here = self.block(d, h)
         remote(here, here, self.send.at[side, s, h], self.recv.at[side, s, h], expert=self.ring.mine).wait_recv()
         if self.goes(side, s + 1, h):
-            self.push(side, s, h)
-        self.across(d, h)
+            self.hop(side, s, h).start()
+        self.across(d, h).start()
 
     def wait_pair(self, d, h):
         slot = d % self.ring.depth
         here = self.out.at[self.ring.pair - self.ring.mine + self.ring.dev(d), self.rows(h)]
         remote(here, here, self.pair_send.at[slot, h], self.pair_recv.at[slot, h], expert=self.ring.mine).wait_recv()
 
-    def finish_pairs(self):
-        for _, d, h in self.pairs:
-            self.wait_pair(d, h)
-
-    def finish_sends(self):
-        for copy in self.copies:
-            copy.wait_send()
-        for copy, _, _ in self.pairs:
-            copy.wait_send()
+    def finish_own(self):
+        for side, h in self.ORDER:
+            if self.goes(side, 1, h):
+                self.hop(side, 0, h).wait_send()
+        self.across(0, 0).wait_send()
+        self.across(0, 1).wait_send()
+
+    def finish_event(self, event):
+        side, s, h = event
+        if self.goes(side, s + 1, h):
+            self.hop(side, s, h).wait_send()
+        self.across(-s if side == 0 else s, h).wait_send()
 
 
 class RingScatter:
@@ -253,8 +248,7 @@
         self.ring, self.part = ring, part
         self.pair_buf, self.held, self.got = bufs
         self.pair_send, self.pair_recv, self.send, self.recv = sems
-        self.half = self.held.shape[1] // 2
-        self.copies = []
+        self.half = self.held(0).shape[0] // 2
 
     @staticmethod
     def scratch(n_exp, block, dtype):
@@ -280,7 +274,7 @@
 
     def across(self, d):
         ring = self.ring
-        return remote(self.part(ring.dev(d) + 1 - 2 * ring.core), self.pair_buf.at[d],
+        return remote(self.part(ring.dev(d) + 1 - 2 * ring.core), self.pair_buf(d),
                       self.pair_send.at[d], self.pair_recv.at[d], expert=ring.pair)
 
     def start_pair(self, d):
@@ -290,22 +284,25 @@
         self.across(d).wait_recv()
 
     def wait_got(self, side, d, h):
-        here = self.got.at[side, d, self.rows(h)]
+        here = self.got(side, d).at[self.rows(h)]
         remote(here, here, self.send.at[side, d, h], self.recv.at[side, d, h], expert=self.ring.mine).wait_recv()
+
+    def hop(self, side, d, h):
+        slot = d if side == 0 else self.ring.depth - d
+        rows = self.rows(h)
+        return remote(self.held(slot).at[rows], self.got(side, d - 1).at[rows], self.send.at[side, d, h],
+                      self.recv.at[side, d - 1, h], expert=self.ring.right if side == 0 else self.ring.left)
 
     def push(self, side, d, h):
         ring = self.ring
         slot = d if side == 0 else ring.depth - d
         rows = self.rows(h)
-        terms = [self.part(ring.dev(slot)).at[rows], self.pair_buf.at[slot, rows]]
+        terms = [self.part(ring.dev(slot)).at[rows], self.pair_buf(slot).at[rows]]
         if self.comes(side, d, h):
             self.wait_got(side, d, h)
-            terms.append(self.got.at[side, d, rows])
-        add_rows(self.held.at[slot, rows], *terms)
-        copy = remote(self.held.at[slot, rows], self.got.at[side, d - 1, rows], self.send.at[side, d, h],
-                      self.recv.at[side, d - 1, h], expert=ring.right if side == 0 else ring.left)
-        copy.start()
-        self.copies.append(copy)
+            terms.append(self.got(side, d).at[rows])
+        add_rows(self.held(slot).at[rows], *terms)
+        self.hop(side, d, h).start()
 
     def first(self):
         far = self.ring.far
@@ -313,13 +310,15 @@
         self.push(0, far, 0)
         self.push(1, far, 1)
 
-    def rest(self):
-        ring, far = self.ring, self.ring.far
-        for d in range(far - 1, 0, -1):
+    def early(self):
+        for d in range(self.ring.far - 1, 0, -1):
             self.wait_pair(d)
             self.push(0, d, 1)
-            self.wait_pair(ring.depth - d)
+            self.wait_pair(self.ring.depth - d)
             self.push(1, d, 0)
+
+    def late(self):
+        for d in range(self.ring.far - 1, 0, -1):
             self.push(0, d, 0)
             self.push(1, d, 1)
 
@@ -327,72 +326,27 @@
         self.wait_pair(0)
         for h in range(2):
             rows = self.rows(h)
-            terms = [self.part(self.ring.mine).at[rows], self.pair_buf.at[0, rows]] + [m.at[rows] for m in more]
+            terms = [self.part(self.ring.mine).at[rows], self.pair_buf(0).at[rows]] + [m.at[rows] for m in more]
             for side in range(2):
                 if self.comes(side, 0, h):
                     self.wait_got(side, 0, h)
-                    terms.append(self.got.at[side, 0, rows])
+                    terms.append(self.got(side, 0).at[rows])
             add_rows(out.at[rows], *terms)
 
     def finish_sends(self):
-        for copy in self.copies:
-            copy.wait_send()
+        far = self.ring.far
+        for side in range(2):
+            for d in range(1, far + 1):
+                for h in range(2):
+                    if d < far or h == side:
+                        self.hop(side, d, h).wait_send()
         for d in range(self.ring.depth):
             self.across(d).wait_send()
 
 
-def ring_gather_body(n_exp, x_ref, out_ref, own_sem, *sems):
-    ring = Ring(n_exp)
-    greet(ring.partners())
-    own = pltpu.make_async_copy(x_ref, out_ref.at[ring.mine], own_sem)
-    own.start()
-    gather = RingGather(ring, x_ref, out_ref, sems)
-    gather.start()
-    for event in gather.events():
-        gather.handle(event)
-    own.wait()
-    gather.finish_pairs()
-    gather.finish_sends()
-
-
-def ring_gather(n_exp, x, collective_id):
-    return pl.pallas_call(
-        functools.partial(ring_gather_body, n_exp),
-        out_shape=jax.ShapeDtypeStruct((n_exp,) + x.shape, x.dtype),
-        in_specs=[pl.BlockSpec(memory_space=VMEM)],
-        out_specs=pl.BlockSpec(memory_space=ANY),
-        scratch_shapes=[pltpu.SemaphoreType.DMA] + RingGather.scratch(n_exp),
-        compiler_params=pltpu.CompilerParams(collective_id=collective_id, has_side_effects=True),
-        name="ring_gather",
-    )(x)
-
-
-def ring_scatter_body(n_exp, more, part, *refs):
-    extra, (out, *rest) = refs[:more], refs[more:]
-    ring = Ring(n_exp)
-    greet(ring.partners())
-    scatter = RingScatter(ring, lambda e: part.at[e], rest[:3], rest[3:])
-    for d in scatter.order():
-        scatter.start_pair(d)
-    scatter.first()
-    scatter.rest()
-    scatter.last(out, *extra)
-    scatter.finish_sends()
-
-
-def ring_scatter(n_exp, part, more, out_type, collective_id):
-    block = part.shape[1:]
-    bufs, sems = RingScatter.scratch(n_exp, block, part.dtype)
-    return pl.pallas_call(
-        functools.partial(ring_scatter_body, n_exp, len(more)),
-        out_shape=jax.ShapeDtypeStruct(block, out_type),
-        in_specs=[pl.BlockSpec(memory_space=VMEM)] * (1 + len(more)),
-        out_specs=pl.BlockSpec(memory_space=VMEM),
-        scratch_shapes=bufs + sems,
-        compiler_params=pltpu.CompilerParams(
-            collective_id=collective_id, has_side_effects=True, vmem_limit_bytes=48 * MIB),
-        name="ring_scatter",
-    )(part, *more)
+def views(bufs):
+    pair_buf, held, got = bufs
+    return (lambda d: pair_buf.at[d], lambda d: held.at[d], lambda side, d: got.at[side, d])
 
 
 def grads_body(n_dp, n_exp, chunks, g_ref, out_ref, pair_buf, total, dp_buf, prefix, suffix, go_r, go_l, final, other,
@@ -564,6 +518,370 @@
     )(grads)
 
 
+SLOTS = 128
+F32, LOW = jnp.float32, jnp.bfloat16
+
+
+def dot(a, b, over_a=1, over_b=0):
+    return lax.dot_general(a, b, (((over_a,), (over_b,)), ((), ())), preferred_element_type=F32)
+
+
+def experts_body(n_dp, n_exp, hid_ref, gy_hbm, routes_t, routes_c, wr_t, w_in_hbm, w_out_hbm, middle,
+                 block_out, hid_sum, gates_out, grads_hbm,
+                 x_all, w_in, w_out, sent, grows, gu, tmp, acts, stage, slots, gates, dots,
+                 pair_buf, held, got, *sems):
+    w_sem, gy_sem, stage_sem, own_sem, ready, gate_send, gate_recv = sems[:7]
+    gather_sems, out_sems, hid_sems = sems[7:11], sems[11:15], sems[15:19]
+    local, _, width = sent.shape
+    tree, hidden_units = hid_ref.shape[0], w_out.shape[1]
+    rows_e = local * SLOTS
+    ring = Ring(n_exp)
+    mine, core, depth = ring.mine, ring.core, ring.depth
+    first = mine * local
+    peers = [lax.rem(mine + k, n_exp) for k in range(1, n_exp)]
+    greet([(None, {"expert": e}) for e in peers])
+
+    weights = [pltpu.make_async_copy(w_in_hbm, w_in, w_sem.at[0]), pltpu.make_async_copy(w_out_hbm, w_out, w_sem.at[1])]
+    gather = RingGather(ring, hid_ref, x_all, gather_sems)
+    gather.start()
+    for copy in weights:
+        copy.start()
+    own = pltpu.make_async_copy(hid_ref, x_all.at[mine], own_sem)
+    own.start()
+
+    def gy_buf(j):
+        return stage.at[pl.ds(pl.multiple_of(lax.rem(j, 2) * tree, 16), tree)]
+
+    def gy_copy(j):
+        return pltpu.make_async_copy(gy_hbm.at[j], gy_buf(j), gy_sem.at[lax.rem(j, 2)])
+
+    gy_copy(0).start()
+
+    below = (lax.broadcasted_iota(jnp.int32, (tree, tree), 0) < lax.broadcasted_iota(jnp.int32, (tree, tree), 1)).astype(LOW)
+    sub16 = lax.broadcasted_iota(jnp.int32, (16, tree), 0)
+
+    def find_slots(j, carry):
+        names = routes_t[j]
+        chosen = jnp.zeros((16, tree), F32)
+        for k in range(names.shape[0]):
+            chosen = jnp.maximum(chosen, jnp.where(names[k : k + 1, :] == first + sub16, 1.0, 0.0))
+        chosen = jnp.where(sub16 < local, chosen, 0.0)
+        rank = dot(chosen.astype(LOW), below)
+        slots[j] = jnp.where(chosen > 0.5, rank, -1.0)[:8]
+        return carry
+
+    lax.fori_loop(0, n_exp, find_slots, 0)
+
+    slot_ids = lax.broadcasted_iota(jnp.int32, (SLOTS, tree), 0).astype(F32)
+
+    def places(j):
+        return jnp.concatenate(
+            [jnp.where(slot_ids == slots[j, i : i + 1, :], 1.0, 0.0).astype(LOW) for i in range(local)], axis=0)
+
+    def places_t(j):
+        names = routes_c[j]
+        lane = lax.broadcasted_iota(jnp.int32, (tree, 128), 1)
+        chosen = jnp.zeros((tree, 128), F32)
+        for k in range(names.shape[1]):
+            chosen = jnp.maximum(chosen, jnp.where(names[:, k : k + 1] == first + lane, 1.0, 0.0))
+        chosen = jnp.where(lane < local, chosen, 0.0)
+        above = (lax.broadcasted_iota(jnp.int32, (tree, tree), 1) < lax.broadcasted_iota(jnp.int32, (tree, tree), 0)).astype(LOW)
+        slot = jnp.where(chosen > 0.5, dot(above, chosen.astype(LOW)), -1.0)
+        lanes = lane.astype(F32)
+        return jnp.concatenate(
+            [jnp.where(lanes == slot[:, i : i + 1], 1.0, 0.0).astype(LOW) for i in range(local)], axis=1)
+
+    def find_gates(j):
+        names = routes_t[j]
+        experts = lax.broadcasted_iota(jnp.int32, (EXPERTS, tree), 0)
+        chosen = jnp.zeros((EXPERTS, tree), F32)
+        for k in range(names.shape[0]):
+            chosen = jnp.maximum(chosen, jnp.where(names[k : k + 1, :] == experts, 1.0, 0.0))
+        logits = jnp.where(chosen > 0.5, dot(wr_t[...], x_all[j], 1, 1), -1e30)
+        powers = jnp.exp(logits - jnp.max(logits, axis=0, keepdims=True))
+        share = powers / jnp.sum(powers, axis=0, keepdims=True)
+        sub = lax.broadcasted_iota(jnp.int32, (8, tree), 0)
+        own_gates = jnp.zeros((8, tree), F32)
+        for i in range(local):
+            row = jnp.sum(jnp.where(experts == first + i, share, 0.0), axis=0, keepdims=True)
+            own_gates = jnp.where(sub == i, row, own_gates)
+        gates[j] = own_gates
+
+    halves = width // 512
+
+    def dispatch(j, src, dest):
+        place = places(j)
+
+        def body(n, carry):
+            cols = pl.ds(pl.multiple_of(n * 512, 512), 512)
+            picked = dot(place, src[:, cols]).astype(LOW)
+            for i in range(local):
+                dest[i, pl.ds(pl.multiple_of(j * SLOTS, SLOTS), SLOTS), cols] = picked[i * SLOTS : (i + 1) * SLOTS]
+            return carry
+
+        lax.fori_loop(0, halves, body, 0)
+
+    def slot_gate(j, e):
+        return jnp.sum(jnp.where(slot_ids == slots[j, pl.ds(e, 1), :], gates[j, pl.ds(e, 1), :], 0.0), axis=1, keepdims=True)
+
+    def forward(chip):
+        pair_rows = pl.ds(pl.multiple_of(chip * 2 * SLOTS, 2 * SLOTS), 2 * SLOTS)
+
+        def one_tree(q, carry):
+            j = 2 * chip + q
+            find_gates(j)
+            dispatch(j, x_all.at[j], sent)
+            return carry
+
+        lax.fori_loop(0, 2, one_tree, 0)
+
+        def one_expert(e, carry):
+            both = dot(sent[e, pair_rows, :], w_in[e])
+            gu[e, pair_rows, :] = both.astype(LOW)
+            a, b = both[:, :hidden_units], both[:, hidden_units:]
+            act = (a / (1.0 + jnp.exp(-a)) * b).astype(LOW).astype(F32)
+            gate = jnp.concatenate([slot_gate(2 * chip, e), slot_gate(2 * chip + 1, e)], axis=0)
+            made = dot((act * gate).astype(LOW), w_out[e]).astype(LOW)
+            for q in range(2):
+                tmp[pl.ds(pl.multiple_of(q * rows_e + e * SLOTS, SLOTS), SLOTS), :] = made[q * SLOTS : (q + 1) * SLOTS]
+            return carry
+
+        lax.fori_loop(0, local, one_expert, 0)
+
+    def combine_out(chip):
+        def one_tree(q, carry):
+            j = 2 * chip + q
+            rows = pl.ds(pl.multiple_of(q * rows_e, rows_e), rows_e)
+            x_all[j] = dot(places_t(j), tmp[rows, :]).astype(LOW)
+            return carry
+
+        lax.fori_loop(0, 2, one_tree, 0)
+
+    def grad_rows(j, carry):
+        pl.when(j + 1 < n_exp)(lambda: gy_copy(j + 1).start())
+        gy_copy(j).wait()
+        dispatch(j, gy_buf(j), grows)
+        return carry
+
+    events = gather.events()
+    out = RingScatter(ring, lambda e: x_all.at[e], views((pair_buf, held, got)), out_sems)
+
+    def chip_at(d):
+        return lax.rem(ring.z + d, depth)
+
+    def group(g, carry):
+        d = jnp.where(g == 0, 0, jnp.where(g == 1, depth - 1, jnp.where(g == 2, 1, 2)))
+        chip = chip_at(d)
+
+        @pl.when(g == 0)
+        def _():
+            own.wait()
+            gather.wait_pair(0, 0)
+            gather.wait_pair(0, 1)
+            for copy in weights:
+                copy.wait()
+
+        @pl.when(g == 1)
+        def _():
+            for event in events[:4]:
+                gather.handle(event)
+            gather.wait_pair(-1, 0)
+            gather.wait_pair(-1, 1)
+
+        @pl.when(g == 2)
+        def _():
+            gather.wait_pair(1, 0)
+            gather.wait_pair(1, 1)
+
+        @pl.when(g == 3)
+        def _():
+            for event in events[4:]:
+                gather.handle(event)
+            gather.wait_pair(2, 0)
+            gather.wait_pair(2, 1)
+
+        forward(chip)
+
+        @pl.when(g == 0)
+        def _():
+            gather.finish_own()
+            lax.fori_loop(0, n_exp, grad_rows, 0)
+
+        for at, d in ((1, -1), (2, 1), (3, 2)):
+            @pl.when(g == at)
+            def _():
+                for event in events:
+                    if event[1] == abs(d) and (abs(d) == 2 or (event[0] == 0) == (d < 0)):
+                        gather.finish_event(event)
+
+        combine_out(chip)
+        pl.when(g == 0)(lambda: out.start_pair(0))
+        pl.when(g == 1)(lambda: out.start_pair(depth - 1))
+        pl.when(g == 2)(lambda: out.start_pair(1))
+        pl.when(g == 3)(lambda: out.start_pair(2))
+        return carry
+
+    lax.fori_loop(0, depth, group, 0)
+    out.first()
+    out.early()
+
+    def stage_copy(e):
+        return pltpu.make_async_copy(stage, grads_hbm.at[e], stage_sem)
+
+    block = 4 * SLOTS
+    sub8 = lax.broadcasted_iota(jnp.int32, (8, tree), 0)
+
+    def backward(e, carry):
+        def one_block(m, inner):
+            rows = pl.ds(pl.multiple_of(m * block, block), block)
+            grad_act = dot(grows[e, rows, :], w_out[e], 1, 1)
+            a = gu[e, rows, pl.ds(0, hidden_units)].astype(F32)
+            b = gu[e, rows, pl.ds(hidden_units, hidden_units)].astype(F32)
+            sg = 1.0 / (1.0 + jnp.exp(-a))
+            sw = a * sg
+            act = (sw * b).astype(LOW).astype(F32)
+            gate = jnp.concatenate([slot_gate(4 * m + q, e) for q in range(4)], axis=0)
+            told = jnp.sum(act * grad_act, axis=1, keepdims=True)
+            acts[rows, :] = (act * gate).astype(LOW)
+            grad_act = grad_act * gate
+            tmp[rows, pl.ds(0, hidden_units)] = (grad_act * b * sg * (1.0 + a * (1.0 - sg))).astype(LOW)
+            tmp[rows, pl.ds(hidden_units, hidden_units)] = (grad_act * sw).astype(LOW)
+            for q in range(4):
+                j = 4 * m + q
+                row = jnp.sum(
+                    jnp.where(slot_ids == slots[j, pl.ds(e, 1), :], told[q * SLOTS : (q + 1) * SLOTS], 0.0),
+                    axis=0, keepdims=True)
+                dots[j] = jnp.where(sub8 == e, row, dots[j])
+            return inner
+
+        lax.fori_loop(0, n_exp // 4, one_block, 0)
+        pl.when(e > 0)(lambda: stage_copy(e - 1).wait())
+        in_rows, out_rows = width // n_dp, hidden_units // n_dp
+        grad_out = dot(acts[...], grows[e], 0, 0).astype(LOW)
+        for d in range(n_dp):
+            stage[pl.ds(d * (in_rows + out_rows) + in_rows, out_rows), :] = grad_out[d * out_rows : (d + 1) * out_rows]
+
+        def in_half(h, inner):
+            grad_in = dot(sent[e, :, pl.ds(pl.multiple_of(h * 512, 512), 512)], tmp[...], 0, 0).astype(LOW)
+            per = 512 // in_rows
+            for k in range(per):
+                at = pl.multiple_of((h * per + k) * (in_rows + out_rows), 16)
+                stage[pl.ds(at, in_rows), :] = grad_in[k * in_rows : (k + 1) * in_rows]
+            return inner
+
+        lax.fori_loop(0, halves, in_half, 0)
+        stage_copy(e).start()
+
+        def back_half(m, inner):
+            rows = pl.ds(pl.multiple_of(m * 512, 512), 512)
+            sent[e, rows, :] = dot(tmp[rows, :], w_in[e], 1, 1).astype(LOW)
+            return inner
+
+        lax.fori_loop(0, n_exp * SLOTS // 512, back_half, 0)
+        pl.when(e == local // 2 - 1)(out.late)
+        return carry
+
+    dots[...] = jnp.zeros(dots.shape, F32)
+    lax.fori_loop(0, local, backward, 0)
+    for partner in (ring.pair, ring.right, ring.left):
+        pl.semaphore_signal(ready, inc=1, device_id={"expert": partner}, device_id_type=MESH)
+
+    gate_copies = []
+    for k, e in enumerate(peers):
+        copy = remote(dots.at[e], gates_out.at[mine], gate_send.at[k], gate_recv.at[k], expert=e)
+        copy.start()
+        gate_copies.append(copy)
+    gates_out[mine] = dots[mine]
+    out.last(block_out, middle)
+
+    def part(j):
+        return grows.at[lax.div(j, 2), pl.ds(pl.multiple_of(lax.rem(j, 2) * tree, 16), tree)]
+
+    def spare(b):
+        return gu.at[b // 3, pl.ds((b % 3) * tree, tree)]
+
+    hid = RingScatter(ring, part, (spare, lambda d: spare(depth + d), lambda side, d: spare(2 * depth + 2 * side + d)), hid_sems)
+
+    def combine_hid(g, carry):
+        d = jnp.where(g == 0, 2, jnp.where(g == 1, 1, jnp.where(g == 2, depth - 1, 0)))
+        chip = chip_at(d)
+
+        def one_tree(q, inner):
+            j = 2 * chip + q
+            rows = pl.ds(pl.multiple_of(j * SLOTS, SLOTS), SLOTS)
+            made = jnp.concatenate([sent[i, rows, :] for i in range(local)], axis=0)
+            part(j)[...] = dot(places_t(j), made).astype(LOW)
+            return inner
+
+        lax.fori_loop(0, 2, one_tree, 0)
+
+        @pl.when(g == 0)
+        def _():
+            pl.semaphore_wait(ready, 3)
+            hid.start_pair(2)
+
+        pl.when(g == 1)(lambda: hid.start_pair(1))
+        pl.when(g == 2)(lambda: hid.start_pair(depth - 1))
+        pl.when(g == 3)(lambda: hid.start_pair(0))
+        pl.when(g == 1)(hid.first)
+        return carry
+
+    lax.fori_loop(0, depth, combine_hid, 0)
+    hid.early()
+    hid.late()
+    hid.last(hid_sum)
+
+    for k, copy in enumerate(gate_copies):
+        copy.wait_send()
+        source = lax.rem(mine + n_exp - 1 - k, n_exp)
+        remote(dots.at[mine], gates_out.at[source], gate_send.at[k], gate_recv.at[k], expert=mine).wait_recv()
+    stage_copy(local - 1).wait()
+    out.finish_sends()
+    hid.finish_sends()
+
+
+def experts(n_dp, n_exp, hidden2, grad_y, routes_all, router, expert_in, expert_out, middle, collective_id):
+    local, width, both = expert_in.shape
+    units = expert_out.shape[1]
+    tree = hidden2.shape[0]
+    rows = n_exp * SLOTS
+    sem = pltpu.SemaphoreType.DMA
+    bufs, out_sems = RingScatter.scratch(n_exp, (tree, width), LOW)
+    _, hid_sems = RingScatter.scratch(n_exp, (tree, width), LOW)
+    shape = jax.ShapeDtypeStruct
+    return pl.pallas_call(
+        functools.partial(experts_body, n_dp, n_exp),
+        out_shape=[
+            shape((tree, width), LOW),
+            shape((tree, width), F32),
+            shape((n_exp, 8, tree), F32),
+            shape((local, width + units, width), LOW),
+        ],
+        in_specs=[pl.BlockSpec(memory_space=s) for s in (VMEM, ANY, VMEM, VMEM, VMEM, ANY, ANY, VMEM)],
+        out_specs=[pl.BlockSpec(memory_space=s) for s in (VMEM, VMEM, VMEM, ANY)],
+        scratch_shapes=[
+            pltpu.VMEM((n_exp, tree, width), LOW),
+            pltpu.VMEM((local, width, both), LOW),
+            pltpu.VMEM((local, units, width), LOW),
+            pltpu.VMEM((local, rows, width), LOW),
+            pltpu.VMEM((local, rows, width), LOW),
+            pltpu.VMEM((local, rows, both), LOW),
+            pltpu.VMEM((max(rows, 2 * local * SLOTS), width), LOW),
+            pltpu.VMEM((rows, units), LOW),
+            pltpu.VMEM((width + units, width), LOW),
+            pltpu.VMEM((n_exp, 8, tree), F32),
+            pltpu.VMEM((n_exp, 8, tree), F32),
+            pltpu.VMEM((n_exp, 8, tree), F32),
+            *bufs,
+            sem((2,)), sem((2,)), sem, sem, pltpu.SemaphoreType.REGULAR, sem((n_exp - 1,)), sem((n_exp - 1,)),
+            *RingGather.scratch(n_exp), *out_sems, *hid_sems,
+        ],
+        compiler_params=pltpu.CompilerParams(
+            collective_id=collective_id, has_side_effects=True, vmem_limit_bytes=63 * MIB),
+        name="experts",
+    )(hidden2, grad_y, routes_all.transpose(0, 2, 1), routes_all, router.T, expert_in, expert_out, middle)
+
+
 def tree_layout(tree_rows):
     unit_rows = tree_rows // 20
     row_index = jnp.arange(tree_rows, dtype=jnp.int32)
@@ -637,6 +955,89 @@
     width_ff = gate_up.shape[-1] // 2
     gate_part = gate_up[..., :width_ff]
     return gate_part / (1.0 + jnp.exp(-gate_part)) * gate_up[..., width_ff:]
+
+
+def experts_plain(
+    n_dp, n_exp, hidden2, grad_y, routes_all, router_full, expert_in, expert_out, middle, collective_id
+):
+    tree_rows, width = hidden2.shape
+    capacity = CAP
+    expert_ids = jnp.arange(EXPERTS, dtype=jnp.int32)
+    here = lax.axis_index("expert")
+    local = expert_in.shape[0]
+    first = here * local
+    hidden_all = lax.all_gather(hidden2, "expert", axis=0, tiled=False)
+    own_ids = first + jnp.arange(local, dtype=jnp.int32)
+    hot_all = routes_all[:, :, :, None] == expert_ids[None, None, None, :]
+    chosen_all = jnp.any(hot_all, axis=2)
+    chosen = jnp.any(routes_all[:, :, :, None] == own_ids[None, None, None, :], axis=2)
+    lower = jnp.tril(jnp.ones((tree_rows, tree_rows), jnp.bfloat16), -1)
+    rank = jnp.einsum(
+        "tu,jue->jet", lower, chosen.astype(jnp.bfloat16), preferred_element_type=jnp.float32
+    ).astype(jnp.int32)
+    slots = jnp.arange(capacity, dtype=jnp.int32)
+    chosen_t = chosen.transpose(0, 2, 1)
+    place = (rank[:, :, None, :] == slots[None, None, :, None]) & chosen_t[:, :, None, :]
+    place = place.astype(jnp.bfloat16)
+    logits_all = jnp.einsum(
+        "jtd,de->jte", hidden_all, router_full, preferred_element_type=jnp.float32
+    )
+    masked = jnp.where(chosen_all, logits_all, -1e30)
+    weight = jnp.exp(masked - jnp.max(masked, axis=-1, keepdims=True))
+    weight = weight / jnp.sum(weight, axis=-1, keepdims=True)
+    gates_own = lax.dynamic_slice_in_dim(weight, first, local, axis=2)
+    gate_slot = jnp.einsum(
+        "jest,jte->ejs", place.astype(jnp.float32), gates_own, precision=lax.Precision.HIGHEST
+    )[..., None]
+    sent = jnp.einsum("jest,jtd->ejsd", place, hidden_all, preferred_element_type=jnp.float32)
+    sent = sent.astype(jnp.bfloat16)
+    grad_rows = jnp.einsum("jest,jtd->ejsd", place, grad_y, preferred_element_type=jnp.float32)
+    grad_rows = grad_rows.astype(jnp.bfloat16)
+    gate_up = jnp.einsum("ejsd,edf->ejsf", sent, expert_in, preferred_element_type=jnp.float32)
+    activated, glu_back = jax.vjp(gated_unit, gate_up)
+    act_low = activated.astype(jnp.bfloat16).astype(jnp.float32)
+    act_scaled = (act_low * gate_slot).astype(jnp.bfloat16)
+    made = jnp.einsum(
+        "ejsf,efd->ejsd", act_scaled, expert_out, preferred_element_type=jnp.float32
+    ).astype(jnp.bfloat16)
+    out_part = jnp.einsum("jest,ejsd->jtd", place, made, preferred_element_type=jnp.float32)
+    out_sum = lax.psum_scatter(
+        out_part.astype(jnp.bfloat16), "expert", scatter_dimension=0, tiled=False
+    ).astype(jnp.float32)
+    result = middle + out_sum
+    block_out = result.astype(jnp.bfloat16)
+    grad_act = jnp.einsum(
+        "ejsd,efd->ejsf", grad_rows, expert_out, preferred_element_type=jnp.float32
+    )
+    gate_dot = jnp.sum(act_low * grad_act, axis=-1)
+    gates_back = jnp.einsum(
+        "jest,ejs->jte", place.astype(jnp.float32), gate_dot, precision=lax.Precision.HIGHEST
+    )
+    grad_out_w = jnp.einsum(
+        "ejsf,ejsd->efd", act_scaled, grad_rows, preferred_element_type=jnp.float32
+    )
+    grad_gate_up = glu_back(grad_act * gate_slot)[0].astype(jnp.bfloat16)
+    grad_sent = jnp.einsum(
+        "ejsf,edf->ejsd", grad_gate_up, expert_in, preferred_element_type=jnp.float32
+    ).astype(jnp.bfloat16)
+    grad_in_w = jnp.einsum(
+        "ejsd,ejsf->edf", sent, grad_gate_up, preferred_element_type=jnp.float32
+    )
+    hid_part = jnp.einsum("jest,ejsd->jtd", place, grad_sent, preferred_element_type=jnp.float32)
+    gates_mine = lax.all_to_all(gates_back, "expert", split_axis=0, concat_axis=2, tiled=True)[0]
+    hid_sum = lax.psum_scatter(
+        hid_part.astype(jnp.bfloat16), "expert", scatter_dimension=0, tiled=False
+    ).astype(jnp.float32)
+    local, units = expert_in.shape[0], expert_out.shape[1]
+    low = jnp.bfloat16
+    grads = jnp.concatenate(
+        [
+            grad_in_w.astype(low).reshape(local, n_dp, width // n_dp, width),
+            grad_out_w.astype(low).reshape(local, n_dp, units // n_dp, width),
+        ],
+        axis=2,
+    ).reshape(local, width + units, width)
+    return block_out, hid_sum, gates_mine.T.reshape(n_exp, local, tree_rows), grads
 
 
 def shards(
@@ -660,6 +1061,8 @@
     kv_width = KV * HD
     score_scale = HD ** (-0.5)
     n_dp, n_exp = lax.axis_size("dp"), lax.axis_size("expert")
+    grad_y = lax.all_gather(cotangent, "expert", axis=0, tiled=False)
+    routes_all = lax.all_gather(routes, "expert", axis=0, tiled=False)
     rows = w_query.shape[0]
     small = jnp.concatenate(
         [w_router, attn_gain[:, None], moe_gain[:, None], jnp.zeros((rows, 128 - EXPERTS - 2), w_router.dtype)], axis=1
@@ -711,69 +1114,12 @@
     picked = jnp.sum(route_hot * logits[:, None, :], axis=2)
     picked_exp = jnp.exp(picked - jnp.max(picked, axis=1, keepdims=True))
     gate_weights = picked_exp / jnp.sum(picked_exp, axis=1, keepdims=True)
-    trees = lax.axis_size("expert")
-    here = lax.axis_index("expert")
-    local = expert_in.shape[0]
-    first = here * local
-    routes_all = lax.all_gather(routes, "expert", axis=0, tiled=False)
-    grad_y = lax.all_gather(cotangent, "expert", axis=0, tiled=False)
-    hidden_all = ring_gather(n_exp, hidden2, 2)
-    own_ids = first + jnp.arange(local, dtype=jnp.int32)
-    hot_all = routes_all[:, :, :, None] == expert_ids[None, None, None, :]
-    chosen_all = jnp.any(hot_all, axis=2)
-    chosen = jnp.any(routes_all[:, :, :, None] == own_ids[None, None, None, :], axis=2)
-    lower = jnp.tril(jnp.ones((tree_rows, tree_rows), jnp.bfloat16), -1)
-    rank = jnp.einsum(
-        "tu,jue->jet", lower, chosen.astype(jnp.bfloat16), preferred_element_type=jnp.float32
-    ).astype(jnp.int32)
-    slots = jnp.arange(capacity, dtype=jnp.int32)
-    chosen_t = chosen.transpose(0, 2, 1)
-    place = (rank[:, :, None, :] == slots[None, None, :, None]) & chosen_t[:, :, None, :]
-    place = place.astype(jnp.bfloat16)
-    logits_all = jnp.einsum(
-        "jtd,de->jte", hidden_all, router_full, preferred_element_type=jnp.float32
-    )
-    masked = jnp.where(chosen_all, logits_all, -1e30)
-    weight = jnp.exp(masked - jnp.max(masked, axis=-1, keepdims=True))
-    weight = weight / jnp.sum(weight, axis=-1, keepdims=True)
-    gates_own = lax.dynamic_slice_in_dim(weight, first, local, axis=2)
-    gate_slot = jnp.einsum(
-        "jest,jte->ejs", place.astype(jnp.float32), gates_own, precision=lax.Precision.HIGHEST
-    )[..., None]
-    sent = jnp.einsum("jest,jtd->ejsd", place, hidden_all, preferred_element_type=jnp.float32)
-    sent = sent.astype(jnp.bfloat16)
-    grad_rows = jnp.einsum("jest,jtd->ejsd", place, grad_y, preferred_element_type=jnp.float32)
-    grad_rows = grad_rows.astype(jnp.bfloat16)
-    gate_up = jnp.einsum("ejsd,edf->ejsf", sent, expert_in, preferred_element_type=jnp.float32)
-    activated, glu_back = jax.vjp(gated_unit, gate_up)
-    act_low = activated.astype(jnp.bfloat16).astype(jnp.float32)
-    act_scaled = (act_low * gate_slot).astype(jnp.bfloat16)
-    made = jnp.einsum(
-        "ejsf,efd->ejsd", act_scaled, expert_out, preferred_element_type=jnp.float32
-    ).astype(jnp.bfloat16)
-    out_part = jnp.einsum("jest,ejsd->jtd", place, made, preferred_element_type=jnp.float32)
-    block_out = ring_scatter(n_exp, out_part.astype(jnp.bfloat16), (middle,), jnp.bfloat16, 3)
+    run_experts = experts if n_exp == 8 else experts_plain
+    block_out, hid_sum, gates_mine, grads_low = run_experts(
+        n_dp, n_exp, hidden2, grad_y, routes_all, router_full, expert_in, expert_out, middle, 2
+    )
+    gates_mine = gates_mine[:, : expert_in.shape[0]].reshape(EXPERTS, tree_rows).T
     grad_result = cotangent.astype(jnp.float32)
-    grad_act = jnp.einsum(
-        "ejsd,efd->ejsf", grad_rows, expert_out, preferred_element_type=jnp.float32
-    )
-    gate_dot = jnp.sum(act_low * grad_act, axis=-1)
-    gates_back = jnp.einsum(
-        "jest,ejs->jte", place.astype(jnp.float32), gate_dot, precision=lax.Precision.HIGHEST
-    )
-    grad_out_w = jnp.einsum(
-        "ejsf,ejsd->efd", act_scaled, grad_rows, preferred_element_type=jnp.float32
-    )
-    grad_gate_up = glu_back(grad_act * gate_slot)[0].astype(jnp.bfloat16)
-    grad_sent = jnp.einsum(
-        "ejsf,edf->ejsd", grad_gate_up, expert_in, preferred_element_type=jnp.float32
-    ).astype(jnp.bfloat16)
-    grad_in_w = jnp.einsum(
-        "ejsd,ejsf->edf", sent, grad_gate_up, preferred_element_type=jnp.float32
-    )
-    hid_part = jnp.einsum("jest,ejsd->jtd", place, grad_sent, preferred_element_type=jnp.float32)
-    gates_mine = lax.all_to_all(gates_back, "expert", split_axis=0, concat_axis=2, tiled=True)[0]
-    hid_sum = ring_scatter(n_exp, hid_part.astype(jnp.bfloat16), (), jnp.float32, 4)
     gate_dense = jnp.sum(route_hot * gate_weights[:, :, None], axis=1)
     grad_logits = (
         gate_dense
@@ -783,14 +1129,9 @@
     grad_hidden2 = hid_sum + jnp.einsum(
         "te,de->td", grad_logits, router_full, preferred_element_type=jnp.float32
     )
-    expert_in_share, expert_out_share = (
-        lax.psum_scatter(
-            grad_in_w.astype(jnp.bfloat16), "dp", scatter_dimension=1, tiled=True
-        ).astype(jnp.float32),
-        lax.psum_scatter(
-            grad_out_w.astype(jnp.bfloat16), "dp", scatter_dimension=1, tiled=True
-        ).astype(jnp.float32),
-    )
+    expert_share = lax.psum_scatter(grads_low, "dp", scatter_dimension=1, tiled=True)
+    expert_in_share = expert_share[:, : width // n_dp].astype(jnp.float32)
+    expert_out_share = expert_share[:, width // n_dp :].astype(jnp.float32)
     grad_mid_norm, grad_gain_second = second_back(grad_hidden2)
     grad_middle = grad_result + grad_mid_norm
     grad_branch = grad_middle.astype(jnp.bfloat16)

time: 551 us -> 445 us (0.81); the launches traced: 541 us -> 441 us
  matrix products: 177 us -> 37.4 us
  Pallas kernels: 265 us -> 308 us
  local copies, waits for them, and re-layouts: 36.2 us -> 44 us
  other arithmetic: 27.4 us -> 21.3 us
    dot_general x14 -> x0, matrix products: 139 us -> none  [the longest x1 18.6 us: shards(): jnp.einsum('ejsd,efd->ejsf', grad_rows, expert_out, preferred_element_typ...]
    pallas_call x3 -> x1, Pallas kernels: 153 us -> 178 us  [experts(): pl.pallas_call(functools.partial(experts_body, n_dp, n_exp), out_shape=[s...]
    pallas_call x1, Pallas kernels: 76 us -> 93.6 us  [reduce_grads(): pl.pallas_call(functools.partial(grads_body, n_dp, n_exp, chunks), out_sh...]
    unnamed x117 -> x77, local copies, waits for them, and re-layouts: 9.27 us -> 13.5 us
  transfers between devices with their start and end apart: 4 -> 2, of which waited for: 0 -> 0; matrix products, arithmetic and copies ran while one was open for 35% -> 19% of each run, Pallas kernels for 49% -> 29%
where the time goes in v3:
time: 445 us; the launch traced here: 441 us
  Pallas kernels  308 us (69%)
  local copies, waits for them, and re-layouts  44 us (10%)
  matrix products  37.4 us (8%)
  other arithmetic  21.3 us (5%)
  blocking collectives  15 us (3%)
  between operations  14.9 us (3%)
    pallas_call x1, Pallas kernels, experts(): pl.pallas_call(functools.partial(experts_body, n_dp, n_exp), out_shape=[s...  178 us
    pallas_call x1, Pallas kernels, reduce_grads(): pl.pallas_call(functools.partial(grads_body, n_dp, n_exp, chunks), out_sh...  93.6 us
    pallas_call x1, Pallas kernels, gather_weights(): pl.pallas_call(functools.partial(weights_body, n_dp), out_shape=out_shape...  35.7 us
    all_gather x1, blocking collectives, shards(): routes_all = lax.all_gather(routes, 'expert', axis=0, tiled=False)  15 us
    unnamed x77, local copies, waits for them, and re-layouts  13.5 us
    concatenate x1, local copies, waits for them, and re-layouts, shards(): jnp.concatenate([grad_w_q.astype(low), grad_w_kv.astype(low), grad_w_out....  11 us
  transfers between devices with their start and end apart: 2, of which 0 were waited for; matrix products, arithmetic and copies ran while one was open for 19% of the time, Pallas kernels for 29%

profile of v3, /device:TPU:0, one launch (start us, length us, event | category | flops | bytes accessed | tf_op | source)
XLA Modules:
  0.0 441.1 jit_solution(17664396420207279027)
XLA Ops:
  7.2 0.7 all-gather.5.cloned.1.call-update
  8.0 0.8 broadcast_in_dim.45
  8.8 0.8 broadcast_in_dim.46
  9.5 0.8 copy.116
  10.5 0.7 maximum_maximum_fusion.refs_3_
  11.2 35.7 %gather_weights.1 = (bf16[1024,1024]{1,0:T(8,128)(2,1)}, bf16[1024,1024]{1,0:T(8,128)(2,1)}, bf16[1024,1024]{1,0:T(8,128)(2,1)}, bf16[1024,128]{1,0:T(8,128)(2,1)}) custom-call(bf16[256,1024]{1,0:T(8,128)(2,1)} %refs_0_.1, bf16[256,1024]{1,0:T(8,128)(2,1)} %refs_1_.1, bf16[256,1024]{1,0:T(8,128)(2,1)} %refs_2_.1, bf16[256,128]{1,0:T(8,128)(2,1)} %maximum_maximum_fusion.refs_3_), custom_call_target="tpu_custom_call" | custom-call | tf_op jit(solution)/shard_map/gather_weights/pallas_call | solution.py:139
  47.0 1.8 copy.124
  48.7 1.4 convert_reduce_fusion
  50.4 2.5 fusion.77
  53.0 0.6 copy-done
  53.7 0.7 gather_fusion
  54.6 0.6 fusion.27
  55.2 0.9 copy.120
  56.1 15.0 %all-gather.2 = s32[8,320,8]{1,2,0:T(8,128)S(1)} all-gather(s32[1,320,8]{1,2,0:T(8,128)S(1)} %bitcast.119), channel_id=3, replica_groups=mesh['dp'=4,'expert'=8] {'expert'}, dimensions={0}, use_global_device_ids=true | all-gather | bytes 92160 | tf_op jit(solution)/shard_map/all_gather | solution.py:1065
  71.0 1.5 copy.125.routes_c
  72.5 0.9 copy.119
  74.0 0.7 broadcast_multiply_fusion.1
  74.9 1.4 copy-done.33
  76.3 1.3 fusion.75
  78.1 0.6 copy-done.27
  78.7 1.5 fusion.80
  80.2 1.2 fusion.3
  81.4 1.8 copy-done.1
  83.2 1.6 fusion.14
  84.8 1.0 multiply_reduce_fusion.2
  86.0 0.8 slice_bitcast_fusion.wr_t
  86.9 1.0 multiply_convert_fusion.hid_ref
  87.9 178.4 %experts.1 = (bf16[320,1024]{1,0:T(8,128)(2,1)}, f32[320,1024]{1,0:T(8,128)}, f32[8,8,320]{2,1,0:T(8,128)}, bf16[4,1536,1024]{2,1,0:T(8,128)(2,1)}) custom-call(bf16[320,1024]{1,0:T(8,128)(2,1)} %multiply_convert_fusion.hid_ref, bf16[8,320,1024]{2,1,0:T(8,128)(2,1)} %bitcast.103, s32[8,8,320]{2,1,0:T(8,128)} %bitcast.108, s32[8,320,8]{2,1,0:T(8,128)} %copy.125.routes_c, ...), custom_call_target="tpu_custom_call" | custom-call | tf_op jit(solution)/shard_map/experts/pallas_call | solution.py:852
  266.4 1.0 copy-done.7
  268.1 0.7 copy-done.3
  268.8 2.0 multiply_reduce_fusion
  270.8 0.4 fusion.17
  271.2 1.0 copy-done.5
  272.2 0.6 copy-done.19
  272.9 0.9 convolution_convert_fusion.3
  273.8 1.2 copy.126
  275.1 0.9 copy.133
  276.0 0.9 convert_element_type.172
  276.9 8.6 %fusion = (f32[8,2,320]{2,1,0:T(2,128)S(1)}, f32[8,320,320,2]{2,1,3,0:T(8,128)}) fusion(f32[8,2,320,320]{2,3,1,0:T(8,128)} %copy-done.1, f32[8,2,320]{2,1,0:T(2,128)S(1)} %bitcast.111, bf16[320,8,64,1]{0,2,3,1:T(8,128)(2,1)} %bitcast.106, bf16[320,8,2,64]{0,3,2,1:T(8,128)(2,1)} %bitcast.97), kind=kOutput, calls=%fused_computation.3 | convolution fusion | flops 214625280 | bytes 14131200 | tf_op jit(solution)/shard_map/tkgd,skd->kgts/dot_general | solution.py:1148
  285.5 6.9 %fusion.2 = bf16[8,2,320,320]{2,3,1,0:T(8,128)(2,1)} fusion(f32[8,320,320,2]{2,1,3,0:T(8,128)} %get-tuple-element.107, f32[8,2,320,320]{2,3,1,0:T(8,128)S(1)} %bitcast.96, f32[8,2,320]{2,1,0:T(2,128)S(1)} %get-tuple-element.106, f32[8,2,320]{2,1,0:T(2,128)S(1)} %bitcast.112), kind=kLoop, calls=%fused_computation.5 | loop fusion | flops 6553600 | bytes 16424960 | tf_op jit(solution)/shard_map/convert_element_type | solution.py:1153
  292.4 4.0 broadcast_multiply_fusion
  296.6 0.8 copy-done.22
  297.5 1.0 bitcast_multiply_fusion.1
  298.6 0.3 fusion.11
  298.9 1.3 copy-done.34
  300.2 1.2 fusion.81
  301.4 1.2 fusion.24
  302.7 0.9 copy-done.32
  303.6 2.3 fusion.16
  305.8 0.9 convert_element_type.171
  306.7 3.0 convolution_convert_fusion.1
  309.8 2.8 convolution_convert_fusion.2
  312.5 1.3 convolution_convert_fusion
  313.8 0.7 broadcast_in_dim.44
  314.5 11.0 %concatenate.36.g_ref = bf16[1024,3200]{1,0:T(8,128)(2,1)} concatenate(bf16[1024,1024]{1,0:T(8,128)(2,1)} %convolution_convert_fusion.2, bf16[1024,1024]{1,0:T(8,128)(2,1)} %convolution_convert_fusion.1, bf16[1024,1024]{1,0:T(8,128)(2,1)S(1)} %convolution_convert_fusion, bf16[1024,32]{1,0:T(8,128)(2,1)} %copy.133, bf16[1024,1]{1,0:T(8,128)(2,1)} %convert_element_type.171, ...), dimensions={1} | concatenate | bytes 13107200 | tf_op jit(solution)/shard_map/concatenate | solution.py:1183
  325.5 93.6 %reduce_grads.1 = f32[256,3200]{1,0:T(8,128)} custom-call(bf16[1024,3200]{1,0:T(8,128)(2,1)} %concatenate.36.g_ref), custom_call_target="tpu_custom_call" | custom-call | tf_op jit(solution)/shard_map/reduce_grads/pallas_call | solution.py:502
  419.1 0.9 slice.86
  420.0 0.7 copy.136
  420.7 1.8 slice_reduce_fusion
  422.5 3.8 fusion.79
  426.3 1.4 fusion.18
  427.7 2.9 slice_convert_fusion.1
  430.7 2.5 slice_convert_fusion
  433.2 0.8 copy.150
  (106 shorter events, 3.4 us)
Async XLA Ops:
  7.2 80.7 %all-gather.5.cloned.1.call-start = ((), (), s32[]{:S(2)}) async-start(), calls=%async_computation.2 | async-start | bytes 5898240 | tf_op jit(solution)/shard_map/all_gather | solution.py:1064
  7.9 42.2 %copy-start.10 = (bf16[320,1024]{1,0:T(8,128)(2,1)S(1)}, bf16[320,1024]{1,0:T(8,128)(2,1)}, u32[]{:S(2)}) copy-start(bf16[320,1024]{1,0:T(8,128)(2,1)} %param.12) | copy-start | bytes 1966084
  7.9 419.8 %reduce-scatter.2.cloned.1.call-start = ((), (), s32[]{:S(2)}) async-start(), calls=%async_computation.1 | async-start | bytes 15728640 | tf_op jit(solution)/shard_map/reduce_scatter | solution.py:1132
  50.4 24.5 %copy-start.30 = (f32[320]{0:T(512)}, f32[320]{0:T(512)S(1)}, u32[]{:S(2)}) copy-start(f32[320]{0:T(512)S(1)} %fusion.68) | copy-start | bytes 3844
  52.9 2.2 copy-start.17
  53.0 0.7 copy-start
  53.0 3.0 copy-start.28
  56.0 17.4 %slice-start.2 = ((f32[320,1024]{1,0:T(8,128)}), f32[320,512]{1,0:T(8,128)S(1)}, s32[]{:S(2)}) async-start(f32[320,1024]{1,0:T(8,128)} %copy-done.17), calls=%async_computation.5 | async-start | bytes 1310720 | tf_op jit(solution)/shard_map/slice | solution.py:1089
  71.0 1.5 copy-start.24
  74.7 1.6 copy-start.33
  77.8 0.9 copy-start.27
  78.7 1.5 copy-start.9
  80.2 3.0 copy-start.1
  80.2 3.0 copy-start.20
  83.2 1.6 copy-start.18
  84.8 1.0 copy-start.14
  84.8 1.2 copy-start.25
  85.8 1.1 copy-start.2
  266.4 1.1 copy-start.7
  266.4 1.6 copy-start.29
  267.5 1.3 copy-start.3
  268.8 2.0 copy-start.16
  270.8 2.1 copy-start.19
  271.2 1.1 copy-start.5
  276.9 8.6 %slice-start = ((s8[7864320]{0:T(1024)(128)(4,1)}), s8[4194304]{0:T(1024)(128)(4,1)S(1)}, s32[]{:S(2)}) async-start(s8[7864320]{0:T(1024)(128)(4,1)} %bitcast.95), calls=%async_computation.3 | async-start | bytes 8388608
  276.9 8.6 %slice-start.1 = ((s8[7864320]{0:T(1024)(128)(4,1)}), s8[3670016]{0:T(1024)(128)(4,1)S(1)}, s32[]{:S(2)}) async-start(s8[7864320]{0:T(1024)(128)(4,1)} %bitcast.95), calls=%async_computation.4 | async-start | bytes 7340032
  292.4 5.1 %copy-start.4 = (bf16[8,2,320,320]{2,3,1,0:T(8,128)(2,1)S(1)}, bf16[8,2,320,320]{2,3,1,0:T(8,128)(2,1)}, u32[]{:S(2)}) copy-start(bf16[8,2,320,320]{2,3,1,0:T(8,128)(2,1)} %fusion.2) | copy-start | bytes 9830404
  296.5 0.9 copy-start.22
  296.5 1.0 copy-start.23
  298.6 1.6 copy-start.34
  300.2 1.2 copy-start.8
  301.4 1.3 copy-start.11
  301.4 1.3 copy-start.31
  301.4 2.1 copy-start.32
  309.8 2.8 copy-start.6
  309.8 2.8 copy-start.15
  422.5 3.8 copy-start.12
  422.5 3.8 copy-start.21
  427.7 2.9 copy-start.13
  430.7 2.5 copy-start.26
Sparse Core Ops, SparseCore 0:
  9.7 59.2 all-gather.4
  266.5 139.2 reduce-scatter.1

commit v4 on v3

--- a/solution.py
+++ b/solution.py
@@ -527,11 +527,12 @@
 
 
 def experts_body(n_dp, n_exp, hid_ref, gy_hbm, routes_t, routes_c, wr_t, w_in_hbm, w_out_hbm, middle,
-                 block_out, hid_sum, gates_out, grads_hbm,
-                 x_all, w_in, w_out, sent, grows, gu, tmp, acts, stage, slots, gates, dots,
+                 block_out, hid_sum, gates_out, in_share, out_share,
+                 x_all, w_in, w_out, sent, grows, gu, tmp, acts, stage, slots, gates, dots, wide,
                  pair_buf, held, got, *sems):
-    w_sem, gy_sem, stage_sem, own_sem, ready, gate_send, gate_recv = sems[:7]
-    gather_sems, out_sems, hid_sems = sems[7:11], sems[11:15], sems[15:19]
+    w_sem, gy_sem, wide_sem, own_sem, ready, gate_send, gate_recv, dp_ready, dp_send, dp_recv = sems[:10]
+    gather_sems, out_sems, hid_sems = sems[10:14], sems[14:18], sems[18:22]
+    me = lax.axis_index("dp")
     local, _, width = sent.shape
     tree, hidden_units = hid_ref.shape[0], w_out.shape[1]
     rows_e = local * SLOTS
@@ -539,7 +540,7 @@
     mine, core, depth = ring.mine, ring.core, ring.depth
     first = mine * local
     peers = [lax.rem(mine + k, n_exp) for k in range(1, n_exp)]
-    greet([(None, {"expert": e}) for e in peers])
+    greet([(None, {"expert": e}) for e in peers] + [(None, {"dp": me ^ bit}) for bit in (1, 2)])
 
     weights = [pltpu.make_async_copy(w_in_hbm, w_in, w_sem.at[0]), pltpu.make_async_copy(w_out_hbm, w_out, w_sem.at[1])]
     gather = RingGather(ring, hid_ref, x_all, gather_sems)
@@ -550,7 +551,7 @@
     own.start()
 
     def gy_buf(j):
-        return stage.at[pl.ds(pl.multiple_of(lax.rem(j, 2) * tree, 16), tree)]
+        return stage.at[lax.rem(j, 2), pl.ds(0, tree)]
 
     def gy_copy(j):
         return pltpu.make_async_copy(gy_hbm.at[j], gy_buf(j), gy_sem.at[lax.rem(j, 2)])
@@ -725,8 +726,53 @@
     out.first()
     out.early()
 
-    def stage_copy(e):
-        return pltpu.make_async_copy(stage, grads_hbm.at[e], stage_sem)
+    in_rows, out_rows = width // n_dp, hidden_units // n_dp
+    cut = (in_rows + out_rows) // 2
+
+    def grad_half(e, r, h):
+        at = 2 * r + h
+        return gu.at[e, pl.ds(at * cut, cut)] if at < 5 else stage.at[e, pl.ds((at - 5) * cut, cut)]
+
+    def grad_land(e, k):
+        return w_in.at[e, pl.ds(k * cut, cut)] if k < 5 else w_out.at[e, pl.ds(0, cut)]
+
+    def grad_hop(e, step, h, which):
+        bit = (1, 2)[h] if step == 0 else (2, 1)[h]
+        r = bit if which == 0 else 3
+        k = 2 * h + which if step == 0 else 4 + h
+        return remote(grad_half(e, r, h), grad_land(e, k), dp_send.at[e, k], dp_recv.at[e, k], dp=me ^ bit)
+
+    def grads_start(e):
+        pl.semaphore_wait(dp_ready.at[e], 2)
+        for which in (1, 0):
+            for h in range(2):
+                grad_hop(e, 0, h, which).start()
+
+    def grads_turn(e):
+        for which in (1, 0):
+            for h in range(2):
+                grad_hop(e, 0, h, which).wait_recv()
+                kept = 0 if which == 0 else (2, 1)[h]
+                add_rows(grad_half(e, kept, h), grad_half(e, kept, h), grad_land(e, 2 * h + which))
+                if which == 1:
+                    grad_hop(e, 1, h, 0).start()
+
+    def wide_copies(e):
+        return (
+            pltpu.make_async_copy(wide.at[pl.ds(0, in_rows)], in_share.at[e], wide_sem.at[0]),
+            pltpu.make_async_copy(wide.at[pl.ds(in_rows, out_rows)], out_share.at[e], wide_sem.at[1]),
+        )
+
+    def grads_end(e):
+        for h in range(2):
+            grad_hop(e, 1, h, 0).wait_recv()
+            add_rows(wide.at[pl.ds(h * cut, cut)], grad_half(e, 0, h), grad_land(e, 4 + h))
+        for copy in wide_copies(e):
+            copy.start()
+        for step, h, which in ((0, 0, 0), (0, 0, 1), (0, 1, 0), (0, 1, 1), (1, 0, 0), (1, 1, 0)):
+            grad_hop(e, step, h, which).wait_send()
+        for copy in wide_copies(e):
+            copy.wait()
 
     block = 4 * SLOTS
     sub8 = lax.broadcasted_iota(jnp.int32, (8, tree), 0)
@@ -755,22 +801,15 @@
             return inner
 
         lax.fori_loop(0, n_exp // 4, one_block, 0)
-        pl.when(e > 0)(lambda: stage_copy(e - 1).wait())
-        in_rows, out_rows = width // n_dp, hidden_units // n_dp
-        grad_out = dot(acts[...], grows[e], 0, 0).astype(LOW)
-        for d in range(n_dp):
-            stage[pl.ds(d * (in_rows + out_rows) + in_rows, out_rows), :] = grad_out[d * out_rows : (d + 1) * out_rows]
-
-        def in_half(h, inner):
-            grad_in = dot(sent[e, :, pl.ds(pl.multiple_of(h * 512, 512), 512)], tmp[...], 0, 0).astype(LOW)
-            per = 512 // in_rows
-            for k in range(per):
-                at = pl.multiple_of((h * per + k) * (in_rows + out_rows), 16)
-                stage[pl.ds(at, in_rows), :] = grad_in[k * in_rows : (k + 1) * in_rows]
-            return inner
-
-        lax.fori_loop(0, halves, in_half, 0)
-        stage_copy(e).start()
+        pl.when(e > 0)(lambda: grads_start(e - 1))
+        for r in range(n_dp):
+            d = me ^ r
+            grad_in = dot(sent[e, :, pl.ds(pl.multiple_of(d * in_rows, in_rows), in_rows)], tmp[...], 0, 0).astype(LOW)
+            grad_out = dot(acts[:, pl.ds(pl.multiple_of(d * out_rows, out_rows), out_rows)], grows[e], 0, 0).astype(LOW)
+            grad_half(e, r, 0)[...] = grad_in[:cut]
+            half = grad_half(e, r, 1)
+            half[pl.ds(0, in_rows - cut), :] = grad_in[cut:]
+            half[pl.ds(in_rows - cut, out_rows), :] = grad_out
 
         def back_half(m, inner):
             rows = pl.ds(pl.multiple_of(m * 512, 512), 512)
@@ -778,13 +817,17 @@
             return inner
 
         lax.fori_loop(0, n_exp * SLOTS // 512, back_half, 0)
+        for bit in (1, 2):
+            pl.semaphore_signal(dp_ready.at[e], inc=1, device_id={"dp": me ^ bit}, device_id_type=MESH)
         pl.when(e == local // 2 - 1)(out.late)
+        pl.when(e >= 2)(lambda: grads_turn(e - 2))
         return carry
 
     dots[...] = jnp.zeros(dots.shape, F32)
+    middle_copy = pltpu.make_async_copy(middle, wide.at[pl.ds(0, tree)], wide_sem.at[0])
+    middle_copy.start()
     lax.fori_loop(0, local, backward, 0)
-    for partner in (ring.pair, ring.right, ring.left):
-        pl.semaphore_signal(ready, inc=1, device_id={"expert": partner}, device_id_type=MESH)
+    grads_start(local - 1)
 
     gate_copies = []
     for k, e in enumerate(peers):
@@ -792,15 +835,12 @@
         copy.start()
         gate_copies.append(copy)
     gates_out[mine] = dots[mine]
-    out.last(block_out, middle)
-
-    def part(j):
-        return grows.at[lax.div(j, 2), pl.ds(pl.multiple_of(lax.rem(j, 2) * tree, 16), tree)]
-
-    def spare(b):
-        return gu.at[b // 3, pl.ds((b % 3) * tree, tree)]
-
-    hid = RingScatter(ring, part, (spare, lambda d: spare(depth + d), lambda side, d: spare(2 * depth + 2 * side + d)), hid_sems)
+    middle_copy.wait()
+    out.last(block_out, wide.at[pl.ds(0, tree)])
+    out.finish_sends()
+    for partner in (ring.pair, ring.right, ring.left):
+        pl.semaphore_signal(ready, inc=1, device_id={"expert": partner}, device_id_type=MESH)
+    hid = RingScatter(ring, lambda e: x_all.at[e], views((pair_buf, held, got)), hid_sems)
 
     def combine_hid(g, carry):
         d = jnp.where(g == 0, 2, jnp.where(g == 1, 1, jnp.where(g == 2, depth - 1, 0)))
@@ -810,7 +850,7 @@
             j = 2 * chip + q
             rows = pl.ds(pl.multiple_of(j * SLOTS, SLOTS), SLOTS)
             made = jnp.concatenate([sent[i, rows, :] for i in range(local)], axis=0)
-            part(j)[...] = dot(places_t(j), made).astype(LOW)
+            x_all[j] = dot(places_t(j), made).astype(LOW)
             return inner
 
         lax.fori_loop(0, 2, one_tree, 0)
@@ -828,15 +868,22 @@
 
     lax.fori_loop(0, depth, combine_hid, 0)
     hid.early()
+    grads_turn(local - 2)
+    grads_end(0)
     hid.late()
-    hid.last(hid_sum)
+    grads_end(1)
+    grads_turn(local - 1)
+    hid.last(wide.at[pl.ds(0, tree)])
+    hid_copy = pltpu.make_async_copy(wide.at[pl.ds(0, tree)], hid_sum, wide_sem.at[0])
+    hid_copy.start()
+    hid_copy.wait()
+    for e in range(2, local):
+        grads_end(e)
 
     for k, copy in enumerate(gate_copies):
         copy.wait_send()
         source = lax.rem(mine + n_exp - 1 - k, n_exp)
         remote(dots.at[mine], gates_out.at[source], gate_send.at[k], gate_recv.at[k], expert=mine).wait_recv()
-    stage_copy(local - 1).wait()
-    out.finish_sends()
     hid.finish_sends()
 
 
@@ -855,10 +902,11 @@
             shape((tree, width), LOW),
             shape((tree, width), F32),
             shape((n_exp, 8, tree), F32),
-            shape((local, width + units, width), LOW),
+            shape((local, width // n_dp, width), F32),
+            shape((local, units // n_dp, width), F32),
         ],
-        in_specs=[pl.BlockSpec(memory_space=s) for s in (VMEM, ANY, VMEM, VMEM, VMEM, ANY, ANY, VMEM)],
-        out_specs=[pl.BlockSpec(memory_space=s) for s in (VMEM, VMEM, VMEM, ANY)],
+        in_specs=[pl.BlockSpec(memory_space=s) for s in (VMEM, ANY, VMEM, VMEM, VMEM, ANY, ANY, ANY)],
+        out_specs=[pl.BlockSpec(memory_space=s) for s in (VMEM, ANY, VMEM, ANY, ANY)],
         scratch_shapes=[
             pltpu.VMEM((n_exp, tree, width), LOW),
             pltpu.VMEM((local, width, both), LOW),
@@ -868,12 +916,14 @@
             pltpu.VMEM((local, rows, both), LOW),
             pltpu.VMEM((max(rows, 2 * local * SLOTS), width), LOW),
             pltpu.VMEM((rows, units), LOW),
-            pltpu.VMEM((width + units, width), LOW),
+            pltpu.VMEM((local, 3 * (width + units) // (2 * n_dp), width), LOW),
             pltpu.VMEM((n_exp, 8, tree), F32),
             pltpu.VMEM((n_exp, 8, tree), F32),
             pltpu.VMEM((n_exp, 8, tree), F32),
+            pltpu.VMEM(((width + units) // n_dp, width), F32),
             *bufs,
-            sem((2,)), sem((2,)), sem, sem, pltpu.SemaphoreType.REGULAR, sem((n_exp - 1,)), sem((n_exp - 1,)),
+            sem((2,)), sem((2,)), sem((2,)), sem, pltpu.SemaphoreType.REGULAR, sem((n_exp - 1,)), sem((n_exp - 1,)),
+            pltpu.SemaphoreType.REGULAR((local,)), sem((local, 6)), sem((local, 6)),
             *RingGather.scratch(n_exp), *out_sems, *hid_sems,
         ],
         compiler_params=pltpu.CompilerParams(
@@ -1037,7 +1087,9 @@
         ],
         axis=2,
     ).reshape(local, width + units, width)
-    return block_out, hid_sum, gates_mine.T.reshape(n_exp, local, tree_rows), grads
+    share = lax.psum_scatter(grads, "dp", scatter_dimension=1, tiled=True).astype(jnp.float32)
+    gates_mine = gates_mine.T.reshape(n_exp, local, tree_rows)
+    return block_out, hid_sum, gates_mine, share[:, : width // n_dp], share[:, width // n_dp :]
 
 
 def shards(
@@ -1114,8 +1166,8 @@
     picked = jnp.sum(route_hot * logits[:, None, :], axis=2)
     picked_exp = jnp.exp(picked - jnp.max(picked, axis=1, keepdims=True))
     gate_weights = picked_exp / jnp.sum(picked_exp, axis=1, keepdims=True)
-    run_experts = experts if n_exp == 8 else experts_plain
-    block_out, hid_sum, gates_mine, grads_low = run_experts(
+    run_experts = experts if (n_dp, n_exp) == (4, 8) else experts_plain
+    block_out, hid_sum, gates_mine, expert_in_share, expert_out_share = run_experts(
         n_dp, n_exp, hidden2, grad_y, routes_all, router_full, expert_in, expert_out, middle, 2
     )
     gates_mine = gates_mine[:, : expert_in.shape[0]].reshape(EXPERTS, tree_rows).T
@@ -1129,9 +1181,6 @@
     grad_hidden2 = hid_sum + jnp.einsum(
         "te,de->td", grad_logits, router_full, preferred_element_type=jnp.float32
     )
-    expert_share = lax.psum_scatter(grads_low, "dp", scatter_dimension=1, tiled=True)
-    expert_in_share = expert_share[:, : width // n_dp].astype(jnp.float32)
-    expert_out_share = expert_share[:, width // n_dp :].astype(jnp.float32)
     grad_mid_norm, grad_gain_second = second_back(grad_hidden2)
     grad_middle = grad_result + grad_mid_norm
     grad_branch = grad_middle.astype(jnp.bfloat16)

time: 445 us -> 442 us (level)
    pallas_call x1, Pallas kernels: 178 us -> 201 us  [experts(): pl.pallas_call(functools.partial(experts_body, n_dp, n_exp), out_shape=[s...]
    pallas_call x1, Pallas kernels: 93.6 us -> 75.6 us  [reduce_grads(): pl.pallas_call(functools.partial(grads_body, n_dp, n_exp, chunks), out_sh...]
    convert_element_type x2 -> x0, other arithmetic: 5.42 us -> none  [the longest x1 2.94 us: shards(): expert_out_share = expert_share[:, width // n_dp:].astype(jnp.float32)]
    unnamed x77 -> x67, local copies, waits for them, and re-layouts: 13.5 us -> 16.5 us
  transfers between devices with their start and end apart: 2 -> 1, of which waited for: 0 -> 0; matrix products, arithmetic and copies ran while one was open for 19% -> 5% of each run, Pallas kernels for 29% -> 8%
where the time goes in v4:
time: 442 us; the launch traced here: 438 us
  Pallas kernels  312 us (71%)
  local copies, waits for them, and re-layouts  39.7 us (9%)
  matrix products  38.1 us (9%)
  other arithmetic  17.1 us (4%)
  between operations  15 us (3%)
  blocking collectives  14.9 us (3%)
    pallas_call x1, Pallas kernels, experts(): pl.pallas_call(functools.partial(experts_body, n_dp, n_exp), out_shape=[s...  201 us
    pallas_call x1, Pallas kernels, reduce_grads(): pl.pallas_call(functools.partial(grads_body, n_dp, n_exp, chunks), out_sh...  75.6 us
    pallas_call x1, Pallas kernels, gather_weights(): pl.pallas_call(functools.partial(weights_body, n_dp), out_shape=out_shape...  35.8 us
    unnamed x67, local copies, waits for them, and re-layouts  16.5 us
    all_gather x1, blocking collectives, shards(): routes_all = lax.all_gather(routes, 'expert', axis=0, tiled=False)  14.9 us
    concatenate x1, local copies, waits for them, and re-layouts, shards(): jnp.concatenate([grad_w_q.astype(low), grad_w_kv.astype(low), grad_w_out....  10.7 us
  transfers between devices with their start and end apart: 1, of which 0 were waited for; matrix products, arithmetic and copies ran while one was open for 5% of the time, Pallas kernels for 8%

profile of v4, /device:TPU:0, one launch (start us, length us, event | category | flops | bytes accessed | tf_op | source)
XLA Modules:
  0.0 438.0 jit_solution(3266199828052765136)
XLA Ops:
  7.2 0.7 all-gather.5.cloned.1.call-update
  7.9 0.8 broadcast_in_dim.45
  8.7 0.8 broadcast_in_dim.46
  9.4 0.8 copy.116
  10.4 0.7 maximum_maximum_fusion.refs_3_
  11.1 35.8 %gather_weights.1 = (bf16[1024,1024]{1,0:T(8,128)(2,1)}, bf16[1024,1024]{1,0:T(8,128)(2,1)}, bf16[1024,1024]{1,0:T(8,128)(2,1)}, bf16[1024,128]{1,0:T(8,128)(2,1)}) custom-call(bf16[256,1024]{1,0:T(8,128)(2,1)} %refs_0_.1, bf16[256,1024]{1,0:T(8,128)(2,1)} %refs_1_.1, bf16[256,1024]{1,0:T(8,128)(2,1)} %refs_2_.1, bf16[256,128]{1,0:T(8,128)(2,1)} %maximum_maximum_fusion.refs_3_), custom_call_target="tpu_custom_call" | custom-call | tf_op jit(solution)/shard_map/gather_weights/pallas_call | solution.py:139
  46.9 1.4 convert_reduce_fusion
  48.4 0.2 fusion.19
  48.6 2.5 fusion.77
  51.2 0.8 copy-done.18
  52.1 0.9 copy.124
  52.9 0.3 copy.121
  53.3 0.7 gather_fusion
  53.9 0.3 fusion.34
  54.2 0.6 fusion.27
  54.8 0.3 copy.120
  55.0 0.2 copy.119
  55.3 14.9 %all-gather.2 = s32[8,320,8]{1,2,0:T(8,128)S(1)} all-gather(s32[1,320,8]{1,2,0:T(8,128)S(1)} %bitcast.117), channel_id=3, replica_groups=mesh['dp'=4,'expert'=8] {'expert'}, dimensions={0}, use_global_device_ids=true | all-gather | bytes 92160 | tf_op jit(solution)/shard_map/all_gather | solution.py:1117
  70.2 1.5 copy.125.routes_c
  71.7 0.3 multiply_cosine_fusion
  72.2 1.5 copy-done.29
  73.7 1.4 fusion.75
  75.2 0.3 fusion.10
  75.5 1.5 fusion.80
  77.1 1.2 fusion.3
  78.3 1.9 copy-done.1
  80.1 1.6 fusion.14
  81.7 1.0 multiply_reduce_fusion.2
  82.7 1.0 copy-done.2
  84.0 0.3 fusion.38
  84.5 0.6 slice_bitcast_fusion.wr_t
  85.2 201.1 %experts.1 = (bf16[320,1024]{1,0:T(8,128)(2,1)}, f32[320,1024]{1,0:T(8,128)}, f32[8,8,320]{2,1,0:T(8,128)}, f32[4,256,1024]{2,1,0:T(8,128)}, f32[4,128,1024]{2,1,0:T(8,128)}) custom-call(bf16[320,1024]{1,0:T(8,128)(2,1)} %copy-done.6, bf16[8,320,1024]{2,1,0:T(8,128)(2,1)} %bitcast.101, s32[8,8,320]{2,1,0:T(8,128)} %bitcast.106, ...), custom_call_target="tpu_custom_call" | custom-call | tf_op jit(solution)/shard_map/experts/pallas_call | solution.py:899
  286.2 0.9 slice.70
  287.2 2.5 multiply_reduce_fusion
  289.7 0.4 fusion.17
  290.1 1.2 copy-done.20
  291.3 0.9 convolution_convert_fusion.3
  292.2 0.4 copy.126
  292.6 0.6 copy-done.23
  293.2 8.0 %fusion = (f32[8,2,320]{2,1,0:T(2,128)S(1)}, f32[8,320,320,2]{2,1,3,0:T(8,128)}) fusion(f32[8,2,320,320]{2,3,1,0:T(8,128)} %copy-done.1, f32[8,2,320]{2,1,0:T(2,128)S(1)} %bitcast.109, bf16[320,8,64,1]{0,2,3,1:T(8,128)(2,1)S(1)} %bitcast.105, bf16[320,8,2,64]{0,3,2,1:T(8,128)(2,1)S(1)} %bitcast.95), kind=kOutput, calls=%fused_computation.3 | convolution fusion | flops 214625280 | bytes 14131200 | tf_op jit(solution)/shard_map/tkgd,skd->kgts/dot_general | solution.py:1197
  301.3 5.2 %fusion.24 = bf16[8,64,320]{2,1,0:T(8,128)(2,1)} fusion(bf16[320,8,2,64]{0,3,2,1:T(8,128)(2,1)S(1)} %bitcast.96, f32[8,2,320,320]{2,3,1,0:T(8,128)} %copy-done.1, f32[8,2,320]{2,1,0:T(2,128)S(1)} %bitcast.110), kind=kOutput, calls=%fused_computation.50 | convolution fusion | flops 213155840 | bytes 7557120 | tf_op jit(solution)/shard_map/kgts,tkgd->skd/dot_general | solution.py:1194
  306.4 7.3 %fusion.2 = bf16[8,2,320,320]{2,3,1,0:T(8,128)(2,1)S(1)} fusion(f32[8,320,320,2]{2,1,3,0:T(8,128)} %get-tuple-element.109, f32[8,2,320,320]{2,3,1,0:T(8,128)} %copy-done.1, f32[8,2,320]{2,1,0:T(2,128)S(1)} %get-tuple-element.108, f32[8,2,320]{2,1,0:T(2,128)S(1)} %bitcast.111), kind=kLoop, calls=%fused_computation.5 | loop fusion | flops 6553600 | bytes 16424960 | tf_op jit(solution)/shard_map/convert_element_type | solution.py:1202
  313.8 1.2 broadcast_multiply_fusion
  315.0 0.9 bitcast_multiply_fusion.1
  316.1 1.2 convolution_convert_fusion
  317.5 0.3 fusion.11
  317.8 0.8 copy-done.11
  318.6 2.8 convolution_convert_fusion.2
  321.3 1.2 fusion.81
  322.5 0.2 convolution_convert_fusion.4
  322.8 0.4 fusion.30
  323.2 0.5 copy-done.26
  323.7 2.8 convolution_convert_fusion.1
  326.5 2.3 fusion.16
  329.5 10.7 %concatenate.36.g_ref = bf16[1024,3200]{1,0:T(8,128)(2,1)} concatenate(bf16[1024,1024]{1,0:T(8,128)(2,1)} %convolution_convert_fusion.2, bf16[1024,1024]{1,0:T(8,128)(2,1)} %convolution_convert_fusion.1, bf16[1024,1024]{1,0:T(8,128)(2,1)S(1)} %convolution_convert_fusion, bf16[1024,32]{1,0:T(8,128)(2,1)S(1)} %copy.133, bf16[1024,1]{1,0:T(8,128)(2,1)S(1)} %convert_element_type.163, ...), dimensions={1} | concatenate | bytes 13107200 | tf_op jit(solution)/shard_map/concatenate | solution.py:1232
  340.2 75.6 %reduce_grads.1 = f32[256,3200]{1,0:T(8,128)} custom-call(bf16[1024,3200]{1,0:T(8,128)(2,1)} %concatenate.36.g_ref), custom_call_target="tpu_custom_call" | custom-call | tf_op jit(solution)/shard_map/reduce_grads/pallas_call | solution.py:502
  415.8 3.8 fusion.79
  419.5 0.8 slice_reduce_fusion
  420.4 0.7 copy.136
  421.1 3.5 fusion.18
  424.5 2.0 copy.152
  426.5 2.1 copy.153
  428.6 1.0 copy-done.21
  429.6 1.3 copy.154
  (90 shorter events, 2.2 us)
Async XLA Ops:
  7.2 41.2 %copy-start.10 = (bf16[320,1024]{1,0:T(8,128)(2,1)S(1)}, bf16[320,1024]{1,0:T(8,128)(2,1)}, u32[]{:S(2)}) copy-start(bf16[320,1024]{1,0:T(8,128)(2,1)} %param.12) | copy-start | bytes 1966084
  7.2 78.0 %all-gather.5.cloned.1.call-start = ((), (), s32[]{:S(2)}) async-start(), calls=%async_computation | async-start | bytes 5898240 | tf_op jit(solution)/shard_map/all_gather | solution.py:1116
  51.1 1.0 copy-start.18
  51.2 2.0 copy-start
  53.2 2.0 copy-start.27
  55.2 23.0 %copy-start.22 = (bf16[320,512]{0,1:T(8,128)(2,1)}, bf16[320,512]{0,1:T(8,128)(2,1)S(1)}, u32[]{:S(2)}) copy-start(bf16[320,512]{0,1:T(8,128)(2,1)S(1)} %copy.119) | copy-start | bytes 983044
  70.2 1.9 copy-start.24
  72.0 1.7 copy-start.29
  72.2 3.3 copy-start.13
  75.5 1.5 copy-start.8
  77.0 3.1 copy-start.1
  80.1 1.6 copy-start.19
  81.7 1.0 copy-start.15
  82.7 1.1 copy-start.2
  82.7 1.2 copy-start.25
  84.0 1.2 copy-start.6
  287.2 2.5 copy-start.3
  287.2 2.5 copy-start.17
  289.7 1.6 copy-start.20
  291.3 24.6 %copy-start.5 = (f32[320,1024]{1,0:T(8,128)}, f32[320,1024]{1,0:T(8,128)S(1)}, u32[]{:S(2)}) copy-start(f32[320,1024]{1,0:T(8,128)S(1)} %fusion.17) | copy-start | bytes 3932164
  292.2 1.0 copy-start.23
  306.4 7.3 %copy-start.9 = (bf16[320,8,2,64]{0,3,2,1:T(8,128)(2,1)S(1)}, bf16[320,8,2,64]{0,3,2,1:T(8,128)(2,1)}, u32[]{:S(2)}) copy-start(bf16[320,8,2,64]{0,3,2,1:T(8,128)(2,1)} %copy-done.8) | copy-start | bytes 1966084
  313.7 1.2 copy-start.14
  314.9 1.1 copy-start.16
  317.5 1.1 copy-start.11
  318.6 2.8 copy-start.30
  321.3 1.2 copy-start.7
  322.7 1.0 copy-start.26
  323.7 2.8 copy-start.28
  415.7 3.8 copy-start.4
  415.7 4.6 %slice-start = ((f32[256,3200]{1,0:T(8,128)}), f32[256,32]{1,0:T(8,128)S(1)}, s32[]{:S(2)}) async-start(f32[256,3200]{1,0:T(8,128)} %reduce_grads.1), calls=%async_computation.1 | async-start | bytes 262144 | tf_op jit(solution)/shard_map/slice | solution.py:1254
  421.1 5.4 %copy-start.12 = (f32[4,256,1024]{2,1,0:T(8,128)S(1)}, f32[4,256,1024]{2,1,0:T(8,128)}, u32[]{:S(2)}) copy-start(f32[4,256,1024]{2,1,0:T(8,128)} %get-tuple-element.135) | copy-start | bytes 12582916
  426.5 3.1 copy-start.21
Sparse Core Ops, SparseCore 0:
  9.7 59.3 all-gather.4

commit v5 on v4

--- a/solution.py
+++ b/solution.py
@@ -63,96 +63,6 @@
     return [bits[p:] + bits[:p] for p in range(len(bits))] or [[]]
 
 
-def weights_body(n_dp, *refs):
-    arrays = 4
-    ins, outs = refs[:arrays], refs[arrays : 2 * arrays]
-    send_sem, recv_sem, pair_send, pair_recv, own_sem = refs[2 * arrays :]
-    me, mine = lax.axis_index("dp"), lax.axis_index("expert")
-    core = lax.rem(mine, 2)
-    pair = mine + 1 - 2 * core
-    orders = bit_orders(n_dp)
-    greet([(None, {"dp": me ^ bit}) for bit in orders[0]] + [(None, {"expert": pair})])
-    shard = ins[0].shape[0]
-    half = shard // 2
-    sends, pairs, owns = [], [], []
-    cuts = min(2, len(orders), half // 16)
-    size = half // cuts
-
-    def pieces(a):
-        return cuts
-
-    def rows(start, side, p):
-        return pl.ds(pl.multiple_of(start + side * half + p * size, 16), size)
-
-    def push(a, p, r, bit):
-        to = me ^ bit
-        there = outs[a].at[rows((me ^ r) * shard, core, p)]
-        src = ins[a].at[rows(0, core, p)] if r == 0 else there
-        copy = remote(src, there, send_sem.at[a, p, r, bit.bit_length() - 1], recv_sem.at[a, p, r ^ bit], dp=to)
-        copy.start()
-        sends.append(copy)
-
-    for a in range(arrays):
-        for p in range(pieces(a)):
-            for bit in orders[p]:
-                push(a, p, 0, bit)
-    for a in range(arrays):
-        copy = pltpu.make_async_copy(
-            ins[a], outs[a].at[pl.ds(pl.multiple_of(me * shard, 16), shard)], own_sem.at[a])
-        copy.start()
-        owns.append(copy)
-    def reach(order):
-        blocks = [0]
-        steps = []
-        for j, bit in enumerate(order):
-            new = [r | bit for r in blocks]
-            steps.append((j, new))
-            blocks = blocks + new
-        return steps
-
-    for j in range(len(orders[0])):
-        for a in range(arrays):
-            for p in range(pieces(a)):
-                order = orders[p]
-                for r in reach(order)[j][1]:
-                    here = outs[a].at[rows((me ^ r) * shard, core, p)]
-                    remote(here, here, send_sem.at[a, p, r, 0], recv_sem.at[a, p, r], dp=me).wait_recv()
-                    for bit in order[j + 1 :]:
-                        push(a, p, r, bit)
-                    copy = remote(here, here, pair_send.at[a, p, r], pair_recv.at[a, p, r], expert=pair)
-                    copy.start()
-                    pairs.append((copy, a, p, r))
-    for copy in owns:
-        copy.wait()
-    for copy in sends:
-        copy.wait_send()
-    for copy, a, p, r in pairs:
-        copy.wait_send()
-        here = outs[a].at[rows((me ^ r) * shard, 1 - core, p)]
-        remote(here, here, pair_send.at[a, p, r], pair_recv.at[a, p, r], expert=pair).wait_recv()
-
-
-def gather_weights(n_dp, arrays, collective_id):
-    orders = bit_orders(n_dp)
-    count, pieces = len(arrays), min(2, len(orders))
-    out_shape = [jax.ShapeDtypeStruct((n_dp * a.shape[0], a.shape[1]), a.dtype) for a in arrays]
-    return pl.pallas_call(
-        functools.partial(weights_body, n_dp),
-        out_shape=out_shape,
-        in_specs=[pl.BlockSpec(memory_space=VMEM)] * count,
-        out_specs=[pl.BlockSpec(memory_space=ANY)] * count,
-        scratch_shapes=[
-            pltpu.SemaphoreType.DMA((count, pieces, n_dp, max(1, n_dp.bit_length() - 1))),
-            pltpu.SemaphoreType.DMA((count, pieces, n_dp)),
-            pltpu.SemaphoreType.DMA((count, pieces, n_dp)),
-            pltpu.SemaphoreType.DMA((count, pieces, n_dp)),
-            pltpu.SemaphoreType.DMA((count,)),
-        ],
-        compiler_params=pltpu.CompilerParams(collective_id=collective_id, has_side_effects=True),
-        name="gather_weights",
-    )(*arrays)
-
-
 class Ring:
     def __init__(self, n_exp):
         self.mine = lax.axis_index("expert")
@@ -349,175 +259,6 @@
     return (lambda d: pair_buf.at[d], lambda d: held.at[d], lambda side, d: got.at[side, d])
 
 
-def grads_body(n_dp, n_exp, chunks, g_ref, out_ref, pair_buf, total, dp_buf, prefix, suffix, go_r, go_l, final, other,
-               pair_send, pair_recv, dp_send, dp_recv, send_r, send_l, recv_r, recv_l, last_send, last_recv):
-    me, mine = lax.axis_index("dp"), lax.axis_index("expert")
-    core = lax.rem(mine, 2)
-    z = lax.div(mine, 2)
-    depth = n_exp // 2
-    pair = mine + 1 - 2 * core
-    has_left, has_right = z > 0, z < depth - 1
-    orders = bit_orders(n_dp)
-    rows = g_ref.shape[0] // n_dp
-    half = rows // 2
-    width = g_ref.shape[1] // chunks
-    greet([(None, {"expert": pair})] + [(None, {"dp": me ^ bit}) for bit in orders[0]]
-          + [(has_left, {"expert": mine - 2}), (has_right, {"expert": mine + 2})])
-
-    def columns(i):
-        return pl.ds(pl.multiple_of(i * width, 128), width)
-
-    def block_of(d, side, i):
-        return g_ref.at[pl.ds(pl.multiple_of(d * rows + side * half, 16), half), columns(i)]
-
-    def across(i, d):
-        return remote(block_of(d, 1 - core, i), pair_buf.at[i, d], pair_send.at[i, d], pair_recv.at[i, d], expert=pair)
-
-    for i in range(chunks):
-        for d in range(n_dp):
-            across(i, d).start()
-
-    def moved(i, j):
-        order = orders[i % len(orders)]
-        blocks = [0]
-        for bit in order[j + 1 :]:
-            blocks = blocks + [r | bit for r in blocks]
-        return order[j], [r | order[j] for r in blocks]
-
-    def dp_copy(i, j, r, bit):
-        return remote(total.at[i, r], dp_buf.at[i, r ^ bit, j], dp_send.at[i, r], dp_recv.at[i, r ^ bit, j], dp=me ^ bit)
-
-    stages = len(orders[0])
-    for i in range(chunks):
-        for r in range(n_dp - 1, -1, -1):
-            d = me ^ r
-            across(i, d).wait_recv()
-            add_rows(total.at[i, r], block_of(d, core, i), pair_buf.at[i, d])
-        if stages:
-            bit, blocks = moved(i, 0)
-            for r in blocks:
-                dp_copy(i, 0, r, bit).start()
-    for j in range(stages):
-        for i in range(chunks):
-            bit, blocks = moved(i, j)
-            for r in blocks:
-                kept = r ^ bit
-                dp_copy(i, j, r, bit).wait_recv()
-                add_rows(total.at[i, kept], total.at[i, kept], dp_buf.at[i, kept, j])
-            if j + 1 < stages:
-                bit, blocks = moved(i, j + 1)
-                for r in blocks:
-                    dp_copy(i, j + 1, r, bit).start()
-
-    def right(i):
-        return remote(go_r.at[i], prefix.at[i], send_r.at[i], recv_r.at[i], expert=mine + 2)
-
-    def left(i):
-        return remote(go_l.at[i], suffix.at[i], send_l.at[i], recv_l.at[i], expert=mine - 2)
-
-    def line(t, carry):
-        i = t - z
-
-        @pl.when(jnp.logical_and(i >= 0, i < chunks))
-        def _():
-            @pl.when(has_left)
-            def _():
-                remote(go_r.at[i], prefix.at[i], send_r.at[i], recv_r.at[i], expert=mine).wait_recv()
-
-            @pl.when(jnp.logical_and(has_left, has_right))
-            def _():
-                add_rows(go_r.at[i], total.at[i, 0], prefix.at[i])
-
-            @pl.when(jnp.logical_not(has_left))
-            def _():
-                add_rows(go_r.at[i], total.at[i, 0])
-
-            pl.when(has_right)(lambda: right(i).start())
-
-        k = t - (depth - 1 - z)
-
-        @pl.when(jnp.logical_and(k >= 0, k < chunks))
-        def _():
-            @pl.when(has_right)
-            def _():
-                remote(go_l.at[k], suffix.at[k], send_l.at[k], recv_l.at[k], expert=mine).wait_recv()
-
-            @pl.when(jnp.logical_and(has_left, has_right))
-            def _():
-                add_rows(go_l.at[k], total.at[k, 0], suffix.at[k])
-
-            @pl.when(jnp.logical_not(has_right))
-            def _():
-                add_rows(go_l.at[k], total.at[k, 0])
-
-            pl.when(has_left)(lambda: left(k).start())
-
-        return carry
-
-    lax.fori_loop(0, chunks + depth - 1, line, 0)
-
-    def last(i):
-        return remote(final.at[i], other.at[i], last_send.at[i], last_recv.at[i], expert=pair)
-
-    for i in range(chunks):
-        @pl.when(jnp.logical_and(has_left, has_right))
-        def _():
-            add_rows(final.at[i], total.at[i, 0], prefix.at[i], suffix.at[i])
-
-        @pl.when(jnp.logical_not(has_left))
-        def _():
-            add_rows(final.at[i], total.at[i, 0], suffix.at[i])
-
-        @pl.when(jnp.logical_not(has_right))
-        def _():
-            add_rows(final.at[i], total.at[i, 0], prefix.at[i])
-
-        last(i).start()
-
-    def place(side, i):
-        return out_ref.at[pl.ds(pl.multiple_of(side * half, 16), half), columns(i)]
-
-    for i in range(chunks):
-        add_rows(place(core, i), final.at[i])
-    for i in range(chunks):
-        last(i).wait_recv()
-        add_rows(place(1 - core, i), other.at[i])
-        last(i).wait_send()
-        pl.when(has_right)(lambda: right(i).wait_send())
-        pl.when(has_left)(lambda: left(i).wait_send())
-        for d in range(n_dp):
-            across(i, d).wait_send()
-        for j in range(stages):
-            bit, blocks = moved(i, j)
-            for r in blocks:
-                dp_copy(i, j, r, bit).wait_send()
-
-
-def reduce_grads(n_dp, n_exp, grads, chunks, collective_id):
-    rows = grads.shape[0] // n_dp
-    half, width = rows // 2, grads.shape[1] // chunks
-    stages = max(1, n_dp.bit_length() - 1)
-    sem = pltpu.SemaphoreType.DMA
-    one = pltpu.VMEM((chunks, half, width), grads.dtype)
-    return pl.pallas_call(
-        functools.partial(grads_body, n_dp, n_exp, chunks),
-        out_shape=jax.ShapeDtypeStruct((rows, grads.shape[1]), jnp.float32),
-        in_specs=[pl.BlockSpec(memory_space=VMEM)],
-        out_specs=pl.BlockSpec(memory_space=VMEM),
-        scratch_shapes=[
-            pltpu.VMEM((chunks, n_dp, half, width), grads.dtype),
-            pltpu.VMEM((chunks, n_dp, half, width), grads.dtype),
-            pltpu.VMEM((chunks, n_dp, stages, half, width), grads.dtype),
-            one, one, one, one, one, one,
-            sem((chunks, n_dp)), sem((chunks, n_dp)), sem((chunks, n_dp)), sem((chunks, n_dp, stages)),
-            sem((chunks,)), sem((chunks,)), sem((chunks,)), sem((chunks,)), sem((chunks,)), sem((chunks,)),
-        ],
-        compiler_params=pltpu.CompilerParams(
-            collective_id=collective_id, has_side_effects=True, vmem_limit_bytes=56 * MIB),
-        name="reduce_grads",
-    )(grads)
-
-
 SLOTS = 128
 F32, LOW = jnp.float32, jnp.bfloat16
 
@@ -526,7 +267,7 @@
     return lax.dot_general(a, b, (((over_a,), (over_b,)), ((), ())), preferred_element_type=F32)
 
 
-def experts_body(n_dp, n_exp, hid_ref, gy_hbm, routes_t, routes_c, wr_t, w_in_hbm, w_out_hbm, middle,
+def experts_body(n_dp, n_exp, hid_ref, gy_hbm, routes_t, wr_t, w_in_hbm, w_out_hbm, middle,
                  block_out, hid_sum, gates_out, in_share, out_share,
                  x_all, w_in, w_out, sent, grows, gu, tmp, acts, stage, slots, gates, dots, wide,
                  pair_buf, held, got, *sems):
@@ -580,14 +321,9 @@
             [jnp.where(slot_ids == slots[j, i : i + 1, :], 1.0, 0.0).astype(LOW) for i in range(local)], axis=0)
 
     def places_t(j):
-        names = routes_c[j]
         lane = lax.broadcasted_iota(jnp.int32, (tree, 128), 1)
-        chosen = jnp.zeros((tree, 128), F32)
-        for k in range(names.shape[1]):
-            chosen = jnp.maximum(chosen, jnp.where(names[:, k : k + 1] == first + lane, 1.0, 0.0))
-        chosen = jnp.where(lane < local, chosen, 0.0)
-        above = (lax.broadcasted_iota(jnp.int32, (tree, tree), 1) < lax.broadcasted_iota(jnp.int32, (tree, tree), 0)).astype(LOW)
-        slot = jnp.where(chosen > 0.5, dot(above, chosen.astype(LOW)), -1.0)
+        pick = jnp.where(lax.broadcasted_iota(jnp.int32, (16, 128), 0) == lax.broadcasted_iota(jnp.int32, (16, 128), 1), 1.0, 0.0)
+        slot = dot(jnp.concatenate([slots[j], jnp.zeros((8, tree), F32)], axis=0).astype(LOW), pick.astype(LOW), 0, 0)
         lanes = lane.astype(F32)
         return jnp.concatenate(
             [jnp.where(lanes == slot[:, i : i + 1], 1.0, 0.0).astype(LOW) for i in range(local)], axis=1)
@@ -905,7 +641,7 @@
             shape((local, width // n_dp, width), F32),
             shape((local, units // n_dp, width), F32),
         ],
-        in_specs=[pl.BlockSpec(memory_space=s) for s in (VMEM, ANY, VMEM, VMEM, VMEM, ANY, ANY, ANY)],
+        in_specs=[pl.BlockSpec(memory_space=s) for s in (VMEM, ANY, VMEM, VMEM, ANY, ANY, ANY)],
         out_specs=[pl.BlockSpec(memory_space=s) for s in (VMEM, ANY, VMEM, ANY, ANY)],
         scratch_shapes=[
             pltpu.VMEM((n_exp, tree, width), LOW),
@@ -929,7 +665,643 @@
         compiler_params=pltpu.CompilerParams(
             collective_id=collective_id, has_side_effects=True, vmem_limit_bytes=63 * MIB),
         name="experts",
-    )(hidden2, grad_y, routes_all.transpose(0, 2, 1), routes_all, router.T, expert_in, expert_out, middle)
+    )(hidden2, grad_y, routes_all, router.T, expert_in, expert_out, middle)
+
+
+def lanes_of(shape):
+    return lax.broadcasted_iota(jnp.int32, shape, 1)
+
+
+def turned(field):
+    low_half = lax.rem(lanes_of(field.shape), HD) < HD // 2
+    return jnp.where(low_half, -pltpu.roll(field, 128 - HD // 2, 1), pltpu.roll(field, HD // 2, 1))
+
+
+def mask_bias(parents, tree):
+    unit = tree // 20
+
+    def segment(row):
+        return jnp.where(row < 8 * unit, 0, jnp.where(row < 12 * unit, 1 + lax.div(row - 8 * unit, unit), 5 + lax.div(row - 12 * unit, unit)))
+
+    count = parents.shape[1]
+    names = parents[...].astype(F32)
+    wide = (tree, count)
+    seg = segment(lax.broadcasted_iota(jnp.int32, wide, 0)).astype(F32)
+    lane = lanes_of(wide).astype(F32)
+    own = seg[:, :1]
+    parent = jnp.sum(jnp.where(lane == seg, names, 0.0), axis=1, keepdims=True)
+    grand = jnp.sum(jnp.where(lane == parent, names, 0.0), axis=1, keepdims=True)
+    square = (tree, tree)
+    row, col = lax.broadcasted_iota(jnp.int32, square, 0), lanes_of(square)
+    there = segment(col).astype(F32)
+    hit = jnp.maximum(
+        jnp.maximum(jnp.where(there == own, 1.0, 0.0), jnp.where(there == parent, 1.0, 0.0)), jnp.where(there == grand, 1.0, 0.0))
+    hit = jnp.where(col <= row, hit, 0.0)
+    return jnp.where(hit > 0.5, 0.0, -1e30)
+
+
+def inverse_rms(field):
+    return lax.rsqrt(jnp.mean(field * field, axis=-1, keepdims=True) + EPSILON)
+
+
+class DpGather:
+    def __init__(self, n_dp, mine, me, ins, outs, sems):
+        self.n_dp, self.me, self.ins, self.outs = n_dp, me, ins, outs
+        self.send, self.recv, self.pair_send, self.pair_recv, self.own_sem = sems
+        self.core = lax.rem(mine, 2)
+        self.pair = mine + 1 - 2 * self.core
+        self.shard = ins[0].shape[0]
+        half = self.shard // 2
+        self.orders = bit_orders(n_dp)
+        self.cuts = min(2, len(self.orders), half // 16)
+        self.size = half // self.cuts
+
+    @staticmethod
+    def scratch(count, n_dp):
+        sem = pltpu.SemaphoreType.DMA
+        bits = max(1, n_dp.bit_length() - 1)
+        return [sem((count, 2, n_dp, bits)), sem((count, 2, n_dp)), sem((count, 2, n_dp)), sem((count, 2, n_dp)), sem((count,))]
+
+    def rows(self, start, side, p):
+        return pl.ds(pl.multiple_of(start + side * (self.shard // 2) + p * self.size, 16), self.size)
+
+    def hop(self, a, p, r, bit):
+        there = self.outs[a].at[self.rows((self.me ^ r) * self.shard, self.core, p)]
+        src = self.ins[a].at[self.rows(0, self.core, p)] if r == 0 else there
+        return remote(src, there, self.send.at[a, p, r, bit.bit_length() - 1], self.recv.at[a, p, r ^ bit], dp=self.me ^ bit)
+
+    def own(self, a):
+        at = pl.ds(pl.multiple_of(self.me * self.shard, 16), self.shard)
+        return pltpu.make_async_copy(self.ins[a], self.outs[a].at[at], self.own_sem.at[a])
+
+    def across(self, a, p, r, side):
+        here = self.outs[a].at[self.rows((self.me ^ r) * self.shard, side, p)]
+        return remote(here, here, self.pair_send.at[a, p, r], self.pair_recv.at[a, p, r], expert=self.pair)
+
+    def start(self, a):
+        for p in range(self.cuts):
+            for bit in self.orders[p]:
+                self.hop(a, p, 0, bit).start()
+        self.own(a).start()
+
+    def stage(self, p, j):
+        order = self.orders[p]
+        blocks = [0]
+        for bit in order[:j]:
+            blocks = blocks + [r | bit for r in blocks]
+        return [r | order[j] for r in blocks], order[j + 1 :]
+
+    def turn(self, a, j):
+        for p in range(self.cuts):
+            blocks, onward = self.stage(p, j)
+            for r in blocks:
+                here = self.outs[a].at[self.rows((self.me ^ r) * self.shard, self.core, p)]
+                remote(here, here, self.send.at[a, p, r, 0], self.recv.at[a, p, r], dp=self.me).wait_recv()
+                for bit in onward:
+                    self.hop(a, p, r, bit).start()
+                self.across(a, p, r, self.core).start()
+
+    def ready(self, a):
+        self.own(a).wait()
+        for p in range(self.cuts):
+            for r in range(1, self.n_dp):
+                self.across(a, p, r, 1 - self.core).wait_recv()
+
+    def finish(self, a):
+        for p in range(self.cuts):
+            for bit in self.orders[p]:
+                self.hop(a, p, 0, bit).wait_send()
+            for j in range(len(self.orders[p])):
+                blocks, onward = self.stage(p, j)
+                for r in blocks:
+                    for bit in onward:
+                        self.hop(a, p, r, bit).wait_send()
+                    self.across(a, p, r, self.core).wait_send()
+
+
+def front_body(n_dp, n_exp, x_ref, gain1, gain2, router, w_query, w_keyval, w_output, routes_t, parents, cosine, sine,
+               hidden, queries, keys, values, attended, middle, hidden2, log_total,
+               query_full, keyval_full, output_full, router_full, gains, routes_all,
+               router_pad, gain_pad, bias, *sems):
+    gather_sems, (gain_send, gain_recv, route_send, route_recv) = sems[:5], sems[5:9]
+    me, mine = lax.axis_index("dp"), lax.axis_index("expert")
+    peers = [lax.rem(mine + k, n_exp) for k in range(1, n_exp)]
+    greet([(None, {"expert": e}) for e in peers] + [(None, {"dp": me ^ k}) for k in range(1, n_dp)])
+    tree, width = x_ref.shape
+    shard = w_query.shape[0]
+
+    router_pad[...] = jnp.zeros(router_pad.shape, LOW)
+    router_pad[:, pl.ds(0, EXPERTS)] = router[...]
+    sub = lax.broadcasted_iota(jnp.int32, (16, shard), 0)
+    gain_pad[...] = jnp.where(sub == 0, gain1[...].astype(F32), jnp.where(sub == 1, gain2[...].astype(F32), 0.0)).astype(LOW)
+
+    gather = DpGather(n_dp, mine, me, (w_query, w_keyval, w_output, router_pad),
+                      (query_full, keyval_full, output_full, router_full), gather_sems)
+
+    def gain_copy(k):
+        return remote(gain_pad, gains.at[me], gain_send.at[k], gain_recv.at[k], dp=me ^ k)
+
+    def route_copy(k, e):
+        return remote(routes_t, routes_all.at[mine], route_send.at[k], route_recv.at[k], expert=e)
+
+    for k in range(1, n_dp):
+        gain_copy(k).start()
+    for a in range(4):
+        gather.start(a)
+    for k, e in enumerate(peers):
+        route_copy(k, e).start()
+    gains[me] = gain_pad[...]
+    routes_all[mine] = routes_t[...]
+    bias[...] = mask_bias(parents, tree)
+    log_total[...] = jnp.zeros(log_total.shape, F32)
+    for k in range(1, n_dp):
+        remote(gain_pad, gains.at[me ^ k], gain_send.at[k], gain_recv.at[k], dp=me).wait_recv()
+
+    def gain_row(i):
+        return jnp.concatenate([gains[d].astype(F32)[i : i + 1] for d in range(n_dp)], axis=1)
+
+    x = x_ref[...].astype(F32)
+    hidden[...] = (x * inverse_rms(x) * gain_row(0)).astype(LOW)
+    stages = len(gather.orders[0])
+    for j in range(stages):
+        for a in range(4 if j + 1 < stages else 2):
+            gather.turn(a, j)
+    gather.ready(0)
+    gather.ready(1)
+
+    def rotate(field):
+        return field * cosine[...] + turned(field) * sine[...]
+
+    left = lanes_of((tree, 128)) < HD
+    tile = 512
+
+    def query_tile(n, carry):
+        cols = pl.ds(pl.multiple_of(n * tile, tile), tile)
+        pre = dot(hidden[...], query_full[:, cols])
+        for i in range(tile // 128):
+            at = pl.multiple_of(n * tile + i * 128, 128)
+            queries[:, pl.ds(at, 128)] = rotate(pre[:, i * 128 : (i + 1) * 128]).astype(LOW)
+        return carry
+
+    lax.fori_loop(0, width // tile, query_tile, 0)
+
+    def spread(field, out, i):
+        other = pltpu.roll(field, HD, 1)
+        out[2 * i] = jnp.where(left, field, other).astype(LOW)
+        out[2 * i + 1] = jnp.where(left, other, field).astype(LOW)
+
+    half = KV * HD
+    pre = dot(hidden[...], keyval_full[:, pl.ds(0, half)])
+    for i in range(half // 128):
+        spread(rotate(pre[:, i * 128 : (i + 1) * 128]), keys, i)
+    pre = dot(hidden[...], keyval_full[:, pl.ds(half, half)])
+    for i in range(half // 128):
+        spread(pre[:, i * 128 : (i + 1) * 128], values, i)
+    for a in range(2, 4):
+        gather.turn(a, stages - 1)
+
+    def heads(c, carry):
+        cols = pl.ds(pl.multiple_of(c * 128, 128), 128)
+        pair = queries[:, cols]
+        made = []
+        for h in range(2):
+            mine_lanes = left if h == 0 else jnp.logical_not(left)
+            query = jnp.where(mine_lanes, pair, jnp.zeros_like(pair))
+            scores = dot(query, keys[c], 1, 1) * HD**-0.5 + bias[...]
+            top = jnp.max(scores, axis=1, keepdims=True)
+            powers = jnp.exp(scores - top)
+            total = jnp.sum(powers, axis=1, keepdims=True)
+            made.append(dot((powers / total).astype(LOW), values[c]))
+            log_total[...] = jnp.where(lanes_of((tree, 128)) == 2 * c + h, top + jnp.log(total), log_total[...])
+        attended[:, cols] = jnp.where(left, made[0], made[1]).astype(LOW)
+        return carry
+
+    lax.fori_loop(0, KV, heads, 0)
+    gather.ready(2)
+    gather.ready(3)
+
+    def middle_tile(n, carry):
+        cols = pl.ds(pl.multiple_of(n * tile, tile), tile)
+        middle[:, cols] = x_ref[:, cols].astype(F32) + dot(attended[...], output_full[:, cols])
+        return carry
+
+    lax.fori_loop(0, width // tile, middle_tile, 0)
+    field = middle[...]
+    hidden2[...] = (field * inverse_rms(field) * gain_row(1)).astype(LOW)
+    for a in range(4):
+        gather.finish(a)
+    for k in range(1, n_dp):
+        gain_copy(k).wait_send()
+    for k, e in enumerate(peers):
+        route_copy(k, e).wait_send()
+        source = lax.rem(mine + n_exp - 1 - k, n_exp)
+        remote(routes_t, routes_all.at[source], route_send.at[k], route_recv.at[k], expert=mine).wait_recv()
+
+
+def front(n_dp, n_exp, tokens, gain1, gain2, router, w_query, w_keyval, w_output, routes_t, parents, tables, collective_id):
+    tree, width = tokens.shape
+    shard = w_query.shape[0]
+    shape, sem = jax.ShapeDtypeStruct, pltpu.SemaphoreType.DMA
+    low = shape((tree, width), LOW)
+    spread = shape((KV, tree, 128), LOW)
+    full = shape((n_dp * shard, width), LOW)
+    return pl.pallas_call(
+        functools.partial(front_body, n_dp, n_exp),
+        out_shape=[
+            low, low, spread, spread, low, shape((tree, width), F32), low, shape((tree, 128), F32),
+            full, full, full, shape((n_dp * shard, 128), LOW), shape((n_dp, 16, shard), LOW),
+            shape((n_exp,) + routes_t.shape, jnp.int32),
+        ],
+        in_specs=[pl.BlockSpec(memory_space=VMEM)] * 11,
+        out_specs=[pl.BlockSpec(memory_space=VMEM)] * 14,
+        scratch_shapes=[
+            pltpu.VMEM((shard, 128), LOW), pltpu.VMEM((16, shard), LOW), pltpu.VMEM((tree, tree), F32),
+            *DpGather.scratch(4, n_dp), sem((n_dp,)), sem((n_dp,)), sem((n_exp - 1,)), sem((n_exp - 1,)),
+        ],
+        compiler_params=pltpu.CompilerParams(
+            collective_id=collective_id, has_side_effects=True, vmem_limit_bytes=56 * MIB),
+        name="front",
+    )(tokens, gain1[None], gain2[None], router, w_query, w_keyval, w_output, routes_t, parents, *tables)
+
+
+class GradSum:
+    def __init__(self, n_dp, n_exp, chunks, own, bufs, sems):
+        self.n_dp, self.chunks, self.own = n_dp, chunks, own
+        (self.pair_in, self.total, self.dp_in, self.prefix, self.suffix, self.go_r, self.go_l, self.final, self.other) = bufs
+        (self.pair_send, self.pair_recv, self.dp_send, self.dp_recv,
+         self.send_r, self.send_l, self.recv_r, self.recv_l, self.last_send, self.last_recv) = sems
+        self.me, self.mine = lax.axis_index("dp"), lax.axis_index("expert")
+        self.core = lax.rem(self.mine, 2)
+        self.z = lax.div(self.mine, 2)
+        self.depth = n_exp // 2
+        self.pair = self.mine + 1 - 2 * self.core
+        self.has_left, self.has_right = self.z > 0, self.z < self.depth - 1
+        self.orders = bit_orders(n_dp)
+
+    @staticmethod
+    def scratch(n_dp, chunks, half, columns):
+        sem = pltpu.SemaphoreType.DMA
+        stages = max(1, n_dp.bit_length() - 1)
+        one = pltpu.VMEM((chunks, half, columns), LOW)
+        many = pltpu.VMEM((chunks, n_dp, half, columns), LOW)
+        bufs = [many, many, many, one, one, one, one, one, one]
+        sems = [sem((chunks, n_dp)), sem((chunks, n_dp)), sem((chunks, n_dp)), sem((chunks, n_dp))]
+        return bufs, sems + [sem((chunks,))] * 6
+
+    def partners(self):
+        return ([(None, {"expert": self.pair})] + [(None, {"dp": self.me ^ bit}) for bit in self.orders[0]]
+                + [(self.has_left, {"expert": self.mine - 2}), (self.has_right, {"expert": self.mine + 2})])
+
+    def across(self, i, d):
+        return remote(self.own.at[i, d, 1 - self.core], self.pair_in.at[i, d], self.pair_send.at[i, d],
+                      self.pair_recv.at[i, d], expert=self.pair)
+
+    def moved(self, i, j):
+        order = self.orders[i % len(self.orders)]
+        blocks = [0]
+        for bit in order[j + 1 :]:
+            blocks = blocks + [r | bit for r in blocks]
+        return order[j], [r | order[j] for r in blocks]
+
+    def dp_copy(self, i, r, bit):
+        return remote(self.total.at[i, r], self.dp_in.at[i, r], self.dp_send.at[i, r], self.dp_recv.at[i, r], dp=self.me ^ bit)
+
+    def start(self, i):
+        for d in range(self.n_dp):
+            self.across(i, d).start()
+
+    def paired(self, i):
+        for r in range(self.n_dp - 1, -1, -1):
+            d = self.me ^ r
+            self.across(i, d).wait_recv()
+            add_rows(self.total.at[i, r], self.own.at[i, d, self.core], self.pair_in.at[i, d])
+        self.leave(i, 0)
+
+    def leave(self, i, j):
+        if j < len(self.orders[0]):
+            bit, blocks = self.moved(i, j)
+            for r in blocks:
+                self.dp_copy(i, r, bit).start()
+
+    def met(self, i, j):
+        bit, blocks = self.moved(i, j)
+        for r in blocks:
+            self.dp_copy(i, r, bit).wait_recv()
+            add_rows(self.total.at[i, r ^ bit], self.total.at[i, r ^ bit], self.dp_in.at[i, r])
+        self.leave(i, j + 1)
+
+    def right(self, i):
+        return remote(self.go_r.at[i], self.prefix.at[i], self.send_r.at[i], self.recv_r.at[i], expert=self.mine + 2)
+
+    def left(self, i):
+        return remote(self.go_l.at[i], self.suffix.at[i], self.send_l.at[i], self.recv_l.at[i], expert=self.mine - 2)
+
+    def line(self, t):
+        i = t - self.z
+        has_left, has_right = self.has_left, self.has_right
+
+        @pl.when(jnp.logical_and(i >= 0, i < self.chunks))
+        def _():
+            @pl.when(has_left)
+            def _():
+                remote(self.go_r.at[i], self.prefix.at[i], self.send_r.at[i], self.recv_r.at[i], expert=self.mine).wait_recv()
+
+            @pl.when(jnp.logical_and(has_left, has_right))
+            def _():
+                add_rows(self.go_r.at[i], self.total.at[i, 0], self.prefix.at[i])
+
+            @pl.when(jnp.logical_not(has_left))
+            def _():
+                add_rows(self.go_r.at[i], self.total.at[i, 0])
+
+            pl.when(has_right)(lambda: self.right(i).start())
+
+        k = t - (self.depth - 1 - self.z)
+
+        @pl.when(jnp.logical_and(k >= 0, k < self.chunks))
+        def _():
+            @pl.when(has_right)
+            def _():
+                remote(self.go_l.at[k], self.suffix.at[k], self.send_l.at[k], self.recv_l.at[k], expert=self.mine).wait_recv()
+
+            @pl.when(jnp.logical_and(has_left, has_right))
+            def _():
+                add_rows(self.go_l.at[k], self.total.at[k, 0], self.suffix.at[k])
+
+            @pl.when(jnp.logical_not(has_right))
+            def _():
+                add_rows(self.go_l.at[k], self.total.at[k, 0])
+
+            pl.when(has_left)(lambda: self.left(k).start())
+
+    def last(self, i):
+        return remote(self.final.at[i], self.other.at[i], self.last_send.at[i], self.last_recv.at[i], expert=self.pair)
+
+    def close(self, i):
+        has_left, has_right = self.has_left, self.has_right
+
+        @pl.when(jnp.logical_and(has_left, has_right))
+        def _():
+            add_rows(self.final.at[i], self.total.at[i, 0], self.prefix.at[i], self.suffix.at[i])
+
+        @pl.when(jnp.logical_not(has_left))
+        def _():
+            add_rows(self.final.at[i], self.total.at[i, 0], self.suffix.at[i])
+
+        @pl.when(jnp.logical_not(has_right))
+        def _():
+            add_rows(self.final.at[i], self.total.at[i, 0], self.prefix.at[i])
+
+        self.last(i).start()
+
+    def finish(self, i):
+        self.last(i).wait_send()
+        pl.when(self.has_right)(lambda: self.right(i).wait_send())
+        pl.when(self.has_left)(lambda: self.left(i).wait_send())
+        for d in range(self.n_dp):
+            self.across(i, d).wait_send()
+        for j in range(len(self.orders[0])):
+            bit, blocks = self.moved(i, j)
+            for r in blocks:
+                self.dp_copy(i, r, bit).wait_send()
+
+
+def two_parts(field):
+    high = field.astype(LOW)
+    return high, (field - high.astype(F32)).astype(LOW)
+
+
+def norm_back(field, gain, grad):
+    r = inverse_rms(field)
+    scaled = grad * gain
+    back = r * scaled - field * (r * r * r) * jnp.mean(field * scaled, axis=-1, keepdims=True)
+    return back, jnp.sum(field * r * grad, axis=0, keepdims=True)
+
+
+def back_body(n_dp, n_exp, local, x_ref, cot, hid_sum, gates_in, routes, parents, cosine, sine,
+              hidden, queries, keys, values, attended, middle, hidden2, log_total,
+              query_full, keyval_full, output_full, router_full, gains,
+              input_grad, grad_q, grad_kv, grad_o, grad_s,
+              bias, branch, grad_att, grad_q_pre, grad_kv_pre, rhs, own, own_s, *rest):
+    big = GradSum(n_dp, n_exp, own.shape[0], own, rest[:9], rest[9:19])
+    little = GradSum(n_dp, n_exp, 1, own_s, rest[19:28], rest[28:38])
+    tree, width = x_ref.shape
+    greet(big.partners())
+    shard = width // n_dp
+    side = shard // 2
+    tile = 512
+    lane = lanes_of((tree, 128))
+    left = lane < HD
+
+    def gain_row(i):
+        return jnp.concatenate([gains[d].astype(F32)[i : i + 1] for d in range(n_dp)], axis=1)
+
+    bias[...] = mask_bias(parents, tree)
+
+    chosen = jnp.zeros((tree, 128), F32)
+    for k in range(routes.shape[1]):
+        chosen = jnp.maximum(chosen, jnp.where(routes[:, k : k + 1] == lane, 1.0, 0.0))
+    logits = jnp.where(chosen > 0.5, dot(hidden2[...], router_full[...]), -1e30)
+    powers = jnp.exp(logits - jnp.max(logits, axis=1, keepdims=True))
+    gate = powers / jnp.sum(powers, axis=1, keepdims=True)
+    count = gates_in.shape[0]
+    where_row = lax.broadcasted_iota(jnp.int32, (count, 128), 0)
+    where_lane = lanes_of((count, 128))
+    group_row = lax.rem(where_row, 8)
+    target = lax.div(where_row, 8) * local + group_row
+    pick = jnp.where(group_row < local, jnp.where(target == where_lane, 1.0, 0.0), 0.0).astype(LOW)
+    high, low = two_parts(gates_in[...])
+    gate_back = dot(high, pick, 0, 0) + dot(low, pick, 0, 0)
+    grad_logits = (gate * (gate_back - jnp.sum(gate * gate_back, axis=1, keepdims=True))).astype(LOW)
+    grad_router = dot(hidden2[...], grad_logits, 0, 0)
+    grad_hidden2 = hid_sum[...] + dot(grad_logits, router_full[...], 1, 1)
+    back, gain2_sum = norm_back(middle[...], gain_row(1), grad_hidden2)
+    grad_middle = cot[...].astype(F32) + back
+    input_grad[...] = grad_middle
+    branch[...] = grad_middle.astype(LOW)
+
+    def chunk_grads(i, lhs, rhs_ref):
+        def part(n, carry):
+            made = dot(lhs[:, pl.ds(pl.multiple_of(n * tile, tile), tile)], rhs_ref[...], 0, 0).astype(LOW)
+            for k in range(tile // side):
+                own[i, n * (tile // shard) + k // 2, k % 2] = made[k * side : (k + 1) * side]
+            return carry
+
+        if tile % shard == 0:
+            lax.fori_loop(0, width // tile, part, 0)
+
+    for i in range(2):
+        rhs[...] = branch[:, pl.ds(i * tile, tile)]
+        chunk_grads(i, attended, rhs)
+        big.start(i)
+
+    def att_tile(n, carry):
+        rows = pl.ds(pl.multiple_of(n * tile, tile), tile)
+        grad_att[:, rows] = dot(branch[...], output_full[rows, :], 1, 1).astype(LOW)
+        return carry
+
+    lax.fori_loop(0, width // tile, att_tile, 0)
+
+    def unrotate(field):
+        return field * cosine[...] - turned(field * sine[...])
+
+    scale = HD**-0.5
+
+    def group(c):
+        cols = pl.ds(pl.multiple_of(c * 128, 128), 128)
+        pair, grad_pair = queries[:, cols], grad_att[:, cols]
+        zero = jnp.zeros_like(pair)
+        key, value = keys[c], values[c]
+        grad_query, grad_key, grad_value = [], 0.0, 0.0
+        for h in range(2):
+            here = left if h == 0 else jnp.logical_not(left)
+            query, grad_out = jnp.where(here, pair, zero), jnp.where(here, grad_pair, zero)
+            logs = jnp.sum(jnp.where(lane == 2 * c + h, log_total[...], 0.0), axis=1, keepdims=True)
+            probs = jnp.exp(dot(query, key, 1, 1) * scale + bias[...] - logs)
+            grad_probs = dot(grad_out, value, 1, 1)
+            grad_scores = (probs * (grad_probs - jnp.sum(probs * grad_probs, axis=1, keepdims=True))).astype(LOW)
+            grad_value = grad_value + dot(probs.astype(LOW), grad_out, 0, 0)
+            grad_query.append(dot(grad_scores, key))
+            grad_key = grad_key + dot(grad_scores, query, 0, 0)
+        grad_q_pre[:, cols] = unrotate(jnp.where(left, grad_query[0], grad_query[1]) * scale).astype(LOW)
+        grad_key = (grad_key + pltpu.roll(grad_key, HD, 1)) * scale
+        return unrotate(grad_key), grad_value + pltpu.roll(grad_value, HD, 1)
+
+    def two_groups(i):
+        key_a, value_a = group(2 * i)
+        key_b, value_b = group(2 * i + 1)
+        at = pl.multiple_of(i * 128, 128)
+        grad_kv_pre[:, pl.ds(at, 128)] = jnp.where(left, key_a, key_b).astype(LOW)
+        at = pl.multiple_of(KV * HD + i * 128, 128)
+        grad_kv_pre[:, pl.ds(at, 128)] = jnp.where(left, value_a, value_b).astype(LOW)
+
+    def gather_rhs(i):
+        rhs[:, pl.ds(0, 256)] = grad_q_pre[:, pl.ds(i * 256, 256)]
+        rhs[:, pl.ds(256, 128)] = grad_kv_pre[:, pl.ds(i * 128, 128)]
+        rhs[:, pl.ds(384, 128)] = grad_kv_pre[:, pl.ds(KV * HD + i * 128, 128)]
+
+    for i in range(KV // 2):
+        two_groups(i)
+        if i == 0:
+            big.paired(0)
+            big.paired(1)
+        if i == 1:
+            big.met(0, 0)
+            big.paired(2)
+        if i == 2:
+            big.met(1, 0)
+            big.met(0, 1)
+            big.paired(3)
+        if i == 3:
+            big.met(1, 1)
+            big.met(2, 0)
+            big.paired(4)
+        gather_rhs(i)
+        chunk_grads(2 + i, hidden, rhs)
+        big.start(2 + i)
+
+    def hidden_tile(n, carry):
+        cols = pl.ds(pl.multiple_of(n * tile, tile), tile)
+        grad = dot(grad_q_pre[...], query_full[cols, :], 1, 1) + dot(grad_kv_pre[...], keyval_full[cols, :], 1, 1)
+        hid_sum_out[:, cols] = grad
+        return carry
+
+    hid_sum_out = rest[38]
+    lax.fori_loop(0, width // tile, hidden_tile, 0)
+    big.paired(5)
+    back, gain1_sum = norm_back(x_ref[...].astype(F32), gain_row(0), hid_sum_out[...])
+    input_grad[...] = input_grad[...] + back
+
+    sub = lax.broadcasted_iota(jnp.int32, (16, width), 0)
+    sums = jnp.zeros((16, width), F32)
+    for k, row in enumerate((gain1_sum, gain2_sum)):
+        first, second = two_parts(row)
+        sums = jnp.where(sub == 2 * k, first.astype(F32), jnp.where(sub == 2 * k + 1, second.astype(F32), sums))
+    line_at = lax.broadcasted_iota(jnp.int32, (16, 128), 0)
+    column = jnp.where(lanes_of((16, 128)) == EXPERTS + lax.div(line_at, 2), jnp.where(line_at < 4, 1.0, 0.0), 0.0).astype(LOW)
+    little_all = (grad_router + dot(sums.astype(LOW), column, 0, 0)).astype(LOW)
+    for d in range(n_dp):
+        for k in range(2):
+            at = d * shard + k * side
+            own_s[0, d, k] = little_all[at : at + side]
+    little.start(0)
+
+    big.met(2, 1)
+    big.met(3, 0)
+    big.met(4, 0)
+    little.paired(0)
+    big.met(3, 1)
+    big.met(5, 0)
+    little.met(0, 0)
+    big.met(4, 1)
+    little.met(0, 1)
+    big.met(5, 1)
+    steps = own.shape[0] + big.depth - 1
+
+    def line(t, carry):
+        big.line(t)
+        return carry
+
+    lax.fori_loop(0, steps, line, 0)
+
+    def little_line(t, carry):
+        little.line(t)
+        return carry
+
+    lax.fori_loop(0, little.depth, little_line, 0)
+
+    def place(i, which, field):
+        rows = pl.ds(pl.multiple_of(which * side, 16), side)
+        if i < 2:
+            add_rows(grad_o.at[rows, pl.ds(i * tile, tile)], field)
+            return
+        i = i - 2
+        add_rows(grad_q.at[rows, pl.ds(i * 256, 256)], field.at[:, pl.ds(0, 256)])
+        add_rows(grad_kv.at[rows, pl.ds(i * 128, 128)], field.at[:, pl.ds(256, 128)])
+        add_rows(grad_kv.at[rows, pl.ds(KV * HD + i * 128, 128)], field.at[:, pl.ds(384, 128)])
+
+    chunks = own.shape[0]
+    for i in range(chunks):
+        big.close(i)
+    little.close(0)
+    for i in range(chunks):
+        place(i, big.core, big.final.at[i])
+    add_rows(grad_s.at[pl.ds(pl.multiple_of(big.core * side, 16), side)], little.final.at[0])
+    for i in range(chunks):
+        big.last(i).wait_recv()
+        place(i, 1 - big.core, big.other.at[i])
+        big.finish(i)
+    little.last(0).wait_recv()
+    add_rows(grad_s.at[pl.ds(pl.multiple_of((1 - big.core) * side, 16), side)], little.other.at[0])
+    little.finish(0)
+
+
+def back(n_dp, n_exp, local, tokens, cotangent, hid_sum, gates_in, routes, parents, tables, saved, collective_id):
+    tree, width = tokens.shape
+    shard = width // n_dp
+    shape = jax.ShapeDtypeStruct
+    side, chunks, tile = shard // 2, 6, 512
+    big_bufs, big_sems = GradSum.scratch(n_dp, chunks, side, tile)
+    little_bufs, little_sems = GradSum.scratch(n_dp, 1, side, 128)
+    vm = pltpu.VMEM
+    args = (tokens, cotangent, hid_sum, gates_in, routes, parents, *tables, *saved)
+    return pl.pallas_call(
+        functools.partial(back_body, n_dp, n_exp, local),
+        out_shape=[
+            shape((tree, width), F32), shape((shard, width), F32), shape((shard, width), F32), shape((shard, width), F32),
+            shape((shard, 128), F32),
+        ],
+        in_specs=[pl.BlockSpec(memory_space=VMEM)] * len(args),
+        out_specs=[pl.BlockSpec(memory_space=VMEM)] * 5,
+        scratch_shapes=[
+            vm((tree, tree), F32), vm((tree, width), LOW), vm((tree, width), LOW), vm((tree, width), LOW), vm((tree, width), LOW),
+            vm((tree, tile), LOW), vm((chunks, n_dp, 2, side, tile), LOW), vm((1, n_dp, 2, side, 128), LOW),
+            *big_bufs, *big_sems, *little_bufs, *little_sems, vm((tree, width), F32),
+        ],
+        compiler_params=pltpu.CompilerParams(
+            collective_id=collective_id, has_side_effects=True, vmem_limit_bytes=60 * MIB),
+        name="back",
+    )(*args)
 
 
 def tree_layout(tree_rows):
@@ -958,47 +1330,10 @@
     return (segment, position)
 
 
-def path_allowed(parent_row, segment):
-    segment_ids = jnp.arange(parent_row.shape[0], dtype=jnp.int32)
-    grandparent = parent_row[parent_row]
-    on_path = (
-        (segment_ids[None, :] == segment_ids[:, None])
-        | (segment_ids[None, :] == parent_row[:, None])
-        | (segment_ids[None, :] == grandparent[:, None])
-    ).astype(jnp.float32)
-    seg_hot = (segment[:, None] == segment_ids[None, :]).astype(jnp.float32)
-    reach = jnp.dot(
-        jnp.dot(seg_hot, on_path, precision=lax.Precision.HIGHEST),
-        seg_hot.T,
-        precision=lax.Precision.HIGHEST,
-    )
-    row_index = jnp.arange(segment.shape[0], dtype=jnp.int32)
-    return (reach > 0.5) & (row_index[None, :] <= row_index[:, None])
-
-
 def rope_tables(position):
     frequency = 10000.0 ** (-jnp.arange(0, HD, 2, dtype=jnp.float32) / HD)
     angles = position.astype(jnp.float32)[:, None] * frequency[None, :]
     return (jnp.concatenate([jnp.cos(angles)] * 2, -1), jnp.concatenate([jnp.sin(angles)] * 2, -1))
-
-
-def turn_half(field):
-    half_width = field.shape[-1] // 2
-    return jnp.concatenate([-field[..., half_width:], field[..., :half_width]], axis=-1)
-
-
-def rotary(field, cosine, sine_table):
-    return field * cosine + turn_half(field) * sine_table
-
-
-def unrotate(grad_field, cosine, sine_table):
-    return grad_field * cosine - turn_half(grad_field * sine_table)
-
-
-def rms_norm(field, gain_vector):
-    return (
-        field * lax.rsqrt(jnp.mean(field * field, axis=-1, keepdims=True) + EPSILON) * gain_vector
-    )
 
 
 def gated_unit(gate_up):
@@ -1012,6 +1347,7 @@
 ):
     tree_rows, width = hidden2.shape
     capacity = CAP
+    routes_all = routes_all.transpose(0, 2, 1)
     expert_ids = jnp.arange(EXPERTS, dtype=jnp.int32)
     here = lax.axis_index("expert")
     local = expert_in.shape[0]
@@ -1088,7 +1424,7 @@
         axis=2,
     ).reshape(local, width + units, width)
     share = lax.psum_scatter(grads, "dp", scatter_dimension=1, tiled=True).astype(jnp.float32)
-    gates_mine = gates_mine.T.reshape(n_exp, local, tree_rows)
+    gates_mine = jnp.pad(gates_mine.T.reshape(n_exp, local, tree_rows), ((0, 0), (0, 8 - local), (0, 0)))
     return block_out, hid_sum, gates_mine, share[:, : width // n_dp], share[:, width // n_dp :]
 
 
@@ -1106,162 +1442,32 @@
     routes,
     parents,
 ):
+    n_dp, n_exp = lax.axis_size("dp"), lax.axis_size("expert")
+    local = expert_in.shape[0]
     tree_rows = tokens.shape[0]
-    width = tokens.shape[1]
-    capacity = CAP
-    groups = H // KV
-    kv_width = KV * HD
-    score_scale = HD ** (-0.5)
-    n_dp, n_exp = lax.axis_size("dp"), lax.axis_size("expert")
     grad_y = lax.all_gather(cotangent, "expert", axis=0, tiled=False)
-    routes_all = lax.all_gather(routes, "expert", axis=0, tiled=False)
-    rows = w_query.shape[0]
-    small = jnp.concatenate(
-        [w_router, attn_gain[:, None], moe_gain[:, None], jnp.zeros((rows, 128 - EXPERTS - 2), w_router.dtype)], axis=1
+    _, position = tree_layout(tree_rows)
+    tables = tuple(jnp.concatenate([table, table], axis=1) for table in rope_tables(position))
+    (hidden, queries, keys, values, attended, middle, hidden2, log_total, *full, gains, routes_all) = front(
+        n_dp, n_exp, tokens, attn_gain, moe_gain, w_router, w_query, w_keyval, w_output, routes.T, parents, tables, 1
     )
-    query_full, keyval_full, output_full, small_full = gather_weights(
-        n_dp, (w_query, w_keyval, w_output, small), 1
+    run_experts = experts if (n_dp, n_exp) == (4, 8) else experts_plain
+    block_out, hid_sum, gate_grads, expert_in_share, expert_out_share = run_experts(
+        n_dp, n_exp, hidden2, grad_y, routes_all, full[3][:, :EXPERTS], expert_in, expert_out, middle, 2
     )
-    router_full = small_full[:, :EXPERTS]
-    gain_first, gain_second = small_full[:, EXPERTS], small_full[:, EXPERTS + 1]
-    inputs = tokens.astype(jnp.float32)
-    segment, position = tree_layout(tree_rows)
-    allowed = path_allowed(parents[0], segment)
-    cosine, sine_table = rope_tables(position)
-    cos_four, sin_four = (cosine[:, None, None, :], sine_table[:, None, None, :])
-    cos_three, sin_three = (cosine[:, None, :], sine_table[:, None, :])
-    normed, first_back = jax.vjp(rms_norm, inputs, gain_first.astype(jnp.float32))
-    hidden = normed.astype(jnp.bfloat16)
-    query_pre = jnp.dot(hidden, query_full, preferred_element_type=jnp.float32)
-    keyval_pre = jnp.dot(hidden, keyval_full, preferred_element_type=jnp.float32)
-    queries = rotary(query_pre.reshape(tree_rows, KV, groups, HD), cos_four, sin_four).astype(
-        jnp.bfloat16
-    )
-    key_heads = rotary(
-        keyval_pre[:, :kv_width].reshape(tree_rows, KV, HD), cos_three, sin_three
-    ).astype(jnp.bfloat16)
-    values = keyval_pre[:, kv_width:].reshape(tree_rows, KV, HD).astype(jnp.bfloat16)
-
-    def score_block():
-        raw_scores = (
-            jnp.einsum("tkgd,skd->kgts", queries, key_heads, preferred_element_type=jnp.float32)
-            * score_scale
-        )
-        return jnp.where(allowed, raw_scores, -1e30)
-
-    scores = score_block()
-    row_max = jnp.max(scores, axis=-1, keepdims=True)
-    exp_scores = jnp.exp(scores - row_max)
-    row_total = jnp.sum(exp_scores, axis=-1, keepdims=True)
-    log_total = row_max + jnp.log(row_total)
-    attn_low = (exp_scores / row_total).astype(jnp.bfloat16)
-    attended = jnp.einsum("kgts,skd->tkgd", attn_low, values, preferred_element_type=jnp.float32)
-    attended = attended.reshape(tree_rows, H * HD).astype(jnp.bfloat16)
-    middle = inputs + jnp.dot(attended, output_full, preferred_element_type=jnp.float32)
-    normed2, second_back = jax.vjp(rms_norm, middle, gain_second.astype(jnp.float32))
-    hidden2 = normed2.astype(jnp.bfloat16)
-    logits = jnp.dot(hidden2, router_full, preferred_element_type=jnp.float32)
-    expert_ids = jnp.arange(EXPERTS, dtype=jnp.int32)
-    route_hot = (routes[:, :, None] == expert_ids[None, None, :]).astype(jnp.float32)
-    picked = jnp.sum(route_hot * logits[:, None, :], axis=2)
-    picked_exp = jnp.exp(picked - jnp.max(picked, axis=1, keepdims=True))
-    gate_weights = picked_exp / jnp.sum(picked_exp, axis=1, keepdims=True)
-    run_experts = experts if (n_dp, n_exp) == (4, 8) else experts_plain
-    block_out, hid_sum, gates_mine, expert_in_share, expert_out_share = run_experts(
-        n_dp, n_exp, hidden2, grad_y, routes_all, router_full, expert_in, expert_out, middle, 2
-    )
-    gates_mine = gates_mine[:, : expert_in.shape[0]].reshape(EXPERTS, tree_rows).T
-    grad_result = cotangent.astype(jnp.float32)
-    gate_dense = jnp.sum(route_hot * gate_weights[:, :, None], axis=1)
-    grad_logits = (
-        gate_dense
-        * (gates_mine - jnp.sum(gate_dense * gates_mine, axis=1, keepdims=True))
-    ).astype(jnp.bfloat16)
-    grad_router = jnp.einsum("td,te->de", hidden2, grad_logits, preferred_element_type=jnp.float32)
-    grad_hidden2 = hid_sum + jnp.einsum(
-        "te,de->td", grad_logits, router_full, preferred_element_type=jnp.float32
-    )
-    grad_mid_norm, grad_gain_second = second_back(grad_hidden2)
-    grad_middle = grad_result + grad_mid_norm
-    grad_branch = grad_middle.astype(jnp.bfloat16)
-    grad_w_out = jnp.einsum("ti,td->id", attended, grad_branch, preferred_element_type=jnp.float32)
-    grad_attended = jnp.einsum(
-        "td,id->ti", grad_branch, output_full, preferred_element_type=jnp.float32
-    )
-    grad_attended = grad_attended.astype(jnp.bfloat16).reshape(tree_rows, KV, groups, HD)
-    attn_probs = jnp.exp(score_block() - log_total)
-    probs_low = attn_probs.astype(jnp.bfloat16)
-    grad_values = jnp.einsum(
-        "kgts,tkgd->skd", probs_low, grad_attended, preferred_element_type=jnp.float32
-    )
-    grad_probs = jnp.einsum(
-        "tkgd,skd->kgts", grad_attended, values, preferred_element_type=jnp.float32
-    )
-    grad_scores = (
-        attn_probs * (grad_probs - jnp.sum(attn_probs * grad_probs, axis=-1, keepdims=True))
-    ).astype(jnp.bfloat16)
-    grad_query_rot = (
-        jnp.einsum("kgts,skd->tkgd", grad_scores, key_heads, preferred_element_type=jnp.float32)
-        * score_scale
-    )
-    grad_keys_rot = (
-        jnp.einsum("kgts,tkgd->skd", grad_scores, queries, preferred_element_type=jnp.float32)
-        * score_scale
-    )
-    grad_query_pre = (
-        unrotate(grad_query_rot, cos_four, sin_four).reshape(tree_rows, H * HD).astype(jnp.bfloat16)
-    )
-    grad_keyval_pre = jnp.concatenate(
-        [
-            unrotate(grad_keys_rot, cos_three, sin_three).reshape(tree_rows, kv_width),
-            grad_values.reshape(tree_rows, kv_width),
-        ],
-        axis=1,
-    ).astype(jnp.bfloat16)
-    grad_w_q = jnp.einsum("td,ti->di", hidden, grad_query_pre, preferred_element_type=jnp.float32)
-    grad_w_kv = jnp.einsum("td,ti->di", hidden, grad_keyval_pre, preferred_element_type=jnp.float32)
-    grad_hidden = jnp.einsum(
-        "ti,di->td", grad_query_pre, query_full, preferred_element_type=jnp.float32
-    ) + jnp.einsum("ti,di->td", grad_keyval_pre, keyval_full, preferred_element_type=jnp.float32)
-    grad_in_norm, grad_gain_first = first_back(grad_hidden)
-    input_grad = grad_middle + grad_in_norm
-    low = jnp.bfloat16
-    share = reduce_grads(
-        n_dp,
-        n_exp,
-        jnp.concatenate(
-            [
-                grad_w_q.astype(low),
-                grad_w_kv.astype(low),
-                grad_w_out.astype(low),
-                grad_router.astype(low),
-                grad_gain_first.astype(low)[:, None],
-                grad_gain_second.astype(low)[:, None],
-                jnp.zeros((width, 128 - EXPERTS - 2), low),
-            ],
-            axis=1,
-        ),
-        5,
-        5,
-    )
-    at = 3 * width
-    shares = (
-        share[:, at + EXPERTS],
-        share[:, :width],
-        share[:, width : 2 * width],
-        share[:, 2 * width : at],
-        share[:, at + EXPERTS + 1],
-        share[:, at : at + EXPERTS],
+    saved = (hidden, queries, keys, values, attended, middle, hidden2, log_total, *full, gains)
+    input_grad, grad_q, grad_kv, grad_o, grad_small = back(
+        n_dp, n_exp, local, tokens, cotangent, hid_sum, gate_grads.reshape(n_exp * 8, tree_rows), routes, parents, tables, saved, 3
     )
     return (
         block_out,
         input_grad,
-        shares[0],
-        shares[1],
-        shares[2],
-        shares[3],
-        shares[4],
-        shares[5],
+        grad_small[:, EXPERTS],
+        grad_q,
+        grad_kv,
+        grad_o,
+        grad_small[:, EXPERTS + 1],
+        grad_small[:, :EXPERTS],
         expert_in_share,
         expert_out_share,
     )

time: 442 us -> 382 us (0.86)
  matrix products: 38.1 us -> 0 us
  Pallas kernels: 312 us -> 344 us
  local copies, waits for them, and re-layouts: 39.7 us -> 20.2 us
  other arithmetic: 17.1 us -> 1.72 us
  blocking collectives: 14.9 us -> 0 us
    dot_general x20 -> x0, matrix products: 38.1 us -> none  [the longest x1 8.03 us: shards(): jnp.einsum('tkgd,skd->kgts', grad_attended, values, preferred_element_typ...]
    pallas_call x2, Pallas kernels: 111 us -> 149 us  [the longest x1 96 us: back(): pl.pallas_call(functools.partial(back_body, n_dp, n_exp, local), out_shap...]
    all_gather x1 -> x0, blocking collectives: 14.9 us -> none  [shards(): routes_all = lax.all_gather(routes, 'expert', axis=0, tiled=False)]
    concatenate x2 -> x0, local copies, waits for them, and re-layouts: 10.8 us -> none  [the longest x1 10.7 us: shards(): jnp.concatenate([grad_w_q.astype(low), grad_w_kv.astype(low), grad_w_out....]
    convert_element_type x7 -> x0, other arithmetic: 9.71 us -> none  [the longest x1 7.28 us: shards(): grad_scores = (attn_probs * (grad_probs - jnp.sum(attn_probs * grad_probs...]
    pallas_call x1, Pallas kernels: 201 us -> 195 us  [experts(): pl.pallas_call(functools.partial(experts_body, n_dp, n_exp), out_shape=[s...]
    unnamed x67 -> x24, local copies, waits for them, and re-layouts: 16.5 us -> 14.2 us
  transfers between devices with their start and end apart: 1 -> 1, of which waited for: 0 -> 1; matrix products, arithmetic and copies ran while one was open for 5% -> 2% of each run, Pallas kernels for 8% -> 14%
where the time goes in v5:
time: 382 us
  Pallas kernels  344 us (90%)
  local copies, waits for them, and re-layouts  20.2 us (5%)
  between operations  14.1 us (4%)
    pallas_call x1, Pallas kernels, experts(): pl.pallas_call(functools.partial(experts_body, n_dp, n_exp), out_shape=[s...  195 us
    pallas_call x1, Pallas kernels, back(): pl.pallas_call(functools.partial(back_body, n_dp, n_exp, local), out_shap...  96 us
    pallas_call x1, Pallas kernels, front(): pl.pallas_call(functools.partial(front_body, n_dp, n_exp), out_shape=[low...  52.6 us
    unnamed x24, local copies, waits for them, and re-layouts  14.2 us
  transfers between devices with their start and end apart: 1, of which 1 were waited for; matrix products, arithmetic and copies ran while one was open for 2% of the time, Pallas kernels for 14%

profile of v5, /device:TPU:0, one launch (start us, length us, event | category | flops | bytes accessed | tf_op | source)
XLA Modules:
  0.0 381.8 jit_solution(16116924487850091283)
XLA Ops:
  7.2 0.0 all-gather.3.cloned.1.call-start
  7.2 0.7 all-gather.3.cloned.1.call-update
  7.9 1.5 copy.26.router
  9.4 1.2 broadcast_in_dim.21.gain1
  10.6 1.2 broadcast_in_dim.22.gain2
  11.8 1.5 copy.28.routes
  13.3 0.6 multiply_sine_fusion
  14.0 1.0 pad_maximum_fusion
  15.0 52.6 %front.1 = (bf16[320,1024]{1,0:T(8,128)(2,1)}, bf16[320,1024]{1,0:T(8,128)(2,1)}, bf16[8,320,128]{2,1,0:T(8,128)(2,1)}, bf16[8,320,128]{2,1,0:T(8,128)(2,1)}, bf...) custom-call(bf16[320,1024]{1,0:T(8,128)(2,1)} %x_ref.3, ...), custom_call_target="tpu_custom_call" | custom-call | tf_op jit(solution)/shard_map/front/pallas_call | solution.py:908
  67.7 1.1 copy.27
  68.8 0.6 slice_bitcast_fusion.wr_t
  69.4 0.9 all-gather.3.cloned.1.call-done
  70.3 195.5 %experts.1 = (bf16[320,1024]{1,0:T(8,128)(2,1)}, f32[320,1024]{1,0:T(8,128)}, f32[8,8,320]{2,1,0:T(8,128)}, f32[4,256,1024]{2,1,0:T(8,128)}, f32[4,128,1024]{2,1,0:T(8,128)}) custom-call(bf16[320,1024]{1,0:T(8,128)(2,1)} %get-tuple-element.34.hid_ref.hidden2, bf16[8,320,1024]{2,1,0:T(8,128)(2,1)} %bitcast.6, s32[8,8,320]{2,1,0:T(8,128)} %get-tuple-element.35.routes_t, ...), custom_call_target="tpu_custom_call" | custom-call | tf_op jit(solution)/shard_map/experts/pallas_call | solution.py:635
  265.8 0.0 copy-start.6
  265.8 96.0 %back.1 = (f32[320,1024]{1,0:T(8,128)}, f32[256,1024]{1,0:T(8,128)}, f32[256,1024]{1,0:T(8,128)}, f32[256,1024]{1,0:T(8,128)}, f32[256,128]{1,0:T(8,128)}) custom-call(bf16[320,1024]{1,0:T(8,128)(2,1)} %x_ref.3, bf16[320,1024]{1,0:T(8,128)(2,1)} %cot.1, f32[320,1024]{1,0:T(8,128)} %get-tuple-element.39.hid_sum, f32[64,320]{1,0:T(8,128)} %bitcast.8, ...), custom_call_target="tpu_custom_call" | custom-call | tf_op jit(solution)/shard_map/back/pallas_call | solution.py:1288
  361.8 0.0 copy-start.2
  361.8 1.9 slice_reduce_fusion
  363.7 0.0 copy-start.5
  363.7 1.7 copy.29
  365.3 0.0 copy-done.6
  365.3 0.8 copy.37
  366.2 0.0 copy-done.2
  366.2 0.0 copy-start.4
  366.2 0.0 copy-start.3
  366.2 1.1 copy.38
  367.2 0.0 copy-done.5
  367.2 0.0 copy-start
  367.2 1.0 copy.39
  368.2 0.0 copy-done.4
  368.2 1.0 copy.40
  369.2 0.0 copy-done.3
  369.2 1.0 copy.41
  370.2 0.3 copy-done
  370.5 0.0 copy-start.1
  370.5 2.1 copy.42
  372.6 1.0 copy-done.1
  373.6 1.3 copy.43
  (2 shorter events, 0.0 us)
Async XLA Ops:
  7.2 63.1 %all-gather.3.cloned.1.call-start = ((), (), s32[]{:S(2)}) async-start(), calls=%async_computation | async-start | bytes 5898240 | tf_op jit(solution)/shard_map/all_gather | solution.py:1448
  265.8 99.6 %copy-start.6 = (bf16[320,1024]{1,0:T(8,128)(2,1)S(1)}, bf16[320,1024]{1,0:T(8,128)(2,1)}, u32[]{:S(2)}) copy-start(bf16[320,1024]{1,0:T(8,128)(2,1)} %get-tuple-element.94) | copy-start | bytes 1966084
  361.8 4.4 %copy-start.2 = (f32[320,1024]{1,0:T(8,128)S(1)}, f32[320,1024]{1,0:T(8,128)}, u32[]{:S(2)}) copy-start(f32[320,1024]{1,0:T(8,128)} %get-tuple-element.95) | copy-start | bytes 3932164
  363.7 3.6 copy-start.5
  366.2 2.0 copy-start.4
  366.2 3.0 copy-start.3
  367.2 3.2 copy-start
  370.5 3.1 copy-start.1
Sparse Core Ops, SparseCore 0:
  9.7 60.5 all-gather.2

commit v6 on v5

--- a/solution.py
+++ b/solution.py
@@ -2,6 +2,7 @@
 
 import jax
 import jax.numpy as jnp
+import numpy as np
 from jax import lax
 from jax.experimental import pallas as pl
 from jax.experimental.pallas import tpu as pltpu
@@ -267,12 +268,12 @@
     return lax.dot_general(a, b, (((over_a,), (over_b,)), ((), ())), preferred_element_type=F32)
 
 
-def experts_body(n_dp, n_exp, hid_ref, gy_hbm, routes_t, wr_t, w_in_hbm, w_out_hbm, middle,
-                 block_out, hid_sum, gates_out, in_share, out_share,
+def experts_body(n_dp, n_exp, hid_ref, gy_hbm, routes_t, wr_t, w_in_hbm, w_out_hbm,
+                 parts_hbm, hid_sum, gates_out, in_share, out_share, late,
                  x_all, w_in, w_out, sent, grows, gu, tmp, acts, stage, slots, gates, dots, wide,
                  pair_buf, held, got, *sems):
-    w_sem, gy_sem, wide_sem, own_sem, ready, gate_send, gate_recv, dp_ready, dp_send, dp_recv = sems[:10]
-    gather_sems, out_sems, hid_sems = sems[10:14], sems[14:18], sems[18:22]
+    w_sem, gy_sem, wide_sem, own_sem, part_sem, late_sem, gate_send, gate_recv, dp_ready, dp_send, dp_recv = sems[:11]
+    gather_sems, hid_sems = sems[11:15], sems[15:19]
     me = lax.axis_index("dp")
     local, _, width = sent.shape
     tree, hidden_units = hid_ref.shape[0], w_out.shape[1]
@@ -334,7 +335,7 @@
         chosen = jnp.zeros((EXPERTS, tree), F32)
         for k in range(names.shape[0]):
             chosen = jnp.maximum(chosen, jnp.where(names[k : k + 1, :] == experts, 1.0, 0.0))
-        logits = jnp.where(chosen > 0.5, dot(wr_t[...], x_all[j], 1, 1), -1e30)
+        logits = jnp.where(chosen > 0.5, dot(wr_t[pl.ds(0, EXPERTS), :], x_all[j], 1, 1), -1e30)
         powers = jnp.exp(logits - jnp.max(logits, axis=0, keepdims=True))
         share = powers / jnp.sum(powers, axis=0, keepdims=True)
         sub = lax.broadcasted_iota(jnp.int32, (8, tree), 0)
@@ -385,11 +386,15 @@
 
         lax.fori_loop(0, local, one_expert, 0)
 
+    def part_copy(j):
+        return pltpu.make_async_copy(x_all.at[j], parts_hbm.at[j], part_sem.at[j])
+
     def combine_out(chip):
         def one_tree(q, carry):
             j = 2 * chip + q
             rows = pl.ds(pl.multiple_of(q * rows_e, rows_e), rows_e)
             x_all[j] = dot(places_t(j), tmp[rows, :]).astype(LOW)
+            part_copy(j).start()
             return carry
 
         lax.fori_loop(0, 2, one_tree, 0)
@@ -401,7 +406,6 @@
         return carry
 
     events = gather.events()
-    out = RingScatter(ring, lambda e: x_all.at[e], views((pair_buf, held, got)), out_sems)
 
     def chip_at(d):
         return lax.rem(ring.z + d, depth)
@@ -452,15 +456,9 @@
                         gather.finish_event(event)
 
         combine_out(chip)
-        pl.when(g == 0)(lambda: out.start_pair(0))
-        pl.when(g == 1)(lambda: out.start_pair(depth - 1))
-        pl.when(g == 2)(lambda: out.start_pair(1))
-        pl.when(g == 3)(lambda: out.start_pair(2))
         return carry
 
     lax.fori_loop(0, depth, group, 0)
-    out.first()
-    out.early()
 
     in_rows, out_rows = width // n_dp, hidden_units // n_dp
     cut = (in_rows + out_rows) // 2
@@ -553,17 +551,24 @@
             return inner
 
         lax.fori_loop(0, n_exp * SLOTS // 512, back_half, 0)
-        for bit in (1, 2):
-            pl.semaphore_signal(dp_ready.at[e], inc=1, device_id={"dp": me ^ bit}, device_id_type=MESH)
-        pl.when(e == local // 2 - 1)(out.late)
+        @pl.when(e < local - 1)
+        def _():
+            for bit in (1, 2):
+                pl.semaphore_signal(dp_ready.at[e], inc=1, device_id={"dp": me ^ bit}, device_id_type=MESH)
+
         pl.when(e >= 2)(lambda: grads_turn(e - 2))
         return carry
 
     dots[...] = jnp.zeros(dots.shape, F32)
-    middle_copy = pltpu.make_async_copy(middle, wide.at[pl.ds(0, tree)], wide_sem.at[0])
-    middle_copy.start()
     lax.fori_loop(0, local, backward, 0)
-    grads_start(local - 1)
+
+    def late_copy(r, h):
+        at = pl.multiple_of((me ^ r) * 2 * cut + h * cut, 16)
+        return pltpu.make_async_copy(grad_half(local - 1, r, h), late.at[pl.ds(at, cut)], late_sem.at[2 * r + h])
+
+    for r in range(n_dp):
+        for h in range(2):
+            late_copy(r, h).start()
 
     gate_copies = []
     for k, e in enumerate(peers):
@@ -571,11 +576,8 @@
         copy.start()
         gate_copies.append(copy)
     gates_out[mine] = dots[mine]
-    middle_copy.wait()
-    out.last(block_out, wide.at[pl.ds(0, tree)])
-    out.finish_sends()
-    for partner in (ring.pair, ring.right, ring.left):
-        pl.semaphore_signal(ready, inc=1, device_id={"expert": partner}, device_id_type=MESH)
+    for j in range(n_exp):
+        part_copy(j).wait()
     hid = RingScatter(ring, lambda e: x_all.at[e], views((pair_buf, held, got)), hid_sems)
 
     def combine_hid(g, carry):
@@ -591,11 +593,7 @@
 
         lax.fori_loop(0, 2, one_tree, 0)
 
-        @pl.when(g == 0)
-        def _():
-            pl.semaphore_wait(ready, 3)
-            hid.start_pair(2)
-
+        pl.when(g == 0)(lambda: hid.start_pair(2))
         pl.when(g == 1)(lambda: hid.start_pair(1))
         pl.when(g == 2)(lambda: hid.start_pair(depth - 1))
         pl.when(g == 3)(lambda: hid.start_pair(0))
@@ -604,18 +602,19 @@
 
     lax.fori_loop(0, depth, combine_hid, 0)
     hid.early()
+    grads_end(0)
     grads_turn(local - 2)
-    grads_end(0)
     hid.late()
     grads_end(1)
-    grads_turn(local - 1)
     hid.last(wide.at[pl.ds(0, tree)])
     hid_copy = pltpu.make_async_copy(wide.at[pl.ds(0, tree)], hid_sum, wide_sem.at[0])
     hid_copy.start()
     hid_copy.wait()
-    for e in range(2, local):
+    for e in range(2, local - 1):
         grads_end(e)
-
+    for r in range(n_dp):
+        for h in range(2):
+            late_copy(r, h).wait()
     for k, copy in enumerate(gate_copies):
         copy.wait_send()
         source = lax.rem(mine + n_exp - 1 - k, n_exp)
@@ -623,26 +622,26 @@
     hid.finish_sends()
 
 
-def experts(n_dp, n_exp, hidden2, grad_y, routes_all, router, expert_in, expert_out, middle, collective_id):
+def experts(n_dp, n_exp, hidden2, grad_y, routes_all, router_t, expert_in, expert_out, collective_id):
     local, width, both = expert_in.shape
     units = expert_out.shape[1]
     tree = hidden2.shape[0]
     rows = n_exp * SLOTS
     sem = pltpu.SemaphoreType.DMA
-    bufs, out_sems = RingScatter.scratch(n_exp, (tree, width), LOW)
-    _, hid_sems = RingScatter.scratch(n_exp, (tree, width), LOW)
+    bufs, hid_sems = RingScatter.scratch(n_exp, (tree, width), LOW)
     shape = jax.ShapeDtypeStruct
     return pl.pallas_call(
         functools.partial(experts_body, n_dp, n_exp),
         out_shape=[
-            shape((tree, width), LOW),
+            shape((n_exp, tree, width), LOW),
             shape((tree, width), F32),
             shape((n_exp, 8, tree), F32),
-            shape((local, width // n_dp, width), F32),
-            shape((local, units // n_dp, width), F32),
+            shape((local - 1, width // n_dp, width), F32),
+            shape((local - 1, units // n_dp, width), F32),
+            shape((width + units, width), LOW),
         ],
-        in_specs=[pl.BlockSpec(memory_space=s) for s in (VMEM, ANY, VMEM, VMEM, ANY, ANY, ANY)],
-        out_specs=[pl.BlockSpec(memory_space=s) for s in (VMEM, ANY, VMEM, ANY, ANY)],
+        in_specs=[pl.BlockSpec(memory_space=s) for s in (VMEM, ANY, VMEM, VMEM, ANY, ANY)],
+        out_specs=[pl.BlockSpec(memory_space=s) for s in (ANY, ANY, VMEM, ANY, ANY, ANY)],
         scratch_shapes=[
             pltpu.VMEM((n_exp, tree, width), LOW),
             pltpu.VMEM((local, width, both), LOW),
@@ -658,14 +657,14 @@
             pltpu.VMEM((n_exp, 8, tree), F32),
             pltpu.VMEM(((width + units) // n_dp, width), F32),
             *bufs,
-            sem((2,)), sem((2,)), sem((2,)), sem, pltpu.SemaphoreType.REGULAR, sem((n_exp - 1,)), sem((n_exp - 1,)),
+            sem((2,)), sem((2,)), sem((2,)), sem, sem((n_exp,)), sem((2 * n_dp,)), sem((n_exp - 1,)), sem((n_exp - 1,)),
             pltpu.SemaphoreType.REGULAR((local,)), sem((local, 6)), sem((local, 6)),
-            *RingGather.scratch(n_exp), *out_sems, *hid_sems,
+            *RingGather.scratch(n_exp), *hid_sems,
         ],
         compiler_params=pltpu.CompilerParams(
             collective_id=collective_id, has_side_effects=True, vmem_limit_bytes=63 * MIB),
         name="experts",
-    )(hidden2, grad_y, routes_all, router.T, expert_in, expert_out, middle)
+    )(hidden2, grad_y, routes_all, router_t, expert_in, expert_out)
 
 
 def lanes_of(shape):
@@ -779,55 +778,67 @@
                     self.across(a, p, r, self.core).wait_send()
 
 
-def front_body(n_dp, n_exp, x_ref, gain1, gain2, router, w_query, w_keyval, w_output, routes_t, parents, cosine, sine,
-               hidden, queries, keys, values, attended, middle, hidden2, log_total,
-               query_full, keyval_full, output_full, router_full, gains, routes_all,
-               router_pad, gain_pad, bias, *sems):
-    gather_sems, (gain_send, gain_recv, route_send, route_recv) = sems[:5], sems[5:9]
+def front_body(n_dp, n_exp, x_ref, gain_pair, router_in, w_query, w_keyval, w_output, routes_t, parents, cosine, sine,
+               hidden_hbm, queries_hbm, keys_hbm, values_hbm, attended, middle, hidden2, log_total,
+               query_hbm, keyval_hbm, output_hbm, router_t, gains, routes_all,
+               hidden, queries, keys, values, query_full, keyval_full, output_full, small, small_all, bias, *sems):
+    gather_sems, (small_send, small_recv, route_send, route_recv, out_sem) = sems[:5], sems[5:10]
     me, mine = lax.axis_index("dp"), lax.axis_index("expert")
     peers = [lax.rem(mine + k, n_exp) for k in range(1, n_exp)]
     greet([(None, {"expert": e}) for e in peers] + [(None, {"dp": me ^ k}) for k in range(1, n_dp)])
     tree, width = x_ref.shape
     shard = w_query.shape[0]
 
-    router_pad[...] = jnp.zeros(router_pad.shape, LOW)
-    router_pad[:, pl.ds(0, EXPERTS)] = router[...]
+    small[...] = jnp.zeros(small.shape, LOW)
+    small[pl.ds(0, EXPERTS), :] = router_in[...]
     sub = lax.broadcasted_iota(jnp.int32, (16, shard), 0)
-    gain_pad[...] = jnp.where(sub == 0, gain1[...].astype(F32), jnp.where(sub == 1, gain2[...].astype(F32), 0.0)).astype(LOW)
-
-    gather = DpGather(n_dp, mine, me, (w_query, w_keyval, w_output, router_pad),
-                      (query_full, keyval_full, output_full, router_full), gather_sems)
-
-    def gain_copy(k):
-        return remote(gain_pad, gains.at[me], gain_send.at[k], gain_recv.at[k], dp=me ^ k)
+    gain_rows = gain_pair[...].astype(F32)
+    small[pl.ds(EXPERTS, 16), :] = jnp.where(sub == 0, gain_rows[:1], jnp.where(sub == 1, gain_rows[1:], 0.0)).astype(LOW)
+
+    gather = DpGather(n_dp, mine, me, (w_query, w_keyval, w_output), (query_full, keyval_full, output_full), gather_sems)
+
+    def small_copy(k):
+        return remote(small, small_all.at[me], small_send.at[k], small_recv.at[k], dp=me ^ k)
 
     def route_copy(k, e):
         return remote(routes_t, routes_all.at[mine], route_send.at[k], route_recv.at[k], expert=e)
 
+    saves = [
+        pltpu.make_async_copy(src, dst, out_sem.at[k])
+        for k, (src, dst) in enumerate((
+            (query_full, query_hbm), (keyval_full, keyval_hbm), (output_full, output_hbm), (hidden, hidden_hbm),
+            (queries, queries_hbm), (keys, keys_hbm), (values, values_hbm)))
+    ]
     for k in range(1, n_dp):
-        gain_copy(k).start()
-    for a in range(4):
-        gather.start(a)
+        small_copy(k).start()
+    gather.start(0)
+    gather.start(1)
     for k, e in enumerate(peers):
         route_copy(k, e).start()
-    gains[me] = gain_pad[...]
+    small_all[me] = small[...]
     routes_all[mine] = routes_t[...]
     bias[...] = mask_bias(parents, tree)
     log_total[...] = jnp.zeros(log_total.shape, F32)
+    x = x_ref[...].astype(F32)
+    scaled = x * inverse_rms(x)
     for k in range(1, n_dp):
-        remote(gain_pad, gains.at[me ^ k], gain_send.at[k], gain_recv.at[k], dp=me).wait_recv()
-
-    def gain_row(i):
-        return jnp.concatenate([gains[d].astype(F32)[i : i + 1] for d in range(n_dp)], axis=1)
-
-    x = x_ref[...].astype(F32)
-    hidden[...] = (x * inverse_rms(x) * gain_row(0)).astype(LOW)
+        remote(small, small_all.at[me ^ k], small_send.at[k], small_recv.at[k], dp=me).wait_recv()
+    joined = jnp.concatenate([small_all[d] for d in range(n_dp)], axis=1)
+    router_t[...] = jnp.zeros(router_t.shape, LOW)
+    router_t[pl.ds(0, EXPERTS), :] = joined[:EXPERTS]
+    gains[...] = joined[EXPERTS:]
+    gain_rows = joined[EXPERTS:].astype(F32)
+    hidden[...] = (scaled * gain_rows[:1]).astype(LOW)
+    saves[3].start()
     stages = len(gather.orders[0])
-    for j in range(stages):
-        for a in range(4 if j + 1 < stages else 2):
-            gather.turn(a, j)
+    for j in range(stages - 1):
+        gather.turn(0, j)
+        gather.turn(1, j)
+    gather.start(2)
+    gather.turn(0, stages - 1)
+    gather.turn(1, stages - 1)
     gather.ready(0)
-    gather.ready(1)
+    saves[0].start()
 
     def rotate(field):
         return field * cosine[...] + turned(field) * sine[...]
@@ -844,6 +855,9 @@
         return carry
 
     lax.fori_loop(0, width // tile, query_tile, 0)
+    saves[4].start()
+    gather.ready(1)
+    saves[1].start()
 
     def spread(field, out, i):
         other = pltpu.roll(field, HD, 1)
@@ -854,11 +868,13 @@
     pre = dot(hidden[...], keyval_full[:, pl.ds(0, half)])
     for i in range(half // 128):
         spread(rotate(pre[:, i * 128 : (i + 1) * 128]), keys, i)
+    saves[5].start()
     pre = dot(hidden[...], keyval_full[:, pl.ds(half, half)])
     for i in range(half // 128):
         spread(pre[:, i * 128 : (i + 1) * 128], values, i)
-    for a in range(2, 4):
-        gather.turn(a, stages - 1)
+    saves[6].start()
+    for j in range(stages):
+        gather.turn(2, j)
 
     def heads(c, carry):
         cols = pl.ds(pl.multiple_of(c * 128, 128), 128)
@@ -878,7 +894,7 @@
 
     lax.fori_loop(0, KV, heads, 0)
     gather.ready(2)
-    gather.ready(3)
+    saves[2].start()
 
     def middle_tile(n, carry):
         cols = pl.ds(pl.multiple_of(n * tile, tile), tile)
@@ -887,47 +903,52 @@
 
     lax.fori_loop(0, width // tile, middle_tile, 0)
     field = middle[...]
-    hidden2[...] = (field * inverse_rms(field) * gain_row(1)).astype(LOW)
-    for a in range(4):
+    hidden2[...] = (field * inverse_rms(field) * gain_rows[1:2]).astype(LOW)
+    for a in range(3):
         gather.finish(a)
     for k in range(1, n_dp):
-        gain_copy(k).wait_send()
+        small_copy(k).wait_send()
     for k, e in enumerate(peers):
         route_copy(k, e).wait_send()
         source = lax.rem(mine + n_exp - 1 - k, n_exp)
         remote(routes_t, routes_all.at[source], route_send.at[k], route_recv.at[k], expert=mine).wait_recv()
-
-
-def front(n_dp, n_exp, tokens, gain1, gain2, router, w_query, w_keyval, w_output, routes_t, parents, tables, collective_id):
+    for copy in saves:
+        copy.wait()
+
+
+def front(n_dp, n_exp, tokens, gain_pair, router_in, w_query, w_keyval, w_output, routes_t, parents, tables, collective_id):
     tree, width = tokens.shape
     shard = w_query.shape[0]
-    shape, sem = jax.ShapeDtypeStruct, pltpu.SemaphoreType.DMA
+    shape, sem, vm = jax.ShapeDtypeStruct, pltpu.SemaphoreType.DMA, pltpu.VMEM
     low = shape((tree, width), LOW)
     spread = shape((KV, tree, 128), LOW)
     full = shape((n_dp * shard, width), LOW)
+    small = (EXPERTS + 16, shard)
     return pl.pallas_call(
         functools.partial(front_body, n_dp, n_exp),
         out_shape=[
             low, low, spread, spread, low, shape((tree, width), F32), low, shape((tree, 128), F32),
-            full, full, full, shape((n_dp * shard, 128), LOW), shape((n_dp, 16, shard), LOW),
+            full, full, full, shape((128, width), LOW), shape((16, width), LOW),
             shape((n_exp,) + routes_t.shape, jnp.int32),
         ],
-        in_specs=[pl.BlockSpec(memory_space=VMEM)] * 11,
-        out_specs=[pl.BlockSpec(memory_space=VMEM)] * 14,
+        in_specs=[pl.BlockSpec(memory_space=VMEM)] * 10,
+        out_specs=[pl.BlockSpec(memory_space=s) for s in [ANY] * 4 + [VMEM] * 4 + [ANY] * 3 + [VMEM] * 3],
         scratch_shapes=[
-            pltpu.VMEM((shard, 128), LOW), pltpu.VMEM((16, shard), LOW), pltpu.VMEM((tree, tree), F32),
-            *DpGather.scratch(4, n_dp), sem((n_dp,)), sem((n_dp,)), sem((n_exp - 1,)), sem((n_exp - 1,)),
+            vm((tree, width), LOW), vm((tree, width), LOW), vm(spread.shape, LOW), vm(spread.shape, LOW),
+            vm(full.shape, LOW), vm(full.shape, LOW), vm(full.shape, LOW),
+            vm(small, LOW), vm((n_dp,) + small, LOW), vm((tree, tree), F32),
+            *DpGather.scratch(3, n_dp), sem((n_dp,)), sem((n_dp,)), sem((n_exp - 1,)), sem((n_exp - 1,)), sem((7,)),
         ],
         compiler_params=pltpu.CompilerParams(
             collective_id=collective_id, has_side_effects=True, vmem_limit_bytes=56 * MIB),
         name="front",
-    )(tokens, gain1[None], gain2[None], router, w_query, w_keyval, w_output, routes_t, parents, *tables)
+    )(tokens, gain_pair, router_in, w_query, w_keyval, w_output, routes_t, parents, *tables)
 
 
 class GradSum:
     def __init__(self, n_dp, n_exp, chunks, own, bufs, sems):
         self.n_dp, self.chunks, self.own = n_dp, chunks, own
-        (self.pair_in, self.total, self.dp_in, self.prefix, self.suffix, self.go_r, self.go_l, self.final, self.other) = bufs
+        (self.pair_in, self.dp_in, self.prefix, self.suffix, self.go_r, self.go_l, self.final, self.other) = bufs
         (self.pair_send, self.pair_recv, self.dp_send, self.dp_recv,
          self.send_r, self.send_l, self.recv_r, self.recv_l, self.last_send, self.last_recv) = sems
         self.me, self.mine = lax.axis_index("dp"), lax.axis_index("expert")
@@ -944,13 +965,16 @@
         stages = max(1, n_dp.bit_length() - 1)
         one = pltpu.VMEM((chunks, half, columns), LOW)
         many = pltpu.VMEM((chunks, n_dp, half, columns), LOW)
-        bufs = [many, many, many, one, one, one, one, one, one]
+        bufs = [many, many, one, one, one, one, one, one]
         sems = [sem((chunks, n_dp)), sem((chunks, n_dp)), sem((chunks, n_dp)), sem((chunks, n_dp))]
         return bufs, sems + [sem((chunks,))] * 6
 
     def partners(self):
-        return ([(None, {"expert": self.pair})] + [(None, {"dp": self.me ^ bit}) for bit in self.orders[0]]
-                + [(self.has_left, {"expert": self.mine - 2}), (self.has_right, {"expert": self.mine + 2})])
+        return [(None, {"dp": self.me ^ bit}) for bit in self.orders[0]] + [
+            (self.has_left, {"expert": self.mine - 2}), (self.has_right, {"expert": self.mine + 2})]
+
+    def total(self, i, r):
+        return self.own.at[i, self.me ^ r, self.core]
 
     def across(self, i, d):
         return remote(self.own.at[i, d, 1 - self.core], self.pair_in.at[i, d], self.pair_send.at[i, d],
@@ -964,7 +988,7 @@
         return order[j], [r | order[j] for r in blocks]
 
     def dp_copy(self, i, r, bit):
-        return remote(self.total.at[i, r], self.dp_in.at[i, r], self.dp_send.at[i, r], self.dp_recv.at[i, r], dp=self.me ^ bit)
+        return remote(self.total(i, r), self.dp_in.at[i, r], self.dp_send.at[i, r], self.dp_recv.at[i, r], dp=self.me ^ bit)
 
     def start(self, i):
         for d in range(self.n_dp):
@@ -974,7 +998,7 @@
         for r in range(self.n_dp - 1, -1, -1):
             d = self.me ^ r
             self.across(i, d).wait_recv()
-            add_rows(self.total.at[i, r], self.own.at[i, d, self.core], self.pair_in.at[i, d])
+            add_rows(self.total(i, r), self.total(i, r), self.pair_in.at[i, d])
         self.leave(i, 0)
 
     def leave(self, i, j):
@@ -987,7 +1011,7 @@
         bit, blocks = self.moved(i, j)
         for r in blocks:
             self.dp_copy(i, r, bit).wait_recv()
-            add_rows(self.total.at[i, r ^ bit], self.total.at[i, r ^ bit], self.dp_in.at[i, r])
+            add_rows(self.total(i, r ^ bit), self.total(i, r ^ bit), self.dp_in.at[i, r])
         self.leave(i, j + 1)
 
     def right(self, i):
@@ -997,7 +1021,7 @@
         return remote(self.go_l.at[i], self.suffix.at[i], self.send_l.at[i], self.recv_l.at[i], expert=self.mine - 2)
 
     def line(self, t):
-        i = t - self.z
+        i = t - 2 * self.z
         has_left, has_right = self.has_left, self.has_right
 
         @pl.when(jnp.logical_and(i >= 0, i < self.chunks))
@@ -1008,15 +1032,15 @@
 
             @pl.when(jnp.logical_and(has_left, has_right))
             def _():
-                add_rows(self.go_r.at[i], self.total.at[i, 0], self.prefix.at[i])
+                add_rows(self.go_r.at[i], self.total(i, 0), self.prefix.at[i])
 
             @pl.when(jnp.logical_not(has_left))
             def _():
-                add_rows(self.go_r.at[i], self.total.at[i, 0])
+                add_rows(self.go_r.at[i], self.total(i, 0))
 
             pl.when(has_right)(lambda: self.right(i).start())
 
-        k = t - (self.depth - 1 - self.z)
+        k = t - 2 * (self.depth - 1 - self.z)
 
         @pl.when(jnp.logical_and(k >= 0, k < self.chunks))
         def _():
@@ -1026,11 +1050,11 @@
 
             @pl.when(jnp.logical_and(has_left, has_right))
             def _():
-                add_rows(self.go_l.at[k], self.total.at[k, 0], self.suffix.at[k])
+                add_rows(self.go_l.at[k], self.total(k, 0), self.suffix.at[k])
 
             @pl.when(jnp.logical_not(has_right))
             def _():
-                add_rows(self.go_l.at[k], self.total.at[k, 0])
+                add_rows(self.go_l.at[k], self.total(k, 0))
 
             pl.when(has_left)(lambda: self.left(k).start())
 
@@ -1042,15 +1066,15 @@
 
         @pl.when(jnp.logical_and(has_left, has_right))
         def _():
-            add_rows(self.final.at[i], self.total.at[i, 0], self.prefix.at[i], self.suffix.at[i])
+            add_rows(self.final.at[i], self.total(i, 0), self.prefix.at[i], self.suffix.at[i])
 
         @pl.when(jnp.logical_not(has_left))
         def _():
-            add_rows(self.final.at[i], self.total.at[i, 0], self.suffix.at[i])
+            add_rows(self.final.at[i], self.total(i, 0), self.suffix.at[i])
 
         @pl.when(jnp.logical_not(has_right))
         def _():
-            add_rows(self.final.at[i], self.total.at[i, 0], self.prefix.at[i])
+            add_rows(self.final.at[i], self.total(i, 0), self.prefix.at[i])
 
         self.last(i).start()
 
@@ -1078,30 +1102,55 @@
     return back, jnp.sum(field * r * grad, axis=0, keepdims=True)
 
 
-def back_body(n_dp, n_exp, local, x_ref, cot, hid_sum, gates_in, routes, parents, cosine, sine,
+def back_body(n_dp, n_exp, local, with_out, x_ref, cot, hid_sum, gates_in, routes_t, parents, cosine, sine,
               hidden, queries, keys, values, attended, middle, hidden2, log_total,
-              query_full, keyval_full, output_full, router_full, gains,
-              input_grad, grad_q, grad_kv, grad_o, grad_s,
-              bias, branch, grad_att, grad_q_pre, grad_kv_pre, rhs, own, own_s, *rest):
-    big = GradSum(n_dp, n_exp, own.shape[0], own, rest[:9], rest[9:19])
-    little = GradSum(n_dp, n_exp, 1, own_s, rest[19:28], rest[28:38])
+              query_hbm, keyval_hbm, output_hbm, router_t, gains, *refs):
+    if with_out:
+        parts_hbm, refs = refs[0], refs[1:]
+    outs, refs = refs[: 5 + with_out], refs[5 + with_out :]
+    input_grad, grad_q, grad_kv, grad_o, grad_s = outs[:5]
+    (bias, branch, grad_att, grad_q_pre, grad_kv_pre, rhs, own, own_s, grad_hid, query_full, keyval_full, output_full,
+     load_sem, *rest) = refs
+    big = GradSum(n_dp, n_exp, own.shape[0], own, rest[:8], rest[8:18])
+    little = GradSum(n_dp, n_exp, 1, own_s, rest[18:26], rest[26:36])
     tree, width = x_ref.shape
-    greet(big.partners())
+    ring = Ring(n_exp)
+    greet(big.partners() + ring.partners())
+    loads = [
+        pltpu.make_async_copy(src, dst, load_sem.at[k])
+        for k, (src, dst) in enumerate(((output_hbm, output_full), (query_hbm, query_full), (keyval_hbm, keyval_full)))
+    ]
+    if with_out:
+        parts, part_sem = rest[36], rest[37]
+        out = RingScatter(ring, lambda e: parts.at[e], views(rest[38:41]), rest[41:45])
+        part_loads = [pltpu.make_async_copy(parts_hbm.at[j], parts.at[j], part_sem.at[j]) for j in range(n_exp)]
+        for copy in part_loads:
+            copy.start()
+    for copy in loads:
+        copy.start()
     shard = width // n_dp
     side = shard // 2
     tile = 512
     lane = lanes_of((tree, 128))
     left = lane < HD
+    if with_out:
+        for copy in part_loads:
+            copy.wait()
+        for d in out.order():
+            out.start_pair(d)
 
     def gain_row(i):
-        return jnp.concatenate([gains[d].astype(F32)[i : i + 1] for d in range(n_dp)], axis=1)
+        return gains[...].astype(F32)[i : i + 1]
 
     bias[...] = mask_bias(parents, tree)
 
+    names = routes_t[...].astype(F32)
+    pick = jnp.where(lax.broadcasted_iota(jnp.int32, (16, 128), 0) == lanes_of((16, 128)), 1.0, 0.0).astype(LOW)
+    names = dot(jnp.concatenate([names, jnp.zeros_like(names)], axis=0).astype(LOW), pick, 0, 0)
     chosen = jnp.zeros((tree, 128), F32)
-    for k in range(routes.shape[1]):
-        chosen = jnp.maximum(chosen, jnp.where(routes[:, k : k + 1] == lane, 1.0, 0.0))
-    logits = jnp.where(chosen > 0.5, dot(hidden2[...], router_full[...]), -1e30)
+    for k in range(routes_t.shape[0]):
+        chosen = jnp.maximum(chosen, jnp.where(names[:, k : k + 1] == lane.astype(F32), 1.0, 0.0))
+    logits = jnp.where(chosen > 0.5, dot(hidden2[...], router_t[...], 1, 1), -1e30)
     powers = jnp.exp(logits - jnp.max(logits, axis=1, keepdims=True))
     gate = powers / jnp.sum(powers, axis=1, keepdims=True)
     count = gates_in.shape[0]
@@ -1113,8 +1162,8 @@
     high, low = two_parts(gates_in[...])
     gate_back = dot(high, pick, 0, 0) + dot(low, pick, 0, 0)
     grad_logits = (gate * (gate_back - jnp.sum(gate * gate_back, axis=1, keepdims=True))).astype(LOW)
-    grad_router = dot(hidden2[...], grad_logits, 0, 0)
-    grad_hidden2 = hid_sum[...] + dot(grad_logits, router_full[...], 1, 1)
+    grad_router = dot(grad_logits, hidden2[...], 0, 0)[:EXPERTS]
+    grad_hidden2 = hid_sum[...] + dot(grad_logits, router_t[...])
     back, gain2_sum = norm_back(middle[...], gain_row(1), grad_hidden2)
     grad_middle = cot[...].astype(F32) + back
     input_grad[...] = grad_middle
@@ -1130,10 +1179,16 @@
         if tile % shard == 0:
             lax.fori_loop(0, width // tile, part, 0)
 
+    if with_out:
+        out.first()
     for i in range(2):
         rhs[...] = branch[:, pl.ds(i * tile, tile)]
         chunk_grads(i, attended, rhs)
         big.start(i)
+
+    if with_out:
+        out.early()
+    loads[0].wait()
 
     def att_tile(n, carry):
         rows = pl.ds(pl.multiple_of(n * tile, tile), tile)
@@ -1182,73 +1237,78 @@
 
     for i in range(KV // 2):
         two_groups(i)
+        gather_rhs(i)
+        chunk_grads(2 + i, hidden, rhs)
+        big.start(2 + i)
         if i == 0:
             big.paired(0)
             big.paired(1)
         if i == 1:
-            big.met(0, 0)
+            if with_out:
+                out.late()
             big.paired(2)
         if i == 2:
+            big.met(0, 0)
             big.met(1, 0)
-            big.met(0, 1)
             big.paired(3)
         if i == 3:
+            big.met(0, 1)
             big.met(1, 1)
+            big.paired(4)
             big.met(2, 0)
-            big.paired(4)
-        gather_rhs(i)
-        chunk_grads(2 + i, hidden, rhs)
-        big.start(2 + i)
+
+    for copy in loads[1:]:
+        copy.wait()
+    big.line(0)
 
     def hidden_tile(n, carry):
         cols = pl.ds(pl.multiple_of(n * tile, tile), tile)
-        grad = dot(grad_q_pre[...], query_full[cols, :], 1, 1) + dot(grad_kv_pre[...], keyval_full[cols, :], 1, 1)
-        hid_sum_out[:, cols] = grad
+        grad_hid[:, cols] = dot(grad_q_pre[...], query_full[cols, :], 1, 1) + dot(grad_kv_pre[...], keyval_full[cols, :], 1, 1)
         return carry
 
-    hid_sum_out = rest[38]
     lax.fori_loop(0, width // tile, hidden_tile, 0)
     big.paired(5)
-    back, gain1_sum = norm_back(x_ref[...].astype(F32), gain_row(0), hid_sum_out[...])
+    big.met(3, 0)
+    big.line(1)
+    back, gain1_sum = norm_back(x_ref[...].astype(F32), gain_row(0), grad_hid[...])
     input_grad[...] = input_grad[...] + back
 
     sub = lax.broadcasted_iota(jnp.int32, (16, width), 0)
-    sums = jnp.zeros((16, width), F32)
-    for k, row in enumerate((gain1_sum, gain2_sum)):
-        first, second = two_parts(row)
-        sums = jnp.where(sub == 2 * k, first.astype(F32), jnp.where(sub == 2 * k + 1, second.astype(F32), sums))
-    line_at = lax.broadcasted_iota(jnp.int32, (16, 128), 0)
-    column = jnp.where(lanes_of((16, 128)) == EXPERTS + lax.div(line_at, 2), jnp.where(line_at < 4, 1.0, 0.0), 0.0).astype(LOW)
-    little_all = (grad_router + dot(sums.astype(LOW), column, 0, 0)).astype(LOW)
+    sums = jnp.where(sub == 0, gain1_sum, jnp.where(sub == 1, gain2_sum, 0.0))
+    little_all = jnp.concatenate([grad_router, sums], axis=0).astype(LOW)
     for d in range(n_dp):
         for k in range(2):
             at = d * shard + k * side
-            own_s[0, d, k] = little_all[at : at + side]
+            own_s[0, d, k] = little_all[:, at : at + side]
     little.start(0)
-
     big.met(2, 1)
-    big.met(3, 0)
+    big.line(2)
     big.met(4, 0)
     little.paired(0)
     big.met(3, 1)
+    big.line(3)
     big.met(5, 0)
     little.met(0, 0)
     big.met(4, 1)
+    big.line(4)
     little.met(0, 1)
     big.met(5, 1)
-    steps = own.shape[0] + big.depth - 1
-
-    def line(t, carry):
+    big.line(5)
+    if with_out:
+        out.last(outs[5], middle)
+    chunks = own.shape[0]
+    hop = 2 * (big.depth - 1)
+    for t in range(chunks, chunks + hop):
         big.line(t)
-        return carry
-
-    lax.fori_loop(0, steps, line, 0)
+        if t >= hop:
+            big.close(t - hop)
 
     def little_line(t, carry):
         little.line(t)
         return carry
 
-    lax.fori_loop(0, little.depth, little_line, 0)
+    lax.fori_loop(0, hop + 1, little_line, 0)
+    little.close(0)
 
     def place(i, which, field):
         rows = pl.ds(pl.multiple_of(which * side, 16), side)
@@ -1260,80 +1320,64 @@
         add_rows(grad_kv.at[rows, pl.ds(i * 128, 128)], field.at[:, pl.ds(256, 128)])
         add_rows(grad_kv.at[rows, pl.ds(KV * HD + i * 128, 128)], field.at[:, pl.ds(384, 128)])
 
-    chunks = own.shape[0]
-    for i in range(chunks):
-        big.close(i)
-    little.close(0)
     for i in range(chunks):
         place(i, big.core, big.final.at[i])
-    add_rows(grad_s.at[pl.ds(pl.multiple_of(big.core * side, 16), side)], little.final.at[0])
+    add_rows(grad_s.at[big.core], little.final.at[0])
     for i in range(chunks):
         big.last(i).wait_recv()
         place(i, 1 - big.core, big.other.at[i])
         big.finish(i)
     little.last(0).wait_recv()
-    add_rows(grad_s.at[pl.ds(pl.multiple_of((1 - big.core) * side, 16), side)], little.other.at[0])
+    add_rows(grad_s.at[1 - big.core], little.other.at[0])
     little.finish(0)
-
-
-def back(n_dp, n_exp, local, tokens, cotangent, hid_sum, gates_in, routes, parents, tables, saved, collective_id):
+    if with_out:
+        out.finish_sends()
+
+
+def back(n_dp, n_exp, local, tokens, cotangent, hid_sum, gates_in, routes_t, parents, tables, saved, parts, collective_id):
     tree, width = tokens.shape
     shard = width // n_dp
-    shape = jax.ShapeDtypeStruct
-    side, chunks, tile = shard // 2, 6, 512
+    shape, vm, sem = jax.ShapeDtypeStruct, pltpu.VMEM, pltpu.SemaphoreType.DMA
+    side, chunks, tile, rows = shard // 2, 6, 512, EXPERTS + 16
     big_bufs, big_sems = GradSum.scratch(n_dp, chunks, side, tile)
-    little_bufs, little_sems = GradSum.scratch(n_dp, 1, side, 128)
-    vm = pltpu.VMEM
-    args = (tokens, cotangent, hid_sum, gates_in, routes, parents, *tables, *saved)
+    little_bufs, little_sems = GradSum.scratch(n_dp, 1, rows, side)
+    args = (tokens, cotangent, hid_sum, gates_in, routes_t, parents, *tables, *saved)
+    spaces = [VMEM] * len(args)
+    spaces[16:19] = [ANY] * 3
+    out_shape = [
+        shape((tree, width), F32), shape((shard, width), F32), shape((shard, width), F32), shape((shard, width), F32),
+        shape((2, rows, side), F32),
+    ]
+    extra = []
+    if parts is not None:
+        args, spaces = (*args, parts), spaces + [ANY]
+        out_shape.append(shape((tree, width), LOW))
+        bufs, sems = RingScatter.scratch(n_exp, (tree, width), LOW)
+        extra = [vm(parts.shape, LOW), sem((n_exp,)), *bufs, *sems]
     return pl.pallas_call(
-        functools.partial(back_body, n_dp, n_exp, local),
-        out_shape=[
-            shape((tree, width), F32), shape((shard, width), F32), shape((shard, width), F32), shape((shard, width), F32),
-            shape((shard, 128), F32),
-        ],
-        in_specs=[pl.BlockSpec(memory_space=VMEM)] * len(args),
-        out_specs=[pl.BlockSpec(memory_space=VMEM)] * 5,
+        functools.partial(back_body, n_dp, n_exp, local, parts is not None),
+        out_shape=out_shape,
+        in_specs=[pl.BlockSpec(memory_space=s) for s in spaces],
+        out_specs=[pl.BlockSpec(memory_space=VMEM)] * len(out_shape),
         scratch_shapes=[
             vm((tree, tree), F32), vm((tree, width), LOW), vm((tree, width), LOW), vm((tree, width), LOW), vm((tree, width), LOW),
-            vm((tree, tile), LOW), vm((chunks, n_dp, 2, side, tile), LOW), vm((1, n_dp, 2, side, 128), LOW),
-            *big_bufs, *big_sems, *little_bufs, *little_sems, vm((tree, width), F32),
+            vm((tree, tile), LOW), vm((chunks, n_dp, 2, side, tile), LOW), vm((1, n_dp, 2, rows, side), LOW),
+            vm((tree, width), F32), vm((width, width), LOW), vm((width, width), LOW), vm((width, width), LOW), sem((3,)),
+            *big_bufs, *big_sems, *little_bufs, *little_sems, *extra,
         ],
         compiler_params=pltpu.CompilerParams(
-            collective_id=collective_id, has_side_effects=True, vmem_limit_bytes=60 * MIB),
+            collective_id=collective_id, has_side_effects=True, vmem_limit_bytes=63 * MIB),
         name="back",
     )(*args)
 
 
-def tree_layout(tree_rows):
-    unit_rows = tree_rows // 20
-    row_index = jnp.arange(tree_rows, dtype=jnp.int32)
-    segment = jnp.where(
-        row_index < 8 * unit_rows,
-        0,
-        jnp.where(
-            row_index < 12 * unit_rows,
-            1 + (row_index - 8 * unit_rows) // unit_rows,
-            5 + (row_index - 12 * unit_rows) // unit_rows,
-        ),
-    )
-    depth_start = jnp.where(segment == 0, 0, jnp.where(segment < 5, 8 * unit_rows, 9 * unit_rows))
-    seg_start = jnp.where(
-        segment == 0,
-        0,
-        jnp.where(
-            segment < 5,
-            8 * unit_rows + (segment - 1) * unit_rows,
-            12 * unit_rows + (segment - 5) * unit_rows,
-        ),
-    )
-    position = depth_start + row_index - seg_start
-    return (segment, position)
-
-
-def rope_tables(position):
-    frequency = 10000.0 ** (-jnp.arange(0, HD, 2, dtype=jnp.float32) / HD)
-    angles = position.astype(jnp.float32)[:, None] * frequency[None, :]
-    return (jnp.concatenate([jnp.cos(angles)] * 2, -1), jnp.concatenate([jnp.sin(angles)] * 2, -1))
+def rope_pairs(tree_rows):
+    unit = tree_rows // 20
+    row = np.arange(tree_rows)
+    position = np.where(row < 8 * unit, row, np.where(row < 12 * unit, 8 * unit + row % unit, 9 * unit + row % unit))
+    frequency = 10000.0 ** (-np.arange(0, HD, 2) / HD)
+    angles = position[:, None] * frequency[None, :]
+    return tuple(jnp.asarray(np.concatenate([table] * 4, axis=1), jnp.float32) for table in (np.cos(angles), np.sin(angles)))
 
 
 def gated_unit(gate_up):
@@ -1343,7 +1387,7 @@
 
 
 def experts_plain(
-    n_dp, n_exp, hidden2, grad_y, routes_all, router_full, expert_in, expert_out, middle, collective_id
+    n_dp, n_exp, hidden2, grad_y, routes_all, router_full, expert_in, expert_out, middle
 ):
     tree_rows, width = hidden2.shape
     capacity = CAP
@@ -1446,28 +1490,40 @@
     local = expert_in.shape[0]
     tree_rows = tokens.shape[0]
     grad_y = lax.all_gather(cotangent, "expert", axis=0, tiled=False)
-    _, position = tree_layout(tree_rows)
-    tables = tuple(jnp.concatenate([table, table], axis=1) for table in rope_tables(position))
+    tables = rope_pairs(tree_rows)
+    routes_t = routes.T
     (hidden, queries, keys, values, attended, middle, hidden2, log_total, *full, gains, routes_all) = front(
-        n_dp, n_exp, tokens, attn_gain, moe_gain, w_router, w_query, w_keyval, w_output, routes.T, parents, tables, 1
+        n_dp, n_exp, tokens, jnp.stack([attn_gain, moe_gain]), w_router.T, w_query, w_keyval, w_output, routes_t, parents, tables, 1
     )
-    run_experts = experts if (n_dp, n_exp) == (4, 8) else experts_plain
-    block_out, hid_sum, gate_grads, expert_in_share, expert_out_share = run_experts(
-        n_dp, n_exp, hidden2, grad_y, routes_all, full[3][:, :EXPERTS], expert_in, expert_out, middle, 2
+    router_t = full[3]
+    if (n_dp, n_exp) == (4, 8):
+        parts, hid_sum, gate_grads, expert_in_share, expert_out_share, late = experts(
+            n_dp, n_exp, hidden2, grad_y, routes_all, router_t, expert_in, expert_out, 2
+        )
+        late_share = lax.psum_scatter(late, "dp", scatter_dimension=0, tiled=True).astype(jnp.float32)[None]
+        rows = expert_in_share.shape[1]
+        expert_in_share = jnp.concatenate([expert_in_share, late_share[:, :rows]], axis=0)
+        expert_out_share = jnp.concatenate([expert_out_share, late_share[:, rows:]], axis=0)
+    else:
+        parts = None
+        block_out, hid_sum, gate_grads, expert_in_share, expert_out_share = experts_plain(
+            n_dp, n_exp, hidden2, grad_y, routes_all, router_t[:EXPERTS].T, expert_in, expert_out, middle
+        )
+    saved = (hidden, queries, keys, values, attended, middle, hidden2, log_total, *full, gains)
+    input_grad, grad_q, grad_kv, grad_o, grad_small, *made = back(
+        n_dp, n_exp, local, tokens, cotangent, hid_sum, gate_grads.reshape(n_exp * 8, tree_rows), routes_t, parents, tables, saved, parts, 3
     )
-    saved = (hidden, queries, keys, values, attended, middle, hidden2, log_total, *full, gains)
-    input_grad, grad_q, grad_kv, grad_o, grad_small = back(
-        n_dp, n_exp, local, tokens, cotangent, hid_sum, gate_grads.reshape(n_exp * 8, tree_rows), routes, parents, tables, saved, 3
-    )
+    if parts is not None:
+        block_out = made[0]
     return (
         block_out,
         input_grad,
-        grad_small[:, EXPERTS],
+        grad_small[:, EXPERTS].reshape(-1),
         grad_q,
         grad_kv,
         grad_o,
-        grad_small[:, EXPERTS + 1],
-        grad_small[:, :EXPERTS],
+        grad_small[:, EXPERTS + 1].reshape(-1),
+        jnp.concatenate([grad_small[0, :EXPERTS], grad_small[1, :EXPERTS]], axis=1).T,
         expert_in_share,
         expert_out_share,
     )

time: 382 us -> 361 us (0.945)
  Pallas kernels: 344 us -> 321 us
  local copies, waits for them, and re-layouts: 20.2 us -> 10.1 us
  waiting for transfers between devices: 1.57 us -> 8.92 us
  other arithmetic: 1.72 us -> 6.26 us
    pallas_call x1, Pallas kernels: 195 us -> 174 us  [experts(): pl.pallas_call(functools.partial(experts_body, n_dp, n_exp), out_shape=[s...]
    unnamed x24 -> x19, local copies, waits for them, and re-layouts: 14.2 us -> 6.59 us
    all_gather x1, waiting for transfers between devices: 0.89 us -> 8.22 us  [shards(): grad_y = lax.all_gather(cotangent, 'expert', axis=0, tiled=False)]
  transfers between devices with their start and end apart: 1 -> 2, of which waited for: 1 -> 1; matrix products, arithmetic and copies ran while one was open for 2% -> 1% of each run, Pallas kernels for 14% -> 41%
where the time goes in v6:
time: 361 us; the launch traced here: 360 us
  Pallas kernels  321 us (89%)
  between operations  14.1 us (4%)
  local copies, waits for them, and re-layouts  10.1 us (3%)
  waiting for transfers between devices  8.92 us (2%)
  other arithmetic  6.26 us (2%)
    pallas_call x1, Pallas kernels, experts(): pl.pallas_call(functools.partial(experts_body, n_dp, n_exp), out_shape=[s...  174 us
    pallas_call x1, Pallas kernels, back(): pl.pallas_call(functools.partial(back_body, n_dp, n_exp, local, parts is...  96.5 us
    pallas_call x1, Pallas kernels, front(): pl.pallas_call(functools.partial(front_body, n_dp, n_exp), out_shape=[low...  50.4 us
    all_gather x1, waiting for transfers between devices, shards(): grad_y = lax.all_gather(cotangent, 'expert', axis=0, tiled=False)  8.22 us
  transfers between devices with their start and end apart: 2, of which 1 were waited for; matrix products, arithmetic and copies ran while one was open for 1% of the time, Pallas kernels for 41%

profile of v6, /device:TPU:0, one launch (start us, length us, event | category | flops | bytes accessed | tf_op | source)
XLA Modules:
  0.0 360.1 jit_solution(11883462609220777899)
XLA Ops:
  7.2 0.0 all-gather.3.cloned.1.call-start
  7.2 0.7 all-gather.3.cloned.1.call-update
  7.9 0.0 reduce-scatter.2.cloned.1.call-start
  8.0 0.7 stack.9
  8.6 0.7 stack.10
  9.3 0.6 pad_maximum_fusion.2.gain_pair
  9.8 50.4 %front.1 = (bf16[320,1024]{1,0:T(8,128)(2,1)}, bf16[320,1024]{1,0:T(8,128)(2,1)}, bf16[8,320,128]{2,1,0:T(8,128)(2,1)}, bf16[8,320,128]{2,1,0:T(8,128)(2,1)}, bf...) custom-call(bf16[320,1024]{1,0:T(8,128)(2,1)} %x_ref.3, ...), custom_call_target="tpu_custom_call" | custom-call | tf_op jit(solution)/shard_map/front/pallas_call | solution.py:927
  60.2 8.2 %all-gather.3.cloned.1.call-done = bf16[2560,1024]{1,0:T(8,128)(2,1)} async-done(((bf16[320,1024]{1,0:T(8,128)(2,1)}), bf16[2560,1024]{1,0:T(8,128)(2,1)}) %all-gather.3.cloned.1.call-update) | async-done | bytes 5242896 | tf_op jit(solution)/shard_map/all_gather | solution.py:1492
  68.4 173.7 %experts.1 = (bf16[8,320,1024]{2,1,0:T(8,128)(2,1)}, f32[320,1024]{1,0:T(8,128)}, f32[8,8,320]{2,1,0:T(8,128)}, f32[3,256,1024]{2,1,0:T(8,128)}, f32[3,128,1024]{2,1,0:T(8,128)}, /*index=5*/bf16[1536,1024]{1,0:T(8,128)(2,1)}) custom-call(bf16[320,1024]{1,0:T(8,128)(2,1)} %get-tuple-element.36.hid_ref.hidden2, bf16[8,320,1024]{2,1,0:T(8,128)(2,1)} %bitcast.15, ...), custom_call_target="tpu_custom_call" | custom-call | tf_op jit(solution)/shard_map/experts/pallas_call | solution.py:633
  242.1 0.0 reduce-scatter.2.cloned.1.call-update
  242.2 96.5 %back.1 = (f32[320,1024]{1,0:T(8,128)}, f32[256,1024]{1,0:T(8,128)}, f32[256,1024]{1,0:T(8,128)}, f32[256,1024]{1,0:T(8,128)}, f32[2,48,128]{2,1,0:T(8,128)}, /*index=5*/bf16[320,1024]{1,0:T(8,128)(2,1)}) custom-call(bf16[320,1024]{1,0:T(8,128)(2,1)} %x_ref.3, bf16[320,1024]{1,0:T(8,128)(2,1)} %cot.1, f32[320,1024]{1,0:T(8,128)} %get-tuple-element.39.hid_sum, ...), custom_call_target="tpu_custom_call" | custom-call | tf_op jit(solution)/shard_map/back/pallas_call | solution.py:1357
  338.7 0.7 slice_bitcast_fusion.1
  339.4 0.6 maximum_bitcast_fusion
  340.1 1.3 fusion
  341.4 0.0 reduce-scatter.2.cloned.1.call-done
  341.4 1.3 bitcast_convert_fusion
  342.7 0.0 copy-start
  342.8 0.1 slice.24
  342.8 1.8 copy-done
  344.6 0.0 copy-start.1
  344.6 2.3 pad_maximum_fusion
  346.9 0.0 copy-done.1
  346.9 0.0 copy-start.6
  346.9 0.0 copy-start.2
  346.9 1.5 pad_maximum_fusion.1
  348.4 0.0 copy-start.5
  348.4 0.0 copy-done.6
  348.4 0.8 copy.29
  349.2 0.0 copy-done.2
  349.2 0.0 copy-start.4
  349.2 1.1 copy.30
  350.3 0.0 copy-done.5
  350.3 0.0 copy-start.3
  350.3 1.0 copy.31
  351.3 0.0 copy-done.4
  351.3 1.0 copy.32
  352.2 0.0 copy-done.3
  352.2 1.0 copy.33
  (1 shorter events, 0.0 us)
Async XLA Ops:
  7.2 61.3 %all-gather.3.cloned.1.call-start = ((), (), s32[]{:S(2)}) async-start(), calls=%async_computation.2 | async-start | bytes 5898240 | tf_op jit(solution)/shard_map/all_gather | solution.py:1492
  7.9 333.5 %reduce-scatter.2.cloned.1.call-start = ((), (), s32[]{:S(2)}) async-start(), calls=%async_computation.1 | async-start | bytes 3932160 | tf_op jit(solution)/shard_map/reduce_scatter | solution.py:1503
  342.7 1.9 copy-start
  344.6 2.3 copy-start.1
  346.9 1.5 copy-start.6
  346.9 2.3 copy-start.2
  348.4 1.9 copy-start.5
  349.2 2.0 copy-start.4
  350.3 1.9 copy-start.3
Sparse Core Ops, SparseCore 0:
  9.7 58.7 all-gather.2
  242.3 57.2 reduce-scatter.1
